TPU v7x, 32 devices: a whole 2x2x4 slice. The times are simulated.
32 devices in a mesh: groups: 2 (over y), chan: 4 (over z), sub: 2 (over x), rep: 2 (over core).
Axes of the slice: x: 2, y: 2, z: 4, core: 2. Of those that a mesh axis runs over, the one named last changes fastest.
Arguments:
- traces: bfloat16 [512, 128, 512], P(('groups', 'sub', 'rep'), 'chan'), parts along dimension 0, may hold values from -6 to 6
- channel_slot: int32 [512], P(('groups', 'sub', 'rep')), parts along dimension 0, may hold values from 0 to 63, as said below
Outputs:
- correlations: float32 [3, 8, 64, 64, 128], P(None, ('groups', 'chan'), 'sub', 'rep'), parts along dimension 1
There are 2 independent parts, one for each index of `groups`. A program takes and returns all parts, laid end to end along the dimension named above; each array names one. Nothing has to cross between parts.
Inputs may be any that keep to these rules, and one draw needn't show every extreme that they name: `channel_slot`: each aligned run of 64 entries is a permutation of 0 .. 63.
All inputs are finite; a program needn't handle non-finite values.
Results may differ from a plain program's by a relative error of at most 0.0052.
Values may be sent and summed in bfloat16 or wider, within the bound.
No kernel may reach another device: no remote copies, remote signals or barrier semaphores. Data moves between devices by JAX's collectives and lax.ppermute only.
A program may use at most 64 MiB of HBM per device.

v0:
```python
import functools
import math

import jax
import jax.numpy as jnp
import numpy as np
from jax import lax
from jax.experimental import pallas as pl
from jax.experimental.pallas import tpu as pltpu
from jax.sharding import PartitionSpec as P

LAGS = 128
ROUNDS = 3
LANES = 128
HALF = LANES // 2
VMEM_BYTES = 32 * 1024 * 1024
ORDER_VMEM_BYTES = 48 * 1024 * 1024
NT = (((1,), (1,)), ((), ()))
BLOCKS = 4
FAR = (0, 1)
NEAR = (2, 3)
KEPT_AT, OWN_AT = 0, 2


def kernel_call(kernel, name, flops, bytes_accessed, vmem_bytes=VMEM_BYTES, **more):
    return pl.pallas_call(
        kernel,
        name=name,
        compiler_params=pltpu.CompilerParams(vmem_limit_bytes=vmem_bytes),
        cost_estimate=pl.CostEstimate(flops=flops, bytes_accessed=bytes_accessed, transcendentals=0),
        **more,
    )


def in_vmem():
    return pl.BlockSpec(memory_space=pltpu.VMEM)


def dft_rows_table(samples):
    bins = samples // 2
    turns = (np.arange(bins)[:, None] * np.arange(samples)[None, :]) % samples
    angles = turns.astype(np.float32) * np.float32(2.0 * math.pi / samples)
    table = np.concatenate([np.cos(angles), -np.sin(angles)], axis=0)
    return jnp.asarray(table.astype(np.float32)).astype(jnp.bfloat16)


def lag_rows_table(samples, scale):
    bins = samples // 2
    offsets = np.arange(LAGS) - LAGS // 2
    turns = (offsets[:, None] * np.arange(bins)[None, :]) % samples
    angles = turns.astype(np.float32) * np.float32(2.0 * math.pi / samples)
    table = np.concatenate([np.cos(angles), -np.sin(angles)], axis=1) * np.float32(scale)
    return jnp.asarray(table.astype(np.float32)).astype(jnp.bfloat16)


def selection(rows, columns, ones):
    table = np.zeros((rows, columns), np.float32)
    for row, column in ones:
        table[row, column] = 1.0
    return jnp.asarray(table).astype(jnp.bfloat16)


def own_picks():
    piece = HALF // BLOCKS
    to_i = []
    for at in range(BLOCKS):
        for n in range(piece):
            to_i.append((at // 2 * piece + n, at % 2 * LANES + HALF + at * piece + n))
    to_j = [(j, copy * HALF + j) for j in range(HALF) for copy in range(2)]
    return selection(2 * piece, 2 * LANES, to_i), selection(LANES, LANES, to_j)


def half_picks():
    count = HALF // 2
    to_i, to_j = [], []
    for odd in range(2):
        for n in range(count):
            to_i.append((n, odd * LANES + odd * HALF + count + n))
            to_j += [(odd * HALF + n, odd * LANES + copy * count + n) for copy in range(4)]
    return selection(count, 2 * LANES, to_i), selection(LANES, 2 * LANES, to_j)


def order_rows(traces, slots, kinds):
    rows, wins, samples = traces.shape
    tiles = samples // LANES
    piece = rows // BLOCKS
    step_wins = 16
    steps = wins // step_wins
    batch = 4
    used = max(kinds, key=len)
    pitch = len(used) * piece + 1

    def kernel(slots_ref, traces_ref, *refs):
        out_refs, (wide, in_ref, slot_ref, sems) = refs[:-4], refs[-4:]
        slot_copy = pltpu.make_async_copy(slots_ref, slot_ref, sems.at[steps])
        slot_copy.start()
        copies = []
        for step in range(steps):
            here = pl.ds(step * step_wins, step_wins)
            copies.append(
                pltpu.make_async_copy(traces_ref.at[:, here, :], in_ref.at[:, here, :], sems.at[step])
            )
            copies[-1].start()
        slot_copy.wait()
        z = lax.axis_index("chan")
        odd = lax.rem(z, 2)
        pair = jnp.where(z < 2, 2, 0)

        def some_windows(step):
            first_win = step * step_wins
            for at, position in enumerate(used):
                block = pair + position + (odd if position % 2 == 0 else -odd)
                first = lax.rem(block, BLOCKS) * piece

                def move(group, carry, at=at, first=first):
                    js = [group * batch + u for u in range(batch)]
                    picked = [
                        in_ref[slot_ref[first + j], pl.ds(first_win, step_wins), :].astype(jnp.float32) for j in js
                    ]
                    for j, row in zip(js, picked):
                        for tile in range(tiles):
                            wide[tile, pl.ds(at * piece + j, step_wins, stride=pitch), :] = row[
                                :, tile * LANES : (tile + 1) * LANES
                            ]
                    return carry

                lax.fori_loop(0, piece // batch, move, 0)

            def pack(w, carry):
                blocks = [
                    wide[tile, pl.ds(w * pitch, len(used) * piece), :].astype(jnp.bfloat16) for tile in range(tiles)
                ]
                for out_ref, kind in zip(out_refs, kinds):
                    first = used.index(kind[0]) * piece
                    for tile, block in enumerate(blocks):
                        out_ref[first_win + w, :, tile * LANES : (tile + 1) * LANES] = block[
                            first : first + len(kind) * piece
                        ]
                return carry

            lax.fori_loop(0, step_wins, pack, 0, unroll=2)

        for step in range(steps):
            copies[step].wait()
            some_windows(step)

    return kernel_call(
        kernel,
        "order_rows",
        0,
        3 * traces.size * 2,
        vmem_bytes=ORDER_VMEM_BYTES,
        out_shape=[jax.ShapeDtypeStruct((wins, len(kind) * piece, samples), jnp.bfloat16) for kind in kinds],
        in_specs=[pl.BlockSpec(memory_space=pltpu.HBM)] * 2,
        out_specs=[in_vmem()] * len(kinds),
        scratch_shapes=[
            pltpu.VMEM((tiles, (step_wins + 1) * pitch, LANES), jnp.float32),
            pltpu.VMEM(traces.shape, traces.dtype),
            pltpu.SMEM(slots.shape, slots.dtype),
            pltpu.SemaphoreType.DMA((steps + 1,)),
        ],
    )(slots, traces)


def diagonal(values, copies):
    blank = jnp.zeros_like(values)
    rows = [[values if at == copy else blank for at in range(copies)] for copy in range(copies)]
    return jnp.concatenate([jnp.concatenate(row, axis=1) for row in rows], axis=0)


def spectra(rows_j, rows_i, tables):
    wins, given, samples = rows_j.shape
    bins = samples // 2
    pairs = wins // 2
    depth = 2 * wins
    folded = HALF // given
    line = depth // folded
    pitch = line + 1
    per_step = 2 * folded
    batch = 8

    def kernel(j_ref, i_ref, table_ref, to_i_ref, to_j_ref, i_out, j_out, wide):
        same = lax.axis_index("sub") == lax.axis_index("rep")

        def spectrum_of(group):
            stacked = []
            for win in [per_step * group + u for u in range(per_step)]:
                here = j_ref[win]
                stacked += [here, jnp.where(same, here, i_ref[win])]
            wave = jnp.concatenate(stacked, axis=0)
            return lax.dot_general(table_ref[...], wave, NT, preferred_element_type=jnp.float32)

        def keep(group, spectrum):
            energy = jnp.sum(spectrum * spectrum, axis=0, keepdims=True) / bins
            white = spectrum * lax.rsqrt(energy + 1e-05)
            for half in range(2):
                for part in range(2):
                    if folded == 1:
                        row = half * wins + part * pairs + group
                    else:
                        row = part * pairs + 2 * group + half
                    wide[pl.ds(row, bins, stride=pitch), :] = white[
                        part * bins : (part + 1) * bins, half * LANES : (half + 1) * LANES
                    ]

        groups = wins // per_step
        at_once = 4

        def some_windows(step, carry):
            first = step * at_once
            last = spectrum_of(first)
            for group in range(1, at_once):
                now = spectrum_of(first + group)
                keep(first + group - 1, last)
                last = now
            keep(first + at_once - 1, last)
            return carry

        lax.fori_loop(0, groups // at_once, some_windows, 0)

        def moved(fs):
            loaded = [wide[pl.ds(f * pitch, line), :].astype(jnp.bfloat16) for f in fs]
            i_rows = [
                lax.dot_general(to_i_ref[...], diagonal(values, 2), NT, preferred_element_type=jnp.float32)
                for values in loaded
            ]
            if folded == 2:
                i_rows = [jnp.concatenate([rows[: given // 2], rows[given // 2 :]], axis=1) for rows in i_rows]
            j_rows = jnp.dot(jnp.concatenate(loaded, axis=0), to_j_ref[...], preferred_element_type=jnp.float32)
            return fs, i_rows, j_rows

        def store(fs, i_rows, j_rows):
            for at, f in enumerate(fs):
                i_out[f] = i_rows[at].astype(jnp.bfloat16)
                for odd in range(folded):
                    j_out[f, odd * line : (odd + 1) * line] = j_rows[
                        at * line : (at + 1) * line, odd * LANES : (odd + 1) * LANES
                    ].astype(jnp.bfloat16)

        def pack(group, carry):
            first = group * 4 * batch
            waiting = moved([first + u for u in range(batch)])
            for at in range(1, 4):
                following = moved([first + at * batch + u for u in range(batch)])
                store(*waiting)
                waiting = following
            store(*waiting)
            return carry

        lax.fori_loop(0, bins // (4 * batch), pack, 0)

    shapes = [(bins, given // 2, LANES), (bins, depth, LANES)]
    return kernel_call(
        kernel,
        "spectra",
        4 * samples * samples * wins * given,
        4 * wins * given * samples * 2,
        out_shape=[jax.ShapeDtypeStruct(shape, jnp.bfloat16) for shape in shapes],
        in_specs=[in_vmem()] * (2 + len(tables)),
        out_specs=[in_vmem()] * len(shapes),
        scratch_shapes=[pltpu.VMEM(((bins + 1) * pitch, LANES), jnp.float32)],
    )(rows_j, rows_i, *tables)


def partial_correlations(lefts, rights, tables, jobs, outs):
    left_arrays = [array for array, _ in lefts]
    right_arrays = [array for array, _, _ in rights]
    bins, depth, _ = right_arrays[0].shape
    piece = HALF // BLOCKS
    pitch = bins + 1
    step_bins = 32
    groups = []
    slices = {}
    for used, groups_here in jobs:
        js = [(rights[right][1], there) for right in used for there in rights[right][2]]
        for left, _, first in groups_here:
            found = []
            for offset in range(2):
                at = first + offset
                for order, (j_other, there) in enumerate(js):
                    if there != at:
                        kind = (lefts[left][1], j_other, there ^ (at % 2))
                        found.append((at, kind, offset * HALF + order * piece))
                        slices.setdefault(at, []).append(kind)
            groups.append(found)
    for kinds in slices.values():
        kinds.sort()
    total = len(groups) * piece
    batch = 4

    def first_of(at):
        (out,) = [positions for positions in outs if at in positions]
        return outs.index(out), sum(len(slices[before]) for before in out[: out.index(at)])

    def kernel(*refs):
        left_refs, rest = refs[: len(lefts)], refs[len(lefts) :]
        right_refs, rest = rest[: len(rights)], rest[len(rights) :]
        lag_ref, same_ref, out_refs, cross = rest[0], rest[1], rest[2:-1], rest[-1]
        lanes = lax.broadcasted_iota(jnp.int32, (depth, LANES), 1)

        first_half = lanes < HALF
        lower = lanes % HALF < HALF // 2
        blank = jnp.zeros((depth, LANES), jnp.bfloat16)

        def turn(values):
            swapped = []
            for first in range(0, depth, depth // 2):
                middle, last = first + depth // 4, first + depth // 2
                swapped += [-values[middle:last], values[first:middle]]
            return jnp.concatenate(swapped, axis=0)

        def right_hand(used, f):
            values = right_refs[used[0]][f]
            if len(used) == 2:
                values = jnp.where(lower, values, right_refs[used[1]][f])
            turned = turn(values)
            return jnp.concatenate(
                [
                    jnp.concatenate([jnp.where(first_half, part, blank) for part in (values, turned)], axis=1),
                    jnp.concatenate([jnp.where(first_half, blank, part) for part in (values, turned)], axis=1),
                ],
                axis=0,
            )

        def products(first_bin, count):
            found = []
            for f in [first_bin + u for u in range(count)]:
                first = 0
                for used, groups_here in jobs:
                    lhs = [left_refs[left][f, row : row + piece] for left, row, _ in groups_here]
                    lhs = jnp.concatenate(lhs, axis=0) if len(lhs) > 1 else lhs[0]
                    product = jnp.dot(lhs, right_hand(used, f), preferred_element_type=jnp.float32)
                    found.append((first * pitch + f, product))
                    first += lhs.shape[0]
            return found

        def keep(found):
            for here, product in found:
                for part in range(2):
                    cross[pl.ds(part * total * pitch + here, product.shape[0], stride=pitch), :] = product[
                        :, part * LANES : (part + 1) * LANES
                    ]

        def some_bins(step, carry):
            first = step * step_bins
            waiting = products(first, batch)
            for at in range(batch, step_bins, batch):
                following = products(first + at, batch)
                keep(waiting)
                waiting = following
            keep(waiting)
            return carry

        lax.fori_loop(0, bins // step_bins, some_bins, 0)

        for index, found in enumerate(groups):
            targets = []
            for at, kind, lane in found:
                out, first = first_of(at)
                targets.append((out_refs[out], first + slices[at].index(kind), lane))

            def summed(i):
                parts = []
                for part in range(2):
                    start = (part * total + index * piece + i) * pitch
                    parts.append(
                        jnp.concatenate([cross[pl.ds(start, bins), :], cross[pl.ds(start + pitch, bins), :]], axis=1)
                    )
                values = jnp.concatenate(parts, axis=0).astype(jnp.bfloat16)
                return i, jnp.dot(lag_ref[...], values, preferred_element_type=jnp.float32)

            def across(i, lagged):
                lagged = lagged.astype(jnp.bfloat16)
                return i, lax.dot_general(same_ref[...], lagged, NT, preferred_element_type=jnp.float32)

            def store(i, rows):
                for half in range(2):
                    for out, place, lane in targets:
                        row = half * LANES + lane
                        out[place, i + half] = rows[row : row + piece].astype(out.dtype)

            sums, rows = summed(0), None
            for i in range(2, piece, 2):
                more = summed(i)
                if rows is not None:
                    store(*rows)
                rows = across(*sums)
                sums = more
            store(*rows)
            store(*across(*sums))

    shapes = [(sum(len(slices[at]) for at in positions), piece, piece, LAGS) for positions in outs]
    types = [jnp.float32 if positions == (OWN_AT,) else jnp.bfloat16 for positions in outs]
    results = kernel_call(
        kernel,
        "partial_correlations",
        4 * total * bins * depth * LANES + 4 * total * bins * LANES * LAGS,
        2 * sum(array.size for array in left_arrays + right_arrays),
        out_shape=[jax.ShapeDtypeStruct(shape, kind) for shape, kind in zip(shapes, types)],
        in_specs=[in_vmem()] * (len(lefts) + len(rights) + len(tables)),
        out_specs=[in_vmem()] * len(shapes),
        scratch_shapes=[pltpu.VMEM(((2 * total + 1) * pitch, LANES), jnp.float32)],
    )(*left_arrays, *right_arrays, *tables)
    return results, slices


def assembled(shares):
    arrays = [array for array, _ in shares]
    _, piece, _, lags = arrays[0].shape
    width = 2 * piece

    def kernel(*refs):
        out, held, sems = refs[-3:]
        sub = lax.axis_index("sub")
        odd = lax.rem(lax.axis_index("chan"), 2)
        copies = []
        for there, round_at in ((0, 1), (1, 2 - 2 * odd), (3, 2 * odd)):
            for i_other in range(2):
                for j_other in range(2):
                    parts = [
                        refs[at][place].astype(jnp.float32)
                        for at, (_, kinds) in enumerate(shares)
                        for place, kind in enumerate(kinds)
                        if kind == (i_other, j_other, there)
                    ]
                    i_first = jnp.where(sub == 0, i_other, 1 - i_other) * piece
                    j_first = pl.multiple_of(jnp.where(sub == 0, j_other, 1 - j_other) * piece, piece)
                    held[round_at, 0, pl.ds(i_first, piece), pl.ds(j_first, piece), :] = functools.reduce(
                        jnp.add, parts
                    )
            at = len(copies)
            copies.append(pltpu.make_async_copy(held.at[round_at], out.at[round_at], sems.at[at]))
            copies[-1].start()
        for copy in copies:
            copy.wait()

    shape = (ROUNDS, 1, width, width, lags)
    return kernel_call(
        kernel,
        "assembled",
        0,
        sum(array.size for array in arrays) * 2,
        out_shape=jax.ShapeDtypeStruct(shape, jnp.float32),
        in_specs=[in_vmem()] * len(arrays),
        out_specs=pl.BlockSpec(memory_space=pl.ANY),
        scratch_shapes=[pltpu.VMEM(shape, jnp.float32), pltpu.SemaphoreType.DMA((ROUNDS,))],
    )(*arrays)


def summed_in_place(traces, channel_slot):
    chan_count = lax.axis_size("chan")
    _, win_here, samples = traces.shape
    piece = HALF // BLOCKS
    scale = (2.0 / (win_here * chan_count * (samples // 2))) ** 0.5
    dft_rows = dft_rows_table(samples)
    same = selection(2 * LANES, 2 * LANES, [(n, n) for n in range(2 * LANES)])
    tables = [lag_rows_table(samples, scale), same]
    everywhere = tuple(range(BLOCKS))

    def over_sub(rows):
        return lax.ppermute(rows, "sub", [(0, 1), (1, 0)])

    def over_core(rows):
        return lax.ppermute(rows, "rep", [(0, 1), (1, 0)])

    def with_device(share, apart):
        return lax.ppermute(share, "chan", [(z, z ^ apart) for z in range(chan_count)])

    def after(value, *others):
        return lax.optimization_barrier((value,) + others)[0]

    def added(share, arrived):
        return (share.astype(jnp.float32) + arrived.astype(jnp.float32)).astype(jnp.bfloat16)

    def for_two_away(kinds):
        return [(i_other, j_other, there ^ 2) for i_other, j_other, there in kinds]

    mine, mine_far, mine_near = order_rows(traces, channel_slot, [everywhere, FAR, NEAR])
    far = over_sub(mine_far)
    near = over_sub(mine_near)

    own_i, own_j = spectra(mine, over_core(mine), (dft_rows, *own_picks()))
    own_left, own_right = (own_i, 0), (own_j, 0, everywhere)
    own_far, own_near = (0, 0, FAR[0]), (0, piece, NEAR[0])
    (kept_1, sent_far_1, own_1, sent_near_1), kinds_1 = partial_correlations(
        [own_left], [own_right], tables, [((0,), [own_far, own_near])], [(0,), (1,), (2,), (3,)]
    )
    arrived_far_1 = with_device(sent_far_1, 1)

    far, arrived_far_1 = lax.optimization_barrier((far, arrived_far_1))
    far_1 = with_device(added(kept_1, arrived_far_1), 2)
    far_i, far_j = spectra(far, over_core(far), (dft_rows, *half_picks()))
    far_left, far_right = (far_i, 1), (far_j, 1, FAR)
    other_far = (1, 0, FAR[0])
    (kept_2, sent_far_2, own_2, sent_near_2), kinds_2 = partial_correlations(
        [own_left, far_left],
        [own_right, far_right],
        tables,
        [((0,), [other_far]), ((1,), [own_far, own_near, other_far])],
        [(0,), (1,), (2,), (3,)],
    )
    sent_far_2, far_1 = lax.optimization_barrier((sent_far_2, far_1))
    arrived_far_2 = with_device(sent_far_2, 1)

    near, arrived_far_2 = lax.optimization_barrier((near, arrived_far_2))
    near_i, near_j = spectra(near, over_core(near), (dft_rows, *half_picks()))
    summed_2 = added(kept_2, arrived_far_2)
    far_2 = with_device(summed_2, 2)
    near_j = after(near_j, summed_2)
    near_left, near_right = (near_i, 1), (near_j, 1, NEAR)
    (kept_3, sent_far_3, own_3, sent_near_3), kinds_3 = partial_correlations(
        [own_left, far_left],
        [near_right],
        tables,
        [((0,), [own_far, other_far, own_near])],
        [(0,), (1,), (2,), (3,)],
    )
    arrived_far_3 = with_device(sent_far_3, 1)
    arrived_near = with_device(jnp.concatenate([sent_near_1, sent_near_2]), 1)
    near_right = (after(near_j, kept_3, sent_far_3, far_2, arrived_near), 1, NEAR)
    (own_4, sent_4), kinds_4 = partial_correlations(
        [near_left], [far_right, near_right], tables, [((0, 1), [(0, 0, NEAR[0])])], [(2,), (3,)]
    )
    arrived_4 = with_device(jnp.concatenate([sent_near_3, sent_4]), 1)
    summed_3 = added(after(kept_3, own_4), arrived_far_3)
    far_3 = with_device(summed_3, 2)
    near_left = (after(near_i, own_4, sent_4, summed_3), 1)
    (own_5, sent_5), kinds_5 = partial_correlations(
        [near_left], [own_right], tables, [((0,), [(0, 0, NEAR[0])])], [(2,), (3,)]
    )
    arrived_5 = with_device(sent_5, 1)
    shares = [
        (own_1, kinds_1[2]),
        (own_2, kinds_2[2]),
        (own_3, kinds_3[2]),
        (own_4, kinds_4[2]),
        (own_5, kinds_5[2]),
        (arrived_near, kinds_1[3] + kinds_2[3]),
        (arrived_4, kinds_3[3] + kinds_4[3]),
        (arrived_5, kinds_5[3]),
        (far_1, for_two_away(kinds_1[0])),
        (far_2, for_two_away(kinds_2[0])),
        (far_3, for_two_away(kinds_3[0])),
    ]
    return assembled(shares)


def from_behind(shard, axis, by):
    count = lax.axis_size(axis)
    return lax.ppermute(shard, axis, [(i, (i + by) % count) for i in range(count)])


def dft_columns(samples, parts, sub_bins):
    shape = (samples, parts, 2, sub_bins)
    time_pos = lax.broadcasted_iota(jnp.int32, shape, 0)
    range_pos = lax.broadcasted_iota(jnp.int32, shape, 1)
    part_pos = lax.broadcasted_iota(jnp.int32, shape, 2)
    bin_pos = lax.broadcasted_iota(jnp.int32, shape, 3)
    frequency = range_pos * sub_bins + bin_pos
    angles = jnp.mod(time_pos * frequency, samples).astype(jnp.float32) * (2.0 * math.pi / samples)
    entries = jnp.where(part_pos == 0, jnp.cos(angles), -jnp.sin(angles))
    return entries.reshape(samples, parts * 2 * sub_bins).astype(jnp.bfloat16)


def lag_table(sub_bins, first_bin, lag_count, samples):
    frequency = first_bin + lax.broadcasted_iota(jnp.int32, (sub_bins, lag_count), 0)
    lag_offset = lax.broadcasted_iota(jnp.int32, (sub_bins, lag_count), 1) - lag_count // 2
    angles = jnp.mod(frequency * lag_offset, samples).astype(jnp.float32) * (2.0 * math.pi / samples)
    return jnp.stack([jnp.cos(angles), -jnp.sin(angles)], axis=1)


def moved_spectra(traces, channel_slot):
    chan_count = lax.axis_size("chan")
    sub_count = lax.axis_size("sub")
    group_rows, win_here, samples = traces.shape
    bin_count = samples // 2
    sub_bins = bin_count // sub_count
    bin_width = 2 * sub_bins
    piece_len = group_rows // chan_count
    picked = jnp.take(traces, channel_slot, axis=0)
    dft_rows = dft_columns(samples, sub_count, sub_bins)
    spectrum = jnp.dot(picked.reshape(-1, samples), dft_rows, preferred_element_type=jnp.float32)
    energy = jnp.sum(spectrum * spectrum, axis=1, keepdims=True) / bin_count
    whitened = (spectrum * lax.rsqrt(energy + 1e-05)).astype(jnp.bfloat16)
    whitened = whitened.reshape(chan_count, piece_len, win_here, sub_count, bin_width)
    regrouped = lax.all_to_all(whitened, "chan", split_axis=0, concat_axis=0, tiled=True)
    regrouped = lax.all_to_all(regrouped, "sub", split_axis=3, concat_axis=3, tiled=True)
    own_half = regrouped.transpose(3, 1, 0, 2, 4).reshape(sub_count * piece_len, chan_count * win_here, bin_width)
    own_block = lax.all_gather(own_half, "rep", axis=0, tiled=True)
    windows = own_block.shape[1]
    own_split = own_block.reshape(own_block.shape[0], windows, 2, sub_bins)
    lag_rows = lag_table(sub_bins, lax.axis_index("sub") * sub_bins, LAGS, samples)
    lag_scale = (2.0 / (windows * bin_count)) ** 0.5
    results = []
    for step in range(1, ROUNDS + 1):
        partner = from_behind(own_half, "chan", -step)
        partner_split = partner.reshape(partner.shape[0], windows, 2, sub_bins)
        turned = jnp.stack([-partner_split[:, :, 1], partner_split[:, :, 0]], axis=2)
        partner_pair = jnp.stack([partner_split, turned], axis=0)
        cross_spec = jnp.einsum("iwpf,qjwpf->fqij", own_split, partner_pair, preferred_element_type=jnp.float32)
        summed = jnp.einsum("fqij,fql->ijl", cross_spec, lag_rows, precision=lax.Precision.HIGHEST)
        results.append(lax.psum_scatter(lag_scale * summed, "sub", scatter_dimension=0, tiled=True))
    return jnp.stack(results)[:, None]


def solution(mesh):
    sizes = mesh.shape
    in_place = sizes["chan"] == BLOCKS == ROUNDS + 1 and sizes["sub"] == 2 and sizes["rep"] == 2
    return jax.shard_map(
        summed_in_place if in_place else moved_spectra,
        mesh=mesh,
        in_specs=(P(("groups", "sub", "rep"), "chan", None), P(("groups", "sub", "rep"))),
        out_specs=P(None, ("groups", "chan"), "sub", "rep", None),
        check_vma=False,
    )
```

profile of v0, /device:TPU:0, one launch (start us, length us, event | category | flops | bytes accessed | tf_op | source)
XLA Modules:
  0.0 102.5 jit_solution(5327672507434761185)
XLA Ops:
  0.7 2.3 %order_rows.1 = (bf16[32,64,512]{2,1,0:T(8,128)(2,1)S(1)}, bf16[32,32,512]{2,1,0:T(8,128)(2,1)S(1)}, bf16[32,32,512]{2,1,0:T(8,128)(2,1)S(1)}) custom-call(s32[64]{0:T(128)S(1)} %copy-done.2, bf16[64,32,512]{2,1,0:T(8,128)(2,1)} %traces_ref.1), custom_call_target="tpu_custom_call" | custom-call | bytes 6291456 | tf_op jit(solution)/shard_map/order_rows/pallas_call | solution.py:147
  3.5 2.6 %collective-permute-start.1 = (bf16[32,32,512]{2,1,0:T(8,128)(2,1)S(1)}, bf16[32,32,512]{2,1,0:T(8,128)(2,1)S(1)}, u32[]{:S(2)}, u32[]{:S(2)}) collective-permute-start(bf16[32,32,512]{2,1,0:T(8,128)(2,1)S(1)} %get-tuple-element.44), channel_id=1, source_target_pairs={{0,2},{2,0},{1,3},{3,1},{4,6},{6,4},{5,7},{7,5},{8,10},{10,8},{9,1... | collective-permute-start | bytes 3145736 | tf_op jit(solution)/shard_map/ppermute | solution.py:461
  7.3 10.5 %spectra.3 = (bf16[256,32,128]{2,1,0:T(8,128)(2,1)S(1)}, bf16[256,64,128]{2,1,0:T(8,128)(2,1)S(1)}) custom-call(bf16[32,64,512]{2,1,0:T(8,128)(2,1)S(1)} %get-tuple-element.40.j_ref, bf16[32,64,512]{2,1,0:T(8,128)(2,1)S(1)} %collective-permute-done.i_ref, bf16[512,512]{1,0:T(8,128)(2,1)S(1)} %copy-done.3, bf16[32,256]{1,0:T(8,128)(2,1)S(1)} %copy-done.7, ...), custom_call_target="tpu_custom_call" | custom-call | flops 2147483648 | bytes 8388608 | tf_op jit(solution)/shard_map/spectra/pallas_call | solution.py:253
  17.8 4.8 %partial_correlations.5 = (bf16[3,16,16,128]{3,2,1,0:T(8,128)(2,1)S(1)}, bf16[3,16,16,128]{3,2,1,0:T(8,128)(2,1)S(1)}, f32[3,16,16,128]{3,2,1,0:T(8,128)S(1)}, bf16[3,16,16,128]{3,2,1,0:T(8,128)(2,1)S(1)}) custom-call(bf16[256,32,128]{2,1,0:T(8,128)(2,1)S(1)} %get-tuple-element.41.refs_0_, bf16[256,64,128]{2,1,0:T(8,128)(2,1)S(1)} %get-tuple-element.42.refs_1_.refs_2_, ...), custom_call_target="tpu_custom_call" | custom-call | flops 805306368 | bytes 6291456 | tf_op jit(solution)/shard_map/partial_correlations/pallas_call | solution.py:394
  22.6 3.0 %collective-permute-start.2 = (bf16[3,16,16,128]{3,2,1,0:T(8,128)(2,1)S(1)}, bf16[3,16,16,128]{3,2,1,0:T(8,128)(2,1)S(1)}, u32[]{:S(2)}, u32[]{:S(2)}) collective-permute-start(bf16[3,16,16,128]{3,2,1,0:T(8,128)(2,1)S(1)} %get-tuple-element.45), channel_id=1, source_target_pairs={{0,4},{4,0},{8,12},{12,8},{1,5},{5,1},{9,13},{13,9},{2,6},{6,2},{1... | collective-permute-start | bytes 589832 | tf_op jit(solution)/shard_map/ppermute | solution.py:467
  25.6 4.2 %collective-permute-done.1.j_ref = bf16[32,32,512]{2,1,0:T(8,128)(2,1)S(1)} collective-permute-done((bf16[32,32,512]{2,1,0:T(8,128)(2,1)S(1)}, bf16[32,32,512]{2,1,0:T(8,128)(2,1)S(1)}, u32[]{:S(2)}, u32[]{:S(2)}) %collective-permute-start.1) | collective-permute-done | bytes 1048608 | tf_op jit(solution)/shard_map/ppermute | solution.py:461
  30.8 1.7 %collective-permute-start.4 = (bf16[32,32,512]{2,1,0:T(8,128)(2,1)S(1)}, bf16[32,32,512]{2,1,0:T(8,128)(2,1)S(1)}, u32[]{:S(2)}, u32[]{:S(2)}) collective-permute-start(bf16[32,32,512]{2,1,0:T(8,128)(2,1)S(1)} %get-tuple-element.50), channel_id=1, source_target_pairs={{0,2},{2,0},{1,3},{3,1},{4,6},{6,4},{5,7},{7,5},{8,10},{10,8},{9,1... | collective-permute-start | bytes 3145736 | tf_op jit(solution)/shard_map/ppermute | solution.py:461
  32.5 2.7 %collective-permute-start.5 = (bf16[3,16,16,128]{3,2,1,0:T(8,128)(2,1)S(1)}, bf16[3,16,16,128]{3,2,1,0:T(8,128)(2,1)S(1)}, u32[]{:S(2)}, u32[]{:S(2)}) collective-permute-start(bf16[3,16,16,128]{3,2,1,0:T(8,128)(2,1)S(1)} %add_convert_fusion.2), channel_id=1, source_target_pairs={{0,8},{4,12},{8,0},{12,4},{1,9},{5,13},{9,1},{13,5},{2,10},{6,14},... | collective-permute-start | bytes 589832 | tf_op jit(solution)/shard_map/ppermute | solution.py:467
  35.2 6.8 %spectra.4 = (bf16[256,16,128]{2,1,0:T(8,128)(2,1)S(1)}, bf16[256,64,128]{2,1,0:T(8,128)(2,1)S(1)}) custom-call(bf16[32,32,512]{2,1,0:T(8,128)(2,1)S(1)} %collective-permute-done.1.j_ref, bf16[32,32,512]{2,1,0:T(8,128)(2,1)S(1)} %collective-permute-done.3.i_ref, bf16[512,512]{1,0:T(8,128)(2,1)S(1)} %copy-done.3, bf16[32,256]{1,0:T(8,128)(2,1)S(1)} %copy-done.6, ...), custom_call_target="tpu_custom_call" | custom-call | flops 1073741824 | bytes 4194304 | tf_op jit(solution)/shard_map/spectra/pallas_call | solution.py:253
  41.9 8.3 %partial_correlations.6 = (bf16[5,16,16,128]{3,2,1,0:T(8,128)(2,1)S(1)}, bf16[5,16,16,128]{3,2,1,0:T(8,128)(2,1)S(1)}, f32[2,16,16,128]{3,2,1,0:T(8,128)S(1)}, bf16[2,16,16,128]{3,2,1,0:T(8,128)(2,1)S(1)}) custom-call(bf16[256,32,128]{2,1,0:T(8,128)(2,1)S(1)} %get-tuple-element.41.refs_0_, bf16[256,16,128]{2,1,0:T(8,128)(2,1)S(1)} %get-tuple-element.47.refs_1_, ...), custom_call_target="tpu_custom_call" | custom-call | flops 1610612736 | bytes 11534336 | tf_op jit(solution)/shard_map/partial_correlations/pallas_call | solution.py:394
  50.3 1.6 %collective-permute-start.6 = (bf16[5,16,16,128]{3,2,1,0:T(8,128)(2,1)S(1)}, bf16[5,16,16,128]{3,2,1,0:T(8,128)(2,1)S(1)}, u32[]{:S(2)}, u32[]{:S(2)}) collective-permute-start(bf16[5,16,16,128]{3,2,1,0:T(8,128)(2,1)S(1)} %get-tuple-element.54), channel_id=1, source_target_pairs={{0,4},{4,0},{8,12},{12,8},{1,5},{5,1},{9,13},{13,9},{2,6},{6,2},{1... | collective-permute-start | bytes 983048 | tf_op jit(solution)/shard_map/ppermute | solution.py:467
  51.9 4.5 %collective-permute-done.4.j_ref = bf16[32,32,512]{2,1,0:T(8,128)(2,1)S(1)} collective-permute-done((bf16[32,32,512]{2,1,0:T(8,128)(2,1)S(1)}, bf16[32,32,512]{2,1,0:T(8,128)(2,1)S(1)}, u32[]{:S(2)}, u32[]{:S(2)}) %collective-permute-start.4) | collective-permute-done | bytes 1048608 | tf_op jit(solution)/shard_map/ppermute | solution.py:461
  56.4 3.5 %collective-permute-done.6 = bf16[5,16,16,128]{3,2,1,0:T(8,128)(2,1)S(1)} collective-permute-done((bf16[5,16,16,128]{3,2,1,0:T(8,128)(2,1)S(1)}, bf16[5,16,16,128]{3,2,1,0:T(8,128)(2,1)S(1)}, u32[]{:S(2)}, u32[]{:S(2)}) %collective-permute-start.6) | collective-permute-done | bytes 327712 | tf_op jit(solution)/shard_map/ppermute | solution.py:467
  59.9 1.6 %collective-permute-start.9 = (bf16[5,16,16,128]{3,2,1,0:T(8,128)(2,1)S(1)}, bf16[5,16,16,128]{3,2,1,0:T(8,128)(2,1)S(1)}, u32[]{:S(2)}, u32[]{:S(2)}) collective-permute-start(bf16[5,16,16,128]{3,2,1,0:T(8,128)(2,1)S(1)} %pad_maximum_fusion), channel_id=1, source_target_pairs={{0,4},{4,0},{8,12},{12,8},{1,5},{5,1},{9,13},{13,9},{2,6},{6,2},{1... | collective-permute-start | bytes 983048 | tf_op jit(solution)/shard_map/ppermute | solution.py:467
  61.7 1.3 %collective-permute-start.8 = (bf16[5,16,16,128]{3,2,1,0:T(8,128)(2,1)S(1)}, bf16[5,16,16,128]{3,2,1,0:T(8,128)(2,1)S(1)}, u32[]{:S(2)}, u32[]{:S(2)}) collective-permute-start(bf16[5,16,16,128]{3,2,1,0:T(8,128)(2,1)S(1)} %add_convert_fusion), channel_id=1, source_target_pairs={{0,8},{4,12},{8,0},{12,4},{1,9},{5,13},{9,1},{13,5},{2,10},{6,14},... | collective-permute-start | bytes 983048 | tf_op jit(solution)/shard_map/ppermute | solution.py:467
  62.9 6.7 %spectra.5 = (bf16[256,16,128]{2,1,0:T(8,128)(2,1)S(1)}, bf16[256,64,128]{2,1,0:T(8,128)(2,1)S(1)}) custom-call(bf16[32,32,512]{2,1,0:T(8,128)(2,1)S(1)} %collective-permute-done.4.j_ref, bf16[32,32,512]{2,1,0:T(8,128)(2,1)S(1)} %collective-permute-done.7.i_ref, bf16[512,512]{1,0:T(8,128)(2,1)S(1)} %copy-done.3, bf16[32,256]{1,0:T(8,128)(2,1)S(1)} %copy-done.6, ...), custom_call_target="tpu_custom_call" | custom-call | flops 1073741824 | bytes 4194304 | tf_op jit(solution)/shard_map/spectra/pallas_call | solution.py:253
  69.7 5.7 %partial_correlations.7 = (bf16[4,16,16,128]{3,2,1,0:T(8,128)(2,1)S(1)}, bf16[4,16,16,128]{3,2,1,0:T(8,128)(2,1)S(1)}, f32[1,16,16,128]{3,2,1,0:T(8,128)S(1)}, bf16[1,16,16,128]{3,2,1,0:T(8,128)(2,1)S(1)}) custom-call(bf16[256,32,128]{2,1,0:T(8,128)(2,1)S(1)} %get-tuple-element.41.refs_0_, bf16[256,16,128]{2,1,0:T(8,128)(2,1)S(1)} %get-tuple-element.47.refs_1_, ...), custom_call_target="tpu_custom_call" | custom-call | flops 1207959552 | bytes 7340032 | tf_op jit(solution)/shard_map/partial_correlations/pallas_call | solution.py:394
  75.4 1.3 %collective-permute-start.10 = (bf16[4,16,16,128]{3,2,1,0:T(8,128)(2,1)S(1)}, bf16[4,16,16,128]{3,2,1,0:T(8,128)(2,1)S(1)}, u32[]{:S(2)}, u32[]{:S(2)}) collective-permute-start(bf16[4,16,16,128]{3,2,1,0:T(8,128)(2,1)S(1)} %get-tuple-element.63), channel_id=1, source_target_pairs={{0,4},{4,0},{8,12},{12,8},{1,5},{5,1},{9,13},{13,9},{2,6},{6,2},{1... | collective-permute-start | bytes 786440 | tf_op jit(solution)/shard_map/ppermute | solution.py:467
  76.7 3.0 %collective-permute-done.8.refs_9_ = bf16[5,16,16,128]{3,2,1,0:T(8,128)(2,1)S(1)} collective-permute-done((bf16[5,16,16,128]{3,2,1,0:T(8,128)(2,1)S(1)}, bf16[5,16,16,128]{3,2,1,0:T(8,128)(2,1)S(1)}, u32[]{:S(2)}, u32[]{:S(2)}) %collective-permute-start.8) | collective-permute-done | bytes 327712 | tf_op jit(solution)/shard_map/ppermute | solution.py:467
  79.6 4.0 %partial_correlations.8 = (f32[3,16,16,128]{3,2,1,0:T(8,128)S(1)}, bf16[3,16,16,128]{3,2,1,0:T(8,128)(2,1)S(1)}) custom-call(bf16[256,16,128]{2,1,0:T(8,128)(2,1)S(1)} %get-tuple-element.70.refs_0_, bf16[256,64,128]{2,1,0:T(8,128)(2,1)S(1)} %get-tuple-element.48.refs_3_.refs_1_, bf16[256,64,128]{2,1,0:T(8,128)(2,1)S(1)} %get-tuple-element.66.refs_2_, ...), custom_call_target="tpu_custom_call" | custom-call | flops 402653184 | bytes 9437184 | tf_op jit(solution)/shard_map/partial_correlations/pallas_call | solution.py:394
  83.8 1.4 %collective-permute-done.10 = bf16[4,16,16,128]{3,2,1,0:T(8,128)(2,1)S(1)} collective-permute-done((bf16[4,16,16,128]{3,2,1,0:T(8,128)(2,1)S(1)}, bf16[4,16,16,128]{3,2,1,0:T(8,128)(2,1)S(1)}, u32[]{:S(2)}, u32[]{:S(2)}) %collective-permute-start.10) | collective-permute-done | bytes 262176 | tf_op jit(solution)/shard_map/ppermute | solution.py:467
  85.5 4.0 %partial_correlations.9 = (f32[3,16,16,128]{3,2,1,0:T(8,128)S(1)}, bf16[3,16,16,128]{3,2,1,0:T(8,128)(2,1)S(1)}) custom-call(bf16[256,16,128]{2,1,0:T(8,128)(2,1)S(1)} %get-tuple-element.70.refs_0_, bf16[256,64,128]{2,1,0:T(8,128)(2,1)S(1)} %get-tuple-element.42.refs_1_.refs_2_, bf16[128,512]{1,0:T(8,128)(2,1)S(1)} %copy-done, bf16[256,256]{1,0:T(8,128)(2,1)S(1)} %copy-done.1), custom_call_target="tpu_custom_call" | custom-call | flops 402653184 | bytes 5242880 | tf_op jit(solution)/shard_map/partial_correlations/pallas_call | solution.py:394
  90.4 4.4 %collective-permute-done.11.refs_6_ = bf16[4,16,16,128]{3,2,1,0:T(8,128)(2,1)S(1)} collective-permute-done((bf16[4,16,16,128]{3,2,1,0:T(8,128)(2,1)S(1)}, bf16[4,16,16,128]{3,2,1,0:T(8,128)(2,1)S(1)}, u32[]{:S(2)}, u32[]{:S(2)}) %collective-permute-start.11) | collective-permute-done | bytes 262176 | tf_op jit(solution)/shard_map/ppermute | solution.py:467
  94.8 6.3 %collective-permute-done.12.refs_7_ = bf16[3,16,16,128]{3,2,1,0:T(8,128)(2,1)S(1)} collective-permute-done((bf16[3,16,16,128]{3,2,1,0:T(8,128)(2,1)S(1)}, bf16[3,16,16,128]{3,2,1,0:T(8,128)(2,1)S(1)}, u32[]{:S(2)}, u32[]{:S(2)}) %collective-permute-start.12) | collective-permute-done | bytes 196640 | tf_op jit(solution)/shard_map/ppermute | solution.py:467
  (35 shorter events, 6.2 us)
Async XLA Ops:
  0.0 0.7 copy-start.2
  0.7 6.6 %copy-start.3 = (bf16[512,512]{1,0:T(8,128)(2,1)S(1)}, bf16[512,512]{1,0:T(8,128)(2,1)}, u32[]{:S(2)}) copy-start(bf16[512,512]{1,0:T(8,128)(2,1)} %constant.21.table_ref) | copy-start | bytes 1572868
  0.7 6.6 %copy-start.5 = (bf16[128,128]{1,0:T(8,128)(2,1)S(1)}, bf16[128,128]{1,0:T(8,128)(2,1)}, u32[]{:S(2)}) copy-start(bf16[128,128]{1,0:T(8,128)(2,1)} %constant.23.to_j_ref) | copy-start | bytes 98308
  0.7 6.6 %copy-start.7 = (bf16[32,256]{1,0:T(8,128)(2,1)S(1)}, bf16[32,256]{1,0:T(8,128)(2,1)}, u32[]{:S(2)}) copy-start(bf16[32,256]{1,0:T(8,128)(2,1)} %constant.22.to_i_ref) | copy-start | bytes 49156
  2.9 4.3 %collective-permute-start = (bf16[32,64,512]{2,1,0:T(8,128)(2,1)S(1)}, bf16[32,64,512]{2,1,0:T(8,128)(2,1)S(1)}, u32[]{:S(2)}, u32[]{:S(2)}) collective-permute-start(bf16[32,64,512]{2,1,0:T(8,128)(2,1)S(1)} %get-tuple-element.40.j_ref), channel_id=1, source_target_pairs={{0,1},{1,0},{2,3},{3,2},{4,5},{5,4},{6,7},{7,6},{8,9},{9,8},{10,11... | collective-permute-start | bytes 6291464 | tf_op jit(solution)/shard_map/ppermute | solution.py:464
  3.5 14.3 %copy-start = (bf16[128,512]{1,0:T(8,128)(2,1)S(1)}, bf16[128,512]{1,0:T(8,128)(2,1)}, u32[]{:S(2)}) copy-start(bf16[128,512]{1,0:T(8,128)(2,1)} %constant.24.refs_2_.refs_4_.refs_3_) | copy-start | bytes 393220
  3.5 14.3 %copy-start.1 = (bf16[256,256]{1,0:T(8,128)(2,1)S(1)}, bf16[256,256]{1,0:T(8,128)(2,1)}, u32[]{:S(2)}) copy-start(bf16[256,256]{1,0:T(8,128)(2,1)} %constant.25.refs_3_.refs_5_.refs_4_) | copy-start | bytes 393220
  3.5 26.3 %collective-permute-start.1 = (bf16[32,32,512]{2,1,0:T(8,128)(2,1)S(1)}, bf16[32,32,512]{2,1,0:T(8,128)(2,1)S(1)}, u32[]{:S(2)}, u32[]{:S(2)}) collective-permute-start(bf16[32,32,512]{2,1,0:T(8,128)(2,1)S(1)} %get-tuple-element.44), channel_id=1, source_target_pairs={{0,2},{2,0},{1,3},{3,1},{4,6},{6,4},{5,7},{7,5},{8,10},{10,8},{9,1... | collective-permute-start | bytes 3145736 | tf_op jit(solution)/shard_map/ppermute | solution.py:461
  17.7 17.4 %copy-start.4 = (bf16[128,256]{1,0:T(8,128)(2,1)S(1)}, bf16[128,256]{1,0:T(8,128)(2,1)}, u32[]{:S(2)}) copy-start(bf16[128,256]{1,0:T(8,128)(2,1)} %constant.27.to_j_ref) | copy-start | bytes 196612
  17.8 17.4 %copy-start.6 = (bf16[32,256]{1,0:T(8,128)(2,1)S(1)}, bf16[32,256]{1,0:T(8,128)(2,1)}, u32[]{:S(2)}) copy-start(bf16[32,256]{1,0:T(8,128)(2,1)} %constant.26.to_i_ref) | copy-start | bytes 49156
  22.6 8.2 %collective-permute-start.2 = (bf16[3,16,16,128]{3,2,1,0:T(8,128)(2,1)S(1)}, bf16[3,16,16,128]{3,2,1,0:T(8,128)(2,1)S(1)}, u32[]{:S(2)}, u32[]{:S(2)}) collective-permute-start(bf16[3,16,16,128]{3,2,1,0:T(8,128)(2,1)S(1)} %get-tuple-element.45), channel_id=1, source_target_pairs={{0,4},{4,0},{8,12},{12,8},{1,5},{5,1},{9,13},{13,9},{2,6},{6,2},{1... | collective-permute-start | bytes 589832 | tf_op jit(solution)/shard_map/ppermute | solution.py:467
  30.8 4.4 %collective-permute-start.3 = (bf16[32,32,512]{2,1,0:T(8,128)(2,1)S(1)}, bf16[32,32,512]{2,1,0:T(8,128)(2,1)S(1)}, u32[]{:S(2)}, u32[]{:S(2)}) collective-permute-start(bf16[32,32,512]{2,1,0:T(8,128)(2,1)S(1)} %collective-permute-done.1.j_ref), channel_id=1, source_target_pairs={{0,1},{1,0},{2,3},{3,2},{4,5},{5,4},{6,7},{7,6},{8,9},{9,8},{10,11... | collective-permute-start | bytes 3145736 | tf_op jit(solution)/shard_map/ppermute | solution.py:464
  30.8 25.6 %collective-permute-start.4 = (bf16[32,32,512]{2,1,0:T(8,128)(2,1)S(1)}, bf16[32,32,512]{2,1,0:T(8,128)(2,1)S(1)}, u32[]{:S(2)}, u32[]{:S(2)}) collective-permute-start(bf16[32,32,512]{2,1,0:T(8,128)(2,1)S(1)} %get-tuple-element.50), channel_id=1, source_target_pairs={{0,2},{2,0},{1,3},{3,1},{4,6},{6,4},{5,7},{7,5},{8,10},{10,8},{9,1... | collective-permute-start | bytes 3145736 | tf_op jit(solution)/shard_map/ppermute | solution.py:461
  32.5 17.7 %collective-permute-start.5 = (bf16[3,16,16,128]{3,2,1,0:T(8,128)(2,1)S(1)}, bf16[3,16,16,128]{3,2,1,0:T(8,128)(2,1)S(1)}, u32[]{:S(2)}, u32[]{:S(2)}) collective-permute-start(bf16[3,16,16,128]{3,2,1,0:T(8,128)(2,1)S(1)} %add_convert_fusion.2), channel_id=1, source_target_pairs={{0,8},{4,12},{8,0},{12,4},{1,9},{5,13},{9,1},{13,5},{2,10},{6,14},... | collective-permute-start | bytes 589832 | tf_op jit(solution)/shard_map/ppermute | solution.py:467
  50.3 9.6 %collective-permute-start.6 = (bf16[5,16,16,128]{3,2,1,0:T(8,128)(2,1)S(1)}, bf16[5,16,16,128]{3,2,1,0:T(8,128)(2,1)S(1)}, u32[]{:S(2)}, u32[]{:S(2)}) collective-permute-start(bf16[5,16,16,128]{3,2,1,0:T(8,128)(2,1)S(1)} %get-tuple-element.54), channel_id=1, source_target_pairs={{0,4},{4,0},{8,12},{12,8},{1,5},{5,1},{9,13},{13,9},{2,6},{6,2},{1... | collective-permute-start | bytes 983048 | tf_op jit(solution)/shard_map/ppermute | solution.py:467
  59.9 3.0 %collective-permute-start.7 = (bf16[32,32,512]{2,1,0:T(8,128)(2,1)S(1)}, bf16[32,32,512]{2,1,0:T(8,128)(2,1)S(1)}, u32[]{:S(2)}, u32[]{:S(2)}) collective-permute-start(bf16[32,32,512]{2,1,0:T(8,128)(2,1)S(1)} %collective-permute-done.4.j_ref), channel_id=1, source_target_pairs={{0,1},{1,0},{2,3},{3,2},{4,5},{5,4},{6,7},{7,6},{8,9},{9,8},{10,11... | collective-permute-start | bytes 3145736 | tf_op jit(solution)/shard_map/ppermute | solution.py:464
  59.9 16.7 %collective-permute-start.9 = (bf16[5,16,16,128]{3,2,1,0:T(8,128)(2,1)S(1)}, bf16[5,16,16,128]{3,2,1,0:T(8,128)(2,1)S(1)}, u32[]{:S(2)}, u32[]{:S(2)}) collective-permute-start(bf16[5,16,16,128]{3,2,1,0:T(8,128)(2,1)S(1)} %pad_maximum_fusion), channel_id=1, source_target_pairs={{0,4},{4,0},{8,12},{12,8},{1,5},{5,1},{9,13},{13,9},{2,6},{6,2},{1... | collective-permute-start | bytes 983048 | tf_op jit(solution)/shard_map/ppermute | solution.py:467
  61.7 18.0 %collective-permute-start.8 = (bf16[5,16,16,128]{3,2,1,0:T(8,128)(2,1)S(1)}, bf16[5,16,16,128]{3,2,1,0:T(8,128)(2,1)S(1)}, u32[]{:S(2)}, u32[]{:S(2)}) collective-permute-start(bf16[5,16,16,128]{3,2,1,0:T(8,128)(2,1)S(1)} %add_convert_fusion), channel_id=1, source_target_pairs={{0,8},{4,12},{8,0},{12,4},{1,9},{5,13},{9,1},{13,5},{2,10},{6,14},... | collective-permute-start | bytes 983048 | tf_op jit(solution)/shard_map/ppermute | solution.py:467
  75.4 9.8 %collective-permute-start.10 = (bf16[4,16,16,128]{3,2,1,0:T(8,128)(2,1)S(1)}, bf16[4,16,16,128]{3,2,1,0:T(8,128)(2,1)S(1)}, u32[]{:S(2)}, u32[]{:S(2)}) collective-permute-start(bf16[4,16,16,128]{3,2,1,0:T(8,128)(2,1)S(1)} %get-tuple-element.63), channel_id=1, source_target_pairs={{0,4},{4,0},{8,12},{12,8},{1,5},{5,1},{9,13},{13,9},{2,6},{6,2},{1... | collective-permute-start | bytes 786440 | tf_op jit(solution)/shard_map/ppermute | solution.py:467
  83.7 11.1 %collective-permute-start.11 = (bf16[4,16,16,128]{3,2,1,0:T(8,128)(2,1)S(1)}, bf16[4,16,16,128]{3,2,1,0:T(8,128)(2,1)S(1)}, u32[]{:S(2)}, u32[]{:S(2)}) collective-permute-start(bf16[4,16,16,128]{3,2,1,0:T(8,128)(2,1)S(1)} %pad_maximum_fusion.1), channel_id=1, source_target_pairs={{0,4},{4,0},{8,12},{12,8},{1,5},{5,1},{9,13},{13,9},{2,6},{6,2},{1... | collective-permute-start | bytes 786440 | tf_op jit(solution)/shard_map/ppermute | solution.py:467
  85.2 15.9 %collective-permute-start.13 = (bf16[4,16,16,128]{3,2,1,0:T(8,128)(2,1)S(1)}, bf16[4,16,16,128]{3,2,1,0:T(8,128)(2,1)S(1)}, u32[]{:S(2)}, u32[]{:S(2)}) collective-permute-start(bf16[4,16,16,128]{3,2,1,0:T(8,128)(2,1)S(1)} %add_convert_fusion.1), channel_id=1, source_target_pairs={{0,8},{4,12},{8,0},{12,4},{1,9},{5,13},{9,1},{13,5},{2,10},{6,14},... | collective-permute-start | bytes 786440 | tf_op jit(solution)/shard_map/ppermute | solution.py:467
  89.5 11.6 %collective-permute-start.12 = (bf16[3,16,16,128]{3,2,1,0:T(8,128)(2,1)S(1)}, bf16[3,16,16,128]{3,2,1,0:T(8,128)(2,1)S(1)}, u32[]{:S(2)}, u32[]{:S(2)}) collective-permute-start(bf16[3,16,16,128]{3,2,1,0:T(8,128)(2,1)S(1)} %get-tuple-element.73), channel_id=1, source_target_pairs={{0,4},{4,0},{8,12},{12,8},{1,5},{5,1},{9,13},{13,9},{2,6},{6,2},{1... | collective-permute-start | bytes 589832 | tf_op jit(solution)/shard_map/ppermute | solution.py:467
where the time goes:
time: 103 us
  Pallas kernels  54.3 us (53%)
  waiting for transfers between devices  29.4 us (29%)
  starting transfers between devices  17.5 us (17%)
    pallas_call x5, Pallas kernels, partial_correlations(): kernel_call(kernel, 'partial_correlations', 4 * total * bins * depth * LA...  26.8 us
    pallas_call x3, Pallas kernels, spectra(): kernel_call(kernel, 'spectra', 4 * samples * samples * wins * given, 4 *...  23.9 us
    ppermute x9, waiting for transfers between devices, with_device(): lax.ppermute(share, 'chan', [(z, z ^ apart) for z in range(chan_count)])  19.6 us
    ppermute x9, starting transfers between devices, with_device(): lax.ppermute(share, 'chan', [(z, z ^ apart) for z in range(chan_count)])  12.7 us
    ppermute x2, waiting for transfers between devices, over_sub(): return lax.ppermute(rows, 'sub', [(0, 1), (1, 0)])  8.65 us
    ppermute x2, starting transfers between devices, over_sub(): return lax.ppermute(rows, 'sub', [(0, 1), (1, 0)])  4.24 us
    pallas_call x1, Pallas kernels, order_rows(): kernel_call(kernel, 'order_rows', 0, 3 * traces.size * 2, vmem_bytes=ORDE...  2.28 us
  transfers between devices with their start and end apart: 14, of which 9 were waited for; matrix products, arithmetic and copies ran while one was open for 0% of the time, Pallas kernels for 50%

commit v1 on v0

--- a/solution.py
+++ b/solution.py
@@ -489,6 +489,7 @@
 
     far, arrived_far_1 = lax.optimization_barrier((far, arrived_far_1))
     far_1 = with_device(added(kept_1, arrived_far_1), 2)
+    arrived_near_1 = with_device(sent_near_1, 1)
     far_i, far_j = spectra(far, over_core(far), (dft_rows, *half_picks()))
     far_left, far_right = (far_i, 1), (far_j, 1, FAR)
     other_far = (1, 0, FAR[0])
@@ -499,7 +500,7 @@
         [((0,), [other_far]), ((1,), [own_far, own_near, other_far])],
         [(0,), (1,), (2,), (3,)],
     )
-    sent_far_2, far_1 = lax.optimization_barrier((sent_far_2, far_1))
+    sent_far_2, far_1, arrived_near_1 = lax.optimization_barrier((sent_far_2, far_1, arrived_near_1))
     arrived_far_2 = with_device(sent_far_2, 1)
 
     near, arrived_far_2 = lax.optimization_barrier((near, arrived_far_2))
@@ -516,8 +517,8 @@
         [(0,), (1,), (2,), (3,)],
     )
     arrived_far_3 = with_device(sent_far_3, 1)
-    arrived_near = with_device(jnp.concatenate([sent_near_1, sent_near_2]), 1)
-    near_right = (after(near_j, kept_3, sent_far_3, far_2, arrived_near), 1, NEAR)
+    arrived_near_2 = with_device(sent_near_2, 1)
+    near_right = (after(near_j, kept_3, sent_far_3, far_2, arrived_near_2), 1, NEAR)
     (own_4, sent_4), kinds_4 = partial_correlations(
         [near_left], [far_right, near_right], tables, [((0, 1), [(0, 0, NEAR[0])])], [(2,), (3,)]
     )
@@ -535,7 +536,8 @@
         (own_3, kinds_3[2]),
         (own_4, kinds_4[2]),
         (own_5, kinds_5[2]),
-        (arrived_near, kinds_1[3] + kinds_2[3]),
+        (arrived_near_1, kinds_1[3]),
+        (arrived_near_2, kinds_2[3]),
         (arrived_4, kinds_3[3] + kinds_4[3]),
         (arrived_5, kinds_5[3]),
         (far_1, for_two_away(kinds_1[0])),

time: 103 us -> 103 us (level)
  waiting for transfers between devices: 29.4 us -> 30.5 us
    ppermute x9 -> x10, starting transfers between devices: 12.7 us -> 12.2 us  [with_device(): lax.ppermute(share, 'chan', [(z, z ^ apart) for z in range(chan_count)])]
    ppermute x9 -> x10, waiting for transfers between devices: 19.6 us -> 20.1 us  [with_device(): lax.ppermute(share, 'chan', [(z, z ^ apart) for z in range(chan_count)])]
  transfers between devices with their start and end apart: 14 -> 15, of which waited for: 9 -> 10; matrix products, arithmetic and copies ran while one was open for 0% -> 0% of each run, Pallas kernels for 50% -> 49%
where the time goes in v1:
time: 103 us
  Pallas kernels  54.3 us (53%)
  waiting for transfers between devices  30.5 us (30%)
  starting transfers between devices  16.9 us (16%)
    pallas_call x5, Pallas kernels, partial_correlations(): kernel_call(kernel, 'partial_correlations', 4 * total * bins * depth * LA...  26.8 us
    pallas_call x3, Pallas kernels, spectra(): kernel_call(kernel, 'spectra', 4 * samples * samples * wins * given, 4 *...  23.9 us
    ppermute x10, waiting for transfers between devices, with_device(): lax.ppermute(share, 'chan', [(z, z ^ apart) for z in range(chan_count)])  20.1 us
    ppermute x10, starting transfers between devices, with_device(): lax.ppermute(share, 'chan', [(z, z ^ apart) for z in range(chan_count)])  12.2 us
    ppermute x2, waiting for transfers between devices, over_sub(): return lax.ppermute(rows, 'sub', [(0, 1), (1, 0)])  8.2 us
    ppermute x2, starting transfers between devices, over_sub(): return lax.ppermute(rows, 'sub', [(0, 1), (1, 0)])  4.24 us
    pallas_call x1, Pallas kernels, order_rows(): kernel_call(kernel, 'order_rows', 0, 3 * traces.size * 2, vmem_bytes=ORDE...  2.28 us
    ppermute x3, waiting for transfers between devices, over_core(): return lax.ppermute(rows, 'rep', [(0, 1), (1, 0)])  2.21 us
  transfers between devices with their start and end apart: 15, of which 10 were waited for; matrix products, arithmetic and copies ran while one was open for 0% of the time, Pallas kernels for 49%

profile of v1, /device:TPU:0, one launch (start us, length us, event | category | flops | bytes accessed | tf_op | source)
XLA Modules:
  0.0 102.9 jit_solution(18136374824821338472)
XLA Ops:
  0.7 2.3 %order_rows.1 = (bf16[32,64,512]{2,1,0:T(8,128)(2,1)S(1)}, bf16[32,32,512]{2,1,0:T(8,128)(2,1)S(1)}, bf16[32,32,512]{2,1,0:T(8,128)(2,1)S(1)}) custom-call(s32[64]{0:T(128)S(1)} %copy-done.2, bf16[64,32,512]{2,1,0:T(8,128)(2,1)} %traces_ref.1), custom_call_target="tpu_custom_call" | custom-call | bytes 6291456 | tf_op jit(solution)/shard_map/order_rows/pallas_call | solution.py:147
  3.5 2.6 %collective-permute-start.1 = (bf16[32,32,512]{2,1,0:T(8,128)(2,1)S(1)}, bf16[32,32,512]{2,1,0:T(8,128)(2,1)S(1)}, u32[]{:S(2)}, u32[]{:S(2)}) collective-permute-start(bf16[32,32,512]{2,1,0:T(8,128)(2,1)S(1)} %get-tuple-element.45), channel_id=1, source_target_pairs={{0,2},{2,0},{1,3},{3,1},{4,6},{6,4},{5,7},{7,5},{8,10},{10,8},{9,1... | collective-permute-start | bytes 3145736 | tf_op jit(solution)/shard_map/ppermute | solution.py:461
  6.1 1.2 %collective-permute-done.i_ref = bf16[32,64,512]{2,1,0:T(8,128)(2,1)S(1)} collective-permute-done((bf16[32,64,512]{2,1,0:T(8,128)(2,1)S(1)}, bf16[32,64,512]{2,1,0:T(8,128)(2,1)S(1)}, u32[]{:S(2)}, u32[]{:S(2)}) %collective-permute-start) | collective-permute-done | bytes 2097184 | tf_op jit(solution)/shard_map/ppermute | solution.py:464
  7.3 10.5 %spectra.3 = (bf16[256,32,128]{2,1,0:T(8,128)(2,1)S(1)}, bf16[256,64,128]{2,1,0:T(8,128)(2,1)S(1)}) custom-call(bf16[32,64,512]{2,1,0:T(8,128)(2,1)S(1)} %get-tuple-element.41.j_ref, bf16[32,64,512]{2,1,0:T(8,128)(2,1)S(1)} %collective-permute-done.i_ref, bf16[512,512]{1,0:T(8,128)(2,1)S(1)} %copy-done.3, bf16[32,256]{1,0:T(8,128)(2,1)S(1)} %copy-done.7, ...), custom_call_target="tpu_custom_call" | custom-call | flops 2147483648 | bytes 8388608 | tf_op jit(solution)/shard_map/spectra/pallas_call | solution.py:253
  17.8 4.8 %partial_correlations.5 = (bf16[3,16,16,128]{3,2,1,0:T(8,128)(2,1)S(1)}, bf16[3,16,16,128]{3,2,1,0:T(8,128)(2,1)S(1)}, f32[3,16,16,128]{3,2,1,0:T(8,128)S(1)}, bf16[3,16,16,128]{3,2,1,0:T(8,128)(2,1)S(1)}) custom-call(bf16[256,32,128]{2,1,0:T(8,128)(2,1)S(1)} %get-tuple-element.42.refs_0_, bf16[256,64,128]{2,1,0:T(8,128)(2,1)S(1)} %get-tuple-element.43.refs_1_.refs_2_, ...), custom_call_target="tpu_custom_call" | custom-call | flops 805306368 | bytes 6291456 | tf_op jit(solution)/shard_map/partial_correlations/pallas_call | solution.py:394
  22.6 3.0 %collective-permute-start.2 = (bf16[3,16,16,128]{3,2,1,0:T(8,128)(2,1)S(1)}, bf16[3,16,16,128]{3,2,1,0:T(8,128)(2,1)S(1)}, u32[]{:S(2)}, u32[]{:S(2)}) collective-permute-start(bf16[3,16,16,128]{3,2,1,0:T(8,128)(2,1)S(1)} %get-tuple-element.46), channel_id=1, source_target_pairs={{0,4},{4,0},{8,12},{12,8},{1,5},{5,1},{9,13},{13,9},{2,6},{6,2},{1... | collective-permute-start | bytes 589832 | tf_op jit(solution)/shard_map/ppermute | solution.py:467
  25.6 4.2 %collective-permute-done.1.j_ref = bf16[32,32,512]{2,1,0:T(8,128)(2,1)S(1)} collective-permute-done((bf16[32,32,512]{2,1,0:T(8,128)(2,1)S(1)}, bf16[32,32,512]{2,1,0:T(8,128)(2,1)S(1)}, u32[]{:S(2)}, u32[]{:S(2)}) %collective-permute-start.1) | collective-permute-done | bytes 1048608 | tf_op jit(solution)/shard_map/ppermute | solution.py:461
  30.8 1.7 %collective-permute-start.4 = (bf16[32,32,512]{2,1,0:T(8,128)(2,1)S(1)}, bf16[32,32,512]{2,1,0:T(8,128)(2,1)S(1)}, u32[]{:S(2)}, u32[]{:S(2)}) collective-permute-start(bf16[32,32,512]{2,1,0:T(8,128)(2,1)S(1)} %get-tuple-element.51), channel_id=1, source_target_pairs={{0,2},{2,0},{1,3},{3,1},{4,6},{6,4},{5,7},{7,5},{8,10},{10,8},{9,1... | collective-permute-start | bytes 3145736 | tf_op jit(solution)/shard_map/ppermute | solution.py:461
  32.5 1.6 %collective-permute-start.6 = (bf16[3,16,16,128]{3,2,1,0:T(8,128)(2,1)S(1)}, bf16[3,16,16,128]{3,2,1,0:T(8,128)(2,1)S(1)}, u32[]{:S(2)}, u32[]{:S(2)}) collective-permute-start(bf16[3,16,16,128]{3,2,1,0:T(8,128)(2,1)S(1)} %get-tuple-element.55), channel_id=1, source_target_pairs={{0,4},{4,0},{8,12},{12,8},{1,5},{5,1},{9,13},{13,9},{2,6},{6,2},{1... | collective-permute-start | bytes 589832 | tf_op jit(solution)/shard_map/ppermute | solution.py:467
  34.1 2.7 %collective-permute-start.5 = (bf16[3,16,16,128]{3,2,1,0:T(8,128)(2,1)S(1)}, bf16[3,16,16,128]{3,2,1,0:T(8,128)(2,1)S(1)}, u32[]{:S(2)}, u32[]{:S(2)}) collective-permute-start(bf16[3,16,16,128]{3,2,1,0:T(8,128)(2,1)S(1)} %add_convert_fusion.2), channel_id=1, source_target_pairs={{0,8},{4,12},{8,0},{12,4},{1,9},{5,13},{9,1},{13,5},{2,10},{6,14},... | collective-permute-start | bytes 589832 | tf_op jit(solution)/shard_map/ppermute | solution.py:467
  36.8 6.8 %spectra.4 = (bf16[256,16,128]{2,1,0:T(8,128)(2,1)S(1)}, bf16[256,64,128]{2,1,0:T(8,128)(2,1)S(1)}) custom-call(bf16[32,32,512]{2,1,0:T(8,128)(2,1)S(1)} %collective-permute-done.1.j_ref, bf16[32,32,512]{2,1,0:T(8,128)(2,1)S(1)} %collective-permute-done.3.i_ref, bf16[512,512]{1,0:T(8,128)(2,1)S(1)} %copy-done.3, bf16[32,256]{1,0:T(8,128)(2,1)S(1)} %copy-done.6, ...), custom_call_target="tpu_custom_call" | custom-call | flops 1073741824 | bytes 4194304 | tf_op jit(solution)/shard_map/spectra/pallas_call | solution.py:253
  43.5 8.3 %partial_correlations.6 = (bf16[5,16,16,128]{3,2,1,0:T(8,128)(2,1)S(1)}, bf16[5,16,16,128]{3,2,1,0:T(8,128)(2,1)S(1)}, f32[2,16,16,128]{3,2,1,0:T(8,128)S(1)}, bf16[2,16,16,128]{3,2,1,0:T(8,128)(2,1)S(1)}) custom-call(bf16[256,32,128]{2,1,0:T(8,128)(2,1)S(1)} %get-tuple-element.42.refs_0_, bf16[256,16,128]{2,1,0:T(8,128)(2,1)S(1)} %get-tuple-element.48.refs_1_, ...), custom_call_target="tpu_custom_call" | custom-call | flops 1610612736 | bytes 11534336 | tf_op jit(solution)/shard_map/partial_correlations/pallas_call | solution.py:394
  52.4 4.0 %collective-permute-done.4.j_ref = bf16[32,32,512]{2,1,0:T(8,128)(2,1)S(1)} collective-permute-done((bf16[32,32,512]{2,1,0:T(8,128)(2,1)S(1)}, bf16[32,32,512]{2,1,0:T(8,128)(2,1)S(1)}, u32[]{:S(2)}, u32[]{:S(2)}) %collective-permute-start.4) | collective-permute-done | bytes 1048608 | tf_op jit(solution)/shard_map/ppermute | solution.py:461
  56.4 4.8 %collective-permute-done.7 = bf16[5,16,16,128]{3,2,1,0:T(8,128)(2,1)S(1)} collective-permute-done((bf16[5,16,16,128]{3,2,1,0:T(8,128)(2,1)S(1)}, bf16[5,16,16,128]{3,2,1,0:T(8,128)(2,1)S(1)}, u32[]{:S(2)}, u32[]{:S(2)}) %collective-permute-start.7) | collective-permute-done | bytes 327712 | tf_op jit(solution)/shard_map/ppermute | solution.py:467
  63.8 6.7 %spectra.5 = (bf16[256,16,128]{2,1,0:T(8,128)(2,1)S(1)}, bf16[256,64,128]{2,1,0:T(8,128)(2,1)S(1)}) custom-call(bf16[32,32,512]{2,1,0:T(8,128)(2,1)S(1)} %collective-permute-done.4.j_ref, bf16[32,32,512]{2,1,0:T(8,128)(2,1)S(1)} %collective-permute-done.8.i_ref, bf16[512,512]{1,0:T(8,128)(2,1)S(1)} %copy-done.3, bf16[32,256]{1,0:T(8,128)(2,1)S(1)} %copy-done.6, ...), custom_call_target="tpu_custom_call" | custom-call | flops 1073741824 | bytes 4194304 | tf_op jit(solution)/shard_map/spectra/pallas_call | solution.py:253
  70.6 5.7 %partial_correlations.7 = (bf16[4,16,16,128]{3,2,1,0:T(8,128)(2,1)S(1)}, bf16[4,16,16,128]{3,2,1,0:T(8,128)(2,1)S(1)}, f32[1,16,16,128]{3,2,1,0:T(8,128)S(1)}, bf16[1,16,16,128]{3,2,1,0:T(8,128)(2,1)S(1)}) custom-call(bf16[256,32,128]{2,1,0:T(8,128)(2,1)S(1)} %get-tuple-element.42.refs_0_, bf16[256,16,128]{2,1,0:T(8,128)(2,1)S(1)} %get-tuple-element.48.refs_1_, ...), custom_call_target="tpu_custom_call" | custom-call | flops 1207959552 | bytes 7340032 | tf_op jit(solution)/shard_map/partial_correlations/pallas_call | solution.py:394
  76.9 2.4 %collective-permute-done.9.refs_10_ = bf16[5,16,16,128]{3,2,1,0:T(8,128)(2,1)S(1)} collective-permute-done((bf16[5,16,16,128]{3,2,1,0:T(8,128)(2,1)S(1)}, bf16[5,16,16,128]{3,2,1,0:T(8,128)(2,1)S(1)}, u32[]{:S(2)}, u32[]{:S(2)}) %collective-permute-start.9) | collective-permute-done | bytes 327712 | tf_op jit(solution)/shard_map/ppermute | solution.py:467
  79.3 4.0 %partial_correlations.8 = (f32[3,16,16,128]{3,2,1,0:T(8,128)S(1)}, bf16[3,16,16,128]{3,2,1,0:T(8,128)(2,1)S(1)}) custom-call(bf16[256,16,128]{2,1,0:T(8,128)(2,1)S(1)} %get-tuple-element.71.refs_0_, bf16[256,64,128]{2,1,0:T(8,128)(2,1)S(1)} %get-tuple-element.49.refs_3_.refs_1_, bf16[256,64,128]{2,1,0:T(8,128)(2,1)S(1)} %get-tuple-element.67.refs_2_, ...), custom_call_target="tpu_custom_call" | custom-call | flops 402653184 | bytes 9437184 | tf_op jit(solution)/shard_map/partial_correlations/pallas_call | solution.py:394
  83.4 1.5 %collective-permute-done.11 = bf16[4,16,16,128]{3,2,1,0:T(8,128)(2,1)S(1)} collective-permute-done((bf16[4,16,16,128]{3,2,1,0:T(8,128)(2,1)S(1)}, bf16[4,16,16,128]{3,2,1,0:T(8,128)(2,1)S(1)}, u32[]{:S(2)}, u32[]{:S(2)}) %collective-permute-start.11) | collective-permute-done | bytes 262176 | tf_op jit(solution)/shard_map/ppermute | solution.py:467
  85.6 4.0 %partial_correlations.9 = (f32[3,16,16,128]{3,2,1,0:T(8,128)S(1)}, bf16[3,16,16,128]{3,2,1,0:T(8,128)(2,1)S(1)}) custom-call(bf16[256,16,128]{2,1,0:T(8,128)(2,1)S(1)} %get-tuple-element.71.refs_0_, bf16[256,64,128]{2,1,0:T(8,128)(2,1)S(1)} %get-tuple-element.43.refs_1_.refs_2_, bf16[128,512]{1,0:T(8,128)(2,1)S(1)} %copy-done, bf16[256,256]{1,0:T(8,128)(2,1)S(1)} %copy-done.1), custom_call_target="tpu_custom_call" | custom-call | flops 402653184 | bytes 5242880 | tf_op jit(solution)/shard_map/partial_correlations/pallas_call | solution.py:394
  89.6 1.6 %collective-permute-start.13 = (bf16[3,16,16,128]{3,2,1,0:T(8,128)(2,1)S(1)}, bf16[3,16,16,128]{3,2,1,0:T(8,128)(2,1)S(1)}, u32[]{:S(2)}, u32[]{:S(2)}) collective-permute-start(bf16[3,16,16,128]{3,2,1,0:T(8,128)(2,1)S(1)} %get-tuple-element.75), channel_id=1, source_target_pairs={{0,4},{4,0},{8,12},{12,8},{1,5},{5,1},{9,13},{13,9},{2,6},{6,2},{1... | collective-permute-start | bytes 589832 | tf_op jit(solution)/shard_map/ppermute | solution.py:467
  91.2 4.1 %collective-permute-done.12.refs_7_ = bf16[4,16,16,128]{3,2,1,0:T(8,128)(2,1)S(1)} collective-permute-done((bf16[4,16,16,128]{3,2,1,0:T(8,128)(2,1)S(1)}, bf16[4,16,16,128]{3,2,1,0:T(8,128)(2,1)S(1)}, u32[]{:S(2)}, u32[]{:S(2)}) %collective-permute-start.12) | collective-permute-done | bytes 262176 | tf_op jit(solution)/shard_map/ppermute | solution.py:467
  95.3 6.2 %collective-permute-done.13.refs_8_ = bf16[3,16,16,128]{3,2,1,0:T(8,128)(2,1)S(1)} collective-permute-done((bf16[3,16,16,128]{3,2,1,0:T(8,128)(2,1)S(1)}, bf16[3,16,16,128]{3,2,1,0:T(8,128)(2,1)S(1)}, u32[]{:S(2)}, u32[]{:S(2)}) %collective-permute-start.13) | collective-permute-done | bytes 196640 | tf_op jit(solution)/shard_map/ppermute | solution.py:467
  101.5 1.2 %assembled.1 = f32[3,1,32,32,128]{4,3,2,1,0:T(8,128)} custom-call(f32[3,16,16,128]{3,2,1,0:T(8,128)S(1)} %get-tuple-element.44.refs_0_, f32[2,16,16,128]{3,2,1,0:T(8,128)S(1)} %get-tuple-element.50.refs_1_, f32[1,16,16,128]{3,2,1,0:T(8,128)S(1)} %get-tuple-element.62.refs_2_, f32[3,16,16,128]{3,2,1,0:T(8,128)S(1)} %get-tuple-element.68.refs_3_, ...), custom_call_target="tpu_custom_call" | custom-call | bytes 2359296 | tf_op jit(solution)/shard_map/assembled/pallas_call | solution.py:438
  (36 shorter events, 6.8 us)
Async XLA Ops:
  0.0 0.7 copy-start.2
  0.7 6.6 %copy-start.3 = (bf16[512,512]{1,0:T(8,128)(2,1)S(1)}, bf16[512,512]{1,0:T(8,128)(2,1)}, u32[]{:S(2)}) copy-start(bf16[512,512]{1,0:T(8,128)(2,1)} %constant.21.table_ref) | copy-start | bytes 1572868
  0.7 6.6 %copy-start.5 = (bf16[128,128]{1,0:T(8,128)(2,1)S(1)}, bf16[128,128]{1,0:T(8,128)(2,1)}, u32[]{:S(2)}) copy-start(bf16[128,128]{1,0:T(8,128)(2,1)} %constant.23.to_j_ref) | copy-start | bytes 98308
  0.7 6.6 %copy-start.7 = (bf16[32,256]{1,0:T(8,128)(2,1)S(1)}, bf16[32,256]{1,0:T(8,128)(2,1)}, u32[]{:S(2)}) copy-start(bf16[32,256]{1,0:T(8,128)(2,1)} %constant.22.to_i_ref) | copy-start | bytes 49156
  2.9 4.3 %collective-permute-start = (bf16[32,64,512]{2,1,0:T(8,128)(2,1)S(1)}, bf16[32,64,512]{2,1,0:T(8,128)(2,1)S(1)}, u32[]{:S(2)}, u32[]{:S(2)}) collective-permute-start(bf16[32,64,512]{2,1,0:T(8,128)(2,1)S(1)} %get-tuple-element.41.j_ref), channel_id=1, source_target_pairs={{0,1},{1,0},{2,3},{3,2},{4,5},{5,4},{6,7},{7,6},{8,9},{9,8},{10,11... | collective-permute-start | bytes 6291464 | tf_op jit(solution)/shard_map/ppermute | solution.py:464
  3.5 14.3 %copy-start = (bf16[128,512]{1,0:T(8,128)(2,1)S(1)}, bf16[128,512]{1,0:T(8,128)(2,1)}, u32[]{:S(2)}) copy-start(bf16[128,512]{1,0:T(8,128)(2,1)} %constant.24.refs_2_.refs_4_.refs_3_) | copy-start | bytes 393220
  3.5 14.3 %copy-start.1 = (bf16[256,256]{1,0:T(8,128)(2,1)S(1)}, bf16[256,256]{1,0:T(8,128)(2,1)}, u32[]{:S(2)}) copy-start(bf16[256,256]{1,0:T(8,128)(2,1)} %constant.25.refs_3_.refs_5_.refs_4_) | copy-start | bytes 393220
  3.5 26.3 %collective-permute-start.1 = (bf16[32,32,512]{2,1,0:T(8,128)(2,1)S(1)}, bf16[32,32,512]{2,1,0:T(8,128)(2,1)S(1)}, u32[]{:S(2)}, u32[]{:S(2)}) collective-permute-start(bf16[32,32,512]{2,1,0:T(8,128)(2,1)S(1)} %get-tuple-element.45), channel_id=1, source_target_pairs={{0,2},{2,0},{1,3},{3,1},{4,6},{6,4},{5,7},{7,5},{8,10},{10,8},{9,1... | collective-permute-start | bytes 3145736 | tf_op jit(solution)/shard_map/ppermute | solution.py:461
  17.7 19.0 %copy-start.4 = (bf16[128,256]{1,0:T(8,128)(2,1)S(1)}, bf16[128,256]{1,0:T(8,128)(2,1)}, u32[]{:S(2)}) copy-start(bf16[128,256]{1,0:T(8,128)(2,1)} %constant.27.to_j_ref) | copy-start | bytes 196612
  17.8 19.0 %copy-start.6 = (bf16[32,256]{1,0:T(8,128)(2,1)S(1)}, bf16[32,256]{1,0:T(8,128)(2,1)}, u32[]{:S(2)}) copy-start(bf16[32,256]{1,0:T(8,128)(2,1)} %constant.26.to_i_ref) | copy-start | bytes 49156
  22.6 8.2 %collective-permute-start.2 = (bf16[3,16,16,128]{3,2,1,0:T(8,128)(2,1)S(1)}, bf16[3,16,16,128]{3,2,1,0:T(8,128)(2,1)S(1)}, u32[]{:S(2)}, u32[]{:S(2)}) collective-permute-start(bf16[3,16,16,128]{3,2,1,0:T(8,128)(2,1)S(1)} %get-tuple-element.46), channel_id=1, source_target_pairs={{0,4},{4,0},{8,12},{12,8},{1,5},{5,1},{9,13},{13,9},{2,6},{6,2},{1... | collective-permute-start | bytes 589832 | tf_op jit(solution)/shard_map/ppermute | solution.py:467
  30.8 6.0 %collective-permute-start.3 = (bf16[32,32,512]{2,1,0:T(8,128)(2,1)S(1)}, bf16[32,32,512]{2,1,0:T(8,128)(2,1)S(1)}, u32[]{:S(2)}, u32[]{:S(2)}) collective-permute-start(bf16[32,32,512]{2,1,0:T(8,128)(2,1)S(1)} %collective-permute-done.1.j_ref), channel_id=1, source_target_pairs={{0,1},{1,0},{2,3},{3,2},{4,5},{5,4},{6,7},{7,6},{8,9},{9,8},{10,11... | collective-permute-start | bytes 3145736 | tf_op jit(solution)/shard_map/ppermute | solution.py:464
  30.8 25.6 %collective-permute-start.4 = (bf16[32,32,512]{2,1,0:T(8,128)(2,1)S(1)}, bf16[32,32,512]{2,1,0:T(8,128)(2,1)S(1)}, u32[]{:S(2)}, u32[]{:S(2)}) collective-permute-start(bf16[32,32,512]{2,1,0:T(8,128)(2,1)S(1)} %get-tuple-element.51), channel_id=1, source_target_pairs={{0,2},{2,0},{1,3},{3,1},{4,6},{6,4},{5,7},{7,5},{8,10},{10,8},{9,1... | collective-permute-start | bytes 3145736 | tf_op jit(solution)/shard_map/ppermute | solution.py:461
  32.5 19.4 %collective-permute-start.6 = (bf16[3,16,16,128]{3,2,1,0:T(8,128)(2,1)S(1)}, bf16[3,16,16,128]{3,2,1,0:T(8,128)(2,1)S(1)}, u32[]{:S(2)}, u32[]{:S(2)}) collective-permute-start(bf16[3,16,16,128]{3,2,1,0:T(8,128)(2,1)S(1)} %get-tuple-element.55), channel_id=1, source_target_pairs={{0,4},{4,0},{8,12},{12,8},{1,5},{5,1},{9,13},{13,9},{2,6},{6,2},{1... | collective-permute-start | bytes 589832 | tf_op jit(solution)/shard_map/ppermute | solution.py:467
  34.1 17.7 %collective-permute-start.5 = (bf16[3,16,16,128]{3,2,1,0:T(8,128)(2,1)S(1)}, bf16[3,16,16,128]{3,2,1,0:T(8,128)(2,1)S(1)}, u32[]{:S(2)}, u32[]{:S(2)}) collective-permute-start(bf16[3,16,16,128]{3,2,1,0:T(8,128)(2,1)S(1)} %add_convert_fusion.2), channel_id=1, source_target_pairs={{0,8},{4,12},{8,0},{12,4},{1,9},{5,13},{9,1},{13,5},{2,10},{6,14},... | collective-permute-start | bytes 589832 | tf_op jit(solution)/shard_map/ppermute | solution.py:467
  51.8 9.3 %collective-permute-start.7 = (bf16[5,16,16,128]{3,2,1,0:T(8,128)(2,1)S(1)}, bf16[5,16,16,128]{3,2,1,0:T(8,128)(2,1)S(1)}, u32[]{:S(2)}, u32[]{:S(2)}) collective-permute-start(bf16[5,16,16,128]{3,2,1,0:T(8,128)(2,1)S(1)} %get-tuple-element.56), channel_id=1, source_target_pairs={{0,4},{4,0},{8,12},{12,8},{1,5},{5,1},{9,13},{13,9},{2,6},{6,2},{1... | collective-permute-start | bytes 983048 | tf_op jit(solution)/shard_map/ppermute | solution.py:467
  61.2 2.7 %collective-permute-start.8 = (bf16[32,32,512]{2,1,0:T(8,128)(2,1)S(1)}, bf16[32,32,512]{2,1,0:T(8,128)(2,1)S(1)}, u32[]{:S(2)}, u32[]{:S(2)}) collective-permute-start(bf16[32,32,512]{2,1,0:T(8,128)(2,1)S(1)} %collective-permute-done.4.j_ref), channel_id=1, source_target_pairs={{0,1},{1,0},{2,3},{3,2},{4,5},{5,4},{6,7},{7,6},{8,9},{9,8},{10,11... | collective-permute-start | bytes 3145736 | tf_op jit(solution)/shard_map/ppermute | solution.py:464
  61.3 18.0 %collective-permute-start.9 = (bf16[5,16,16,128]{3,2,1,0:T(8,128)(2,1)S(1)}, bf16[5,16,16,128]{3,2,1,0:T(8,128)(2,1)S(1)}, u32[]{:S(2)}, u32[]{:S(2)}) collective-permute-start(bf16[5,16,16,128]{3,2,1,0:T(8,128)(2,1)S(1)} %add_convert_fusion), channel_id=1, source_target_pairs={{0,8},{4,12},{8,0},{12,4},{1,9},{5,13},{9,1},{13,5},{2,10},{6,14},... | collective-permute-start | bytes 983048 | tf_op jit(solution)/shard_map/ppermute | solution.py:467
  61.7 15.2 %collective-permute-start.10 = (bf16[2,16,16,128]{3,2,1,0:T(8,128)(2,1)S(1)}, bf16[2,16,16,128]{3,2,1,0:T(8,128)(2,1)S(1)}, u32[]{:S(2)}, u32[]{:S(2)}) collective-permute-start(bf16[2,16,16,128]{3,2,1,0:T(8,128)(2,1)S(1)} %get-tuple-element.66), channel_id=1, source_target_pairs={{0,4},{4,0},{8,12},{12,8},{1,5},{5,1},{9,13},{13,9},{2,6},{6,2},{1... | collective-permute-start | bytes 393224 | tf_op jit(solution)/shard_map/ppermute | solution.py:467
  76.3 8.6 %collective-permute-start.11 = (bf16[4,16,16,128]{3,2,1,0:T(8,128)(2,1)S(1)}, bf16[4,16,16,128]{3,2,1,0:T(8,128)(2,1)S(1)}, u32[]{:S(2)}, u32[]{:S(2)}) collective-permute-start(bf16[4,16,16,128]{3,2,1,0:T(8,128)(2,1)S(1)} %get-tuple-element.65), channel_id=1, source_target_pairs={{0,4},{4,0},{8,12},{12,8},{1,5},{5,1},{9,13},{13,9},{2,6},{6,2},{1... | collective-permute-start | bytes 786440 | tf_op jit(solution)/shard_map/ppermute | solution.py:467
  83.3 11.9 %collective-permute-start.12 = (bf16[4,16,16,128]{3,2,1,0:T(8,128)(2,1)S(1)}, bf16[4,16,16,128]{3,2,1,0:T(8,128)(2,1)S(1)}, u32[]{:S(2)}, u32[]{:S(2)}) collective-permute-start(bf16[4,16,16,128]{3,2,1,0:T(8,128)(2,1)S(1)} %pad_maximum_fusion), channel_id=1, source_target_pairs={{0,4},{4,0},{8,12},{12,8},{1,5},{5,1},{9,13},{13,9},{2,6},{6,2},{1... | collective-permute-start | bytes 786440 | tf_op jit(solution)/shard_map/ppermute | solution.py:467
  85.0 16.5 %collective-permute-start.14 = (bf16[4,16,16,128]{3,2,1,0:T(8,128)(2,1)S(1)}, bf16[4,16,16,128]{3,2,1,0:T(8,128)(2,1)S(1)}, u32[]{:S(2)}, u32[]{:S(2)}) collective-permute-start(bf16[4,16,16,128]{3,2,1,0:T(8,128)(2,1)S(1)} %add_convert_fusion.1), channel_id=1, source_target_pairs={{0,8},{4,12},{8,0},{12,4},{1,9},{5,13},{9,1},{13,5},{2,10},{6,14},... | collective-permute-start | bytes 786440 | tf_op jit(solution)/shard_map/ppermute | solution.py:467
  89.6 11.9 %collective-permute-start.13 = (bf16[3,16,16,128]{3,2,1,0:T(8,128)(2,1)S(1)}, bf16[3,16,16,128]{3,2,1,0:T(8,128)(2,1)S(1)}, u32[]{:S(2)}, u32[]{:S(2)}) collective-permute-start(bf16[3,16,16,128]{3,2,1,0:T(8,128)(2,1)S(1)} %get-tuple-element.75), channel_id=1, source_target_pairs={{0,4},{4,0},{8,12},{12,8},{1,5},{5,1},{9,13},{13,9},{2,6},{6,2},{1... | collective-permute-start | bytes 589832 | tf_op jit(solution)/shard_map/ppermute | solution.py:467

commit v2 on v1

--- a/solution.py
+++ b/solution.py
@@ -188,20 +188,23 @@
                 here = j_ref[win]
                 stacked += [here, jnp.where(same, here, i_ref[win])]
             wave = jnp.concatenate(stacked, axis=0)
-            return lax.dot_general(table_ref[...], wave, NT, preferred_element_type=jnp.float32)
+            return [
+                lax.dot_general(
+                    table_ref[part * bins : (part + 1) * bins], wave, NT, preferred_element_type=jnp.float32
+                )
+                for part in range(2)
+            ]
 
         def keep(group, spectrum):
-            energy = jnp.sum(spectrum * spectrum, axis=0, keepdims=True) / bins
-            white = spectrum * lax.rsqrt(energy + 1e-05)
+            energy = sum(jnp.sum(values * values, axis=0, keepdims=True) for values in spectrum) / bins
+            white = [values * lax.rsqrt(energy + 1e-05) for values in spectrum]
             for half in range(2):
                 for part in range(2):
                     if folded == 1:
                         row = half * wins + part * pairs + group
                     else:
                         row = part * pairs + 2 * group + half
-                    wide[pl.ds(row, bins, stride=pitch), :] = white[
-                        part * bins : (part + 1) * bins, half * LANES : (half + 1) * LANES
-                    ]
+                    wide[pl.ds(row, bins, stride=pitch), :] = white[part][:, half * LANES : (half + 1) * LANES]
 
         groups = wins // per_step
         at_once = 4

time: 103 us -> 103 us (level)
  no operation moved by 1% of the time
where the time goes in v2:
time: 103 us
  Pallas kernels  54.1 us (53%)
  waiting for transfers between devices  30.6 us (30%)
  starting transfers between devices  16.9 us (16%)
    pallas_call x5, Pallas kernels, partial_correlations(): kernel_call(kernel, 'partial_correlations', 4 * total * bins * depth * LA...  26.8 us
    pallas_call x3, Pallas kernels, spectra(): kernel_call(kernel, 'spectra', 4 * samples * samples * wins * given, 4 *...  23.7 us
    ppermute x10, waiting for transfers between devices, with_device(): lax.ppermute(share, 'chan', [(z, z ^ apart) for z in range(chan_count)])  20.1 us
    ppermute x10, starting transfers between devices, with_device(): lax.ppermute(share, 'chan', [(z, z ^ apart) for z in range(chan_count)])  12.1 us
    ppermute x2, waiting for transfers between devices, over_sub(): return lax.ppermute(rows, 'sub', [(0, 1), (1, 0)])  8.33 us
    ppermute x2, starting transfers between devices, over_sub(): return lax.ppermute(rows, 'sub', [(0, 1), (1, 0)])  4.24 us
    pallas_call x1, Pallas kernels, order_rows(): kernel_call(kernel, 'order_rows', 0, 3 * traces.size * 2, vmem_bytes=ORDE...  2.28 us
    ppermute x3, waiting for transfers between devices, over_core(): return lax.ppermute(rows, 'rep', [(0, 1), (1, 0)])  2.2 us
  transfers between devices with their start and end apart: 15, of which 10 were waited for; matrix products, arithmetic and copies ran while one was open for 0% of the time, Pallas kernels for 49%

profile of v2, /device:TPU:0, one launch (start us, length us, event | category | flops | bytes accessed | tf_op | source)
XLA Modules:
  0.0 102.8 jit_solution(7022780044742515706)
XLA Ops:
  0.7 2.3 %order_rows.1 = (bf16[32,64,512]{2,1,0:T(8,128)(2,1)S(1)}, bf16[32,32,512]{2,1,0:T(8,128)(2,1)S(1)}, bf16[32,32,512]{2,1,0:T(8,128)(2,1)S(1)}) custom-call(s32[64]{0:T(128)S(1)} %copy-done.2, bf16[64,32,512]{2,1,0:T(8,128)(2,1)} %traces_ref.1), custom_call_target="tpu_custom_call" | custom-call | bytes 6291456 | tf_op jit(solution)/shard_map/order_rows/pallas_call | solution.py:147
  3.5 2.6 %collective-permute-start.1 = (bf16[32,32,512]{2,1,0:T(8,128)(2,1)S(1)}, bf16[32,32,512]{2,1,0:T(8,128)(2,1)S(1)}, u32[]{:S(2)}, u32[]{:S(2)}) collective-permute-start(bf16[32,32,512]{2,1,0:T(8,128)(2,1)S(1)} %get-tuple-element.45), channel_id=1, source_target_pairs={{0,2},{2,0},{1,3},{3,1},{4,6},{6,4},{5,7},{7,5},{8,10},{10,8},{9,1... | collective-permute-start | bytes 3145736 | tf_op jit(solution)/shard_map/ppermute | solution.py:464
  6.1 1.2 %collective-permute-done.i_ref = bf16[32,64,512]{2,1,0:T(8,128)(2,1)S(1)} collective-permute-done((bf16[32,64,512]{2,1,0:T(8,128)(2,1)S(1)}, bf16[32,64,512]{2,1,0:T(8,128)(2,1)S(1)}, u32[]{:S(2)}, u32[]{:S(2)}) %collective-permute-start) | collective-permute-done | bytes 2097184 | tf_op jit(solution)/shard_map/ppermute | solution.py:467
  7.3 10.4 %spectra.3 = (bf16[256,32,128]{2,1,0:T(8,128)(2,1)S(1)}, bf16[256,64,128]{2,1,0:T(8,128)(2,1)S(1)}) custom-call(bf16[32,64,512]{2,1,0:T(8,128)(2,1)S(1)} %get-tuple-element.41.j_ref, bf16[32,64,512]{2,1,0:T(8,128)(2,1)S(1)} %collective-permute-done.i_ref, bf16[512,512]{1,0:T(8,128)(2,1)S(1)} %copy-done.3, bf16[32,256]{1,0:T(8,128)(2,1)S(1)} %copy-done.7, ...), custom_call_target="tpu_custom_call" | custom-call | flops 2147483648 | bytes 8388608 | tf_op jit(solution)/shard_map/spectra/pallas_call | solution.py:256
  17.7 4.8 %partial_correlations.5 = (bf16[3,16,16,128]{3,2,1,0:T(8,128)(2,1)S(1)}, bf16[3,16,16,128]{3,2,1,0:T(8,128)(2,1)S(1)}, f32[3,16,16,128]{3,2,1,0:T(8,128)S(1)}, bf16[3,16,16,128]{3,2,1,0:T(8,128)(2,1)S(1)}) custom-call(bf16[256,32,128]{2,1,0:T(8,128)(2,1)S(1)} %get-tuple-element.42.refs_0_, bf16[256,64,128]{2,1,0:T(8,128)(2,1)S(1)} %get-tuple-element.43.refs_1_.refs_2_, ...), custom_call_target="tpu_custom_call" | custom-call | flops 805306368 | bytes 6291456 | tf_op jit(solution)/shard_map/partial_correlations/pallas_call | solution.py:397
  22.5 3.0 %collective-permute-start.2 = (bf16[3,16,16,128]{3,2,1,0:T(8,128)(2,1)S(1)}, bf16[3,16,16,128]{3,2,1,0:T(8,128)(2,1)S(1)}, u32[]{:S(2)}, u32[]{:S(2)}) collective-permute-start(bf16[3,16,16,128]{3,2,1,0:T(8,128)(2,1)S(1)} %get-tuple-element.46), channel_id=1, source_target_pairs={{0,4},{4,0},{8,12},{12,8},{1,5},{5,1},{9,13},{13,9},{2,6},{6,2},{1... | collective-permute-start | bytes 589832 | tf_op jit(solution)/shard_map/ppermute | solution.py:470
  25.5 4.3 %collective-permute-done.1.j_ref = bf16[32,32,512]{2,1,0:T(8,128)(2,1)S(1)} collective-permute-done((bf16[32,32,512]{2,1,0:T(8,128)(2,1)S(1)}, bf16[32,32,512]{2,1,0:T(8,128)(2,1)S(1)}, u32[]{:S(2)}, u32[]{:S(2)}) %collective-permute-start.1) | collective-permute-done | bytes 1048608 | tf_op jit(solution)/shard_map/ppermute | solution.py:464
  30.7 1.7 %collective-permute-start.4 = (bf16[32,32,512]{2,1,0:T(8,128)(2,1)S(1)}, bf16[32,32,512]{2,1,0:T(8,128)(2,1)S(1)}, u32[]{:S(2)}, u32[]{:S(2)}) collective-permute-start(bf16[32,32,512]{2,1,0:T(8,128)(2,1)S(1)} %get-tuple-element.51), channel_id=1, source_target_pairs={{0,2},{2,0},{1,3},{3,1},{4,6},{6,4},{5,7},{7,5},{8,10},{10,8},{9,1... | collective-permute-start | bytes 3145736 | tf_op jit(solution)/shard_map/ppermute | solution.py:464
  32.4 1.6 %collective-permute-start.6 = (bf16[3,16,16,128]{3,2,1,0:T(8,128)(2,1)S(1)}, bf16[3,16,16,128]{3,2,1,0:T(8,128)(2,1)S(1)}, u32[]{:S(2)}, u32[]{:S(2)}) collective-permute-start(bf16[3,16,16,128]{3,2,1,0:T(8,128)(2,1)S(1)} %get-tuple-element.55), channel_id=1, source_target_pairs={{0,4},{4,0},{8,12},{12,8},{1,5},{5,1},{9,13},{13,9},{2,6},{6,2},{1... | collective-permute-start | bytes 589832 | tf_op jit(solution)/shard_map/ppermute | solution.py:470
  34.0 2.7 %collective-permute-start.5 = (bf16[3,16,16,128]{3,2,1,0:T(8,128)(2,1)S(1)}, bf16[3,16,16,128]{3,2,1,0:T(8,128)(2,1)S(1)}, u32[]{:S(2)}, u32[]{:S(2)}) collective-permute-start(bf16[3,16,16,128]{3,2,1,0:T(8,128)(2,1)S(1)} %add_convert_fusion.2), channel_id=1, source_target_pairs={{0,8},{4,12},{8,0},{12,4},{1,9},{5,13},{9,1},{13,5},{2,10},{6,14},... | collective-permute-start | bytes 589832 | tf_op jit(solution)/shard_map/ppermute | solution.py:470
  36.7 6.7 %spectra.4 = (bf16[256,16,128]{2,1,0:T(8,128)(2,1)S(1)}, bf16[256,64,128]{2,1,0:T(8,128)(2,1)S(1)}) custom-call(bf16[32,32,512]{2,1,0:T(8,128)(2,1)S(1)} %collective-permute-done.1.j_ref, bf16[32,32,512]{2,1,0:T(8,128)(2,1)S(1)} %collective-permute-done.3.i_ref, bf16[512,512]{1,0:T(8,128)(2,1)S(1)} %copy-done.3, bf16[32,256]{1,0:T(8,128)(2,1)S(1)} %copy-done.6, ...), custom_call_target="tpu_custom_call" | custom-call | flops 1073741824 | bytes 4194304 | tf_op jit(solution)/shard_map/spectra/pallas_call | solution.py:256
  43.4 8.3 %partial_correlations.6 = (bf16[5,16,16,128]{3,2,1,0:T(8,128)(2,1)S(1)}, bf16[5,16,16,128]{3,2,1,0:T(8,128)(2,1)S(1)}, f32[2,16,16,128]{3,2,1,0:T(8,128)S(1)}, bf16[2,16,16,128]{3,2,1,0:T(8,128)(2,1)S(1)}) custom-call(bf16[256,32,128]{2,1,0:T(8,128)(2,1)S(1)} %get-tuple-element.42.refs_0_, bf16[256,16,128]{2,1,0:T(8,128)(2,1)S(1)} %get-tuple-element.48.refs_1_, ...), custom_call_target="tpu_custom_call" | custom-call | flops 1610612736 | bytes 11534336 | tf_op jit(solution)/shard_map/partial_correlations/pallas_call | solution.py:397
  52.2 4.1 %collective-permute-done.4.j_ref = bf16[32,32,512]{2,1,0:T(8,128)(2,1)S(1)} collective-permute-done((bf16[32,32,512]{2,1,0:T(8,128)(2,1)S(1)}, bf16[32,32,512]{2,1,0:T(8,128)(2,1)S(1)}, u32[]{:S(2)}, u32[]{:S(2)}) %collective-permute-start.4) | collective-permute-done | bytes 1048608 | tf_op jit(solution)/shard_map/ppermute | solution.py:464
  56.3 4.7 %collective-permute-done.7 = bf16[5,16,16,128]{3,2,1,0:T(8,128)(2,1)S(1)} collective-permute-done((bf16[5,16,16,128]{3,2,1,0:T(8,128)(2,1)S(1)}, bf16[5,16,16,128]{3,2,1,0:T(8,128)(2,1)S(1)}, u32[]{:S(2)}, u32[]{:S(2)}) %collective-permute-start.7) | collective-permute-done | bytes 327712 | tf_op jit(solution)/shard_map/ppermute | solution.py:470
  63.7 6.7 %spectra.5 = (bf16[256,16,128]{2,1,0:T(8,128)(2,1)S(1)}, bf16[256,64,128]{2,1,0:T(8,128)(2,1)S(1)}) custom-call(bf16[32,32,512]{2,1,0:T(8,128)(2,1)S(1)} %collective-permute-done.4.j_ref, bf16[32,32,512]{2,1,0:T(8,128)(2,1)S(1)} %collective-permute-done.8.i_ref, bf16[512,512]{1,0:T(8,128)(2,1)S(1)} %copy-done.3, bf16[32,256]{1,0:T(8,128)(2,1)S(1)} %copy-done.6, ...), custom_call_target="tpu_custom_call" | custom-call | flops 1073741824 | bytes 4194304 | tf_op jit(solution)/shard_map/spectra/pallas_call | solution.py:256
  70.4 5.7 %partial_correlations.7 = (bf16[4,16,16,128]{3,2,1,0:T(8,128)(2,1)S(1)}, bf16[4,16,16,128]{3,2,1,0:T(8,128)(2,1)S(1)}, f32[1,16,16,128]{3,2,1,0:T(8,128)S(1)}, bf16[1,16,16,128]{3,2,1,0:T(8,128)(2,1)S(1)}) custom-call(bf16[256,32,128]{2,1,0:T(8,128)(2,1)S(1)} %get-tuple-element.42.refs_0_, bf16[256,16,128]{2,1,0:T(8,128)(2,1)S(1)} %get-tuple-element.48.refs_1_, ...), custom_call_target="tpu_custom_call" | custom-call | flops 1207959552 | bytes 7340032 | tf_op jit(solution)/shard_map/partial_correlations/pallas_call | solution.py:397
  76.7 2.5 %collective-permute-done.9.refs_10_ = bf16[5,16,16,128]{3,2,1,0:T(8,128)(2,1)S(1)} collective-permute-done((bf16[5,16,16,128]{3,2,1,0:T(8,128)(2,1)S(1)}, bf16[5,16,16,128]{3,2,1,0:T(8,128)(2,1)S(1)}, u32[]{:S(2)}, u32[]{:S(2)}) %collective-permute-start.9) | collective-permute-done | bytes 327712 | tf_op jit(solution)/shard_map/ppermute | solution.py:470
  79.2 4.0 %partial_correlations.8 = (f32[3,16,16,128]{3,2,1,0:T(8,128)S(1)}, bf16[3,16,16,128]{3,2,1,0:T(8,128)(2,1)S(1)}) custom-call(bf16[256,16,128]{2,1,0:T(8,128)(2,1)S(1)} %get-tuple-element.71.refs_0_, bf16[256,64,128]{2,1,0:T(8,128)(2,1)S(1)} %get-tuple-element.49.refs_3_.refs_1_, bf16[256,64,128]{2,1,0:T(8,128)(2,1)S(1)} %get-tuple-element.67.refs_2_, ...), custom_call_target="tpu_custom_call" | custom-call | flops 402653184 | bytes 9437184 | tf_op jit(solution)/shard_map/partial_correlations/pallas_call | solution.py:397
  83.3 1.5 %collective-permute-done.11 = bf16[4,16,16,128]{3,2,1,0:T(8,128)(2,1)S(1)} collective-permute-done((bf16[4,16,16,128]{3,2,1,0:T(8,128)(2,1)S(1)}, bf16[4,16,16,128]{3,2,1,0:T(8,128)(2,1)S(1)}, u32[]{:S(2)}, u32[]{:S(2)}) %collective-permute-start.11) | collective-permute-done | bytes 262176 | tf_op jit(solution)/shard_map/ppermute | solution.py:470
  85.4 4.0 %partial_correlations.9 = (f32[3,16,16,128]{3,2,1,0:T(8,128)S(1)}, bf16[3,16,16,128]{3,2,1,0:T(8,128)(2,1)S(1)}) custom-call(bf16[256,16,128]{2,1,0:T(8,128)(2,1)S(1)} %get-tuple-element.71.refs_0_, bf16[256,64,128]{2,1,0:T(8,128)(2,1)S(1)} %get-tuple-element.43.refs_1_.refs_2_, bf16[128,512]{1,0:T(8,128)(2,1)S(1)} %copy-done, bf16[256,256]{1,0:T(8,128)(2,1)S(1)} %copy-done.1), custom_call_target="tpu_custom_call" | custom-call | flops 402653184 | bytes 5242880 | tf_op jit(solution)/shard_map/partial_correlations/pallas_call | solution.py:397
  89.4 1.6 %collective-permute-start.13 = (bf16[3,16,16,128]{3,2,1,0:T(8,128)(2,1)S(1)}, bf16[3,16,16,128]{3,2,1,0:T(8,128)(2,1)S(1)}, u32[]{:S(2)}, u32[]{:S(2)}) collective-permute-start(bf16[3,16,16,128]{3,2,1,0:T(8,128)(2,1)S(1)} %get-tuple-element.75), channel_id=1, source_target_pairs={{0,4},{4,0},{8,12},{12,8},{1,5},{5,1},{9,13},{13,9},{2,6},{6,2},{1... | collective-permute-start | bytes 589832 | tf_op jit(solution)/shard_map/ppermute | solution.py:470
  91.0 4.1 %collective-permute-done.12.refs_7_ = bf16[4,16,16,128]{3,2,1,0:T(8,128)(2,1)S(1)} collective-permute-done((bf16[4,16,16,128]{3,2,1,0:T(8,128)(2,1)S(1)}, bf16[4,16,16,128]{3,2,1,0:T(8,128)(2,1)S(1)}, u32[]{:S(2)}, u32[]{:S(2)}) %collective-permute-start.12) | collective-permute-done | bytes 262176 | tf_op jit(solution)/shard_map/ppermute | solution.py:470
  95.1 6.3 %collective-permute-done.13.refs_8_ = bf16[3,16,16,128]{3,2,1,0:T(8,128)(2,1)S(1)} collective-permute-done((bf16[3,16,16,128]{3,2,1,0:T(8,128)(2,1)S(1)}, bf16[3,16,16,128]{3,2,1,0:T(8,128)(2,1)S(1)}, u32[]{:S(2)}, u32[]{:S(2)}) %collective-permute-start.13) | collective-permute-done | bytes 196640 | tf_op jit(solution)/shard_map/ppermute | solution.py:470
  101.4 1.2 %assembled.1 = f32[3,1,32,32,128]{4,3,2,1,0:T(8,128)} custom-call(f32[3,16,16,128]{3,2,1,0:T(8,128)S(1)} %get-tuple-element.44.refs_0_, f32[2,16,16,128]{3,2,1,0:T(8,128)S(1)} %get-tuple-element.50.refs_1_, f32[1,16,16,128]{3,2,1,0:T(8,128)S(1)} %get-tuple-element.62.refs_2_, f32[3,16,16,128]{3,2,1,0:T(8,128)S(1)} %get-tuple-element.68.refs_3_, ...), custom_call_target="tpu_custom_call" | custom-call | bytes 2359296 | tf_op jit(solution)/shard_map/assembled/pallas_call | solution.py:441
  (36 shorter events, 6.6 us)
Async XLA Ops:
  0.0 0.7 copy-start.2
  0.7 6.6 %copy-start.3 = (bf16[512,512]{1,0:T(8,128)(2,1)S(1)}, bf16[512,512]{1,0:T(8,128)(2,1)}, u32[]{:S(2)}) copy-start(bf16[512,512]{1,0:T(8,128)(2,1)} %constant.21.table_ref) | copy-start | bytes 1572868
  0.7 6.6 %copy-start.5 = (bf16[128,128]{1,0:T(8,128)(2,1)S(1)}, bf16[128,128]{1,0:T(8,128)(2,1)}, u32[]{:S(2)}) copy-start(bf16[128,128]{1,0:T(8,128)(2,1)} %constant.23.to_j_ref) | copy-start | bytes 98308
  0.7 6.6 %copy-start.7 = (bf16[32,256]{1,0:T(8,128)(2,1)S(1)}, bf16[32,256]{1,0:T(8,128)(2,1)}, u32[]{:S(2)}) copy-start(bf16[32,256]{1,0:T(8,128)(2,1)} %constant.22.to_i_ref) | copy-start | bytes 49156
  2.9 4.3 %collective-permute-start = (bf16[32,64,512]{2,1,0:T(8,128)(2,1)S(1)}, bf16[32,64,512]{2,1,0:T(8,128)(2,1)S(1)}, u32[]{:S(2)}, u32[]{:S(2)}) collective-permute-start(bf16[32,64,512]{2,1,0:T(8,128)(2,1)S(1)} %get-tuple-element.41.j_ref), channel_id=1, source_target_pairs={{0,1},{1,0},{2,3},{3,2},{4,5},{5,4},{6,7},{7,6},{8,9},{9,8},{10,11... | collective-permute-start | bytes 6291464 | tf_op jit(solution)/shard_map/ppermute | solution.py:467
  3.5 14.2 %copy-start = (bf16[128,512]{1,0:T(8,128)(2,1)S(1)}, bf16[128,512]{1,0:T(8,128)(2,1)}, u32[]{:S(2)}) copy-start(bf16[128,512]{1,0:T(8,128)(2,1)} %constant.24.refs_2_.refs_4_.refs_3_) | copy-start | bytes 393220
  3.5 14.2 %copy-start.1 = (bf16[256,256]{1,0:T(8,128)(2,1)S(1)}, bf16[256,256]{1,0:T(8,128)(2,1)}, u32[]{:S(2)}) copy-start(bf16[256,256]{1,0:T(8,128)(2,1)} %constant.25.refs_3_.refs_5_.refs_4_) | copy-start | bytes 393220
  3.5 26.3 %collective-permute-start.1 = (bf16[32,32,512]{2,1,0:T(8,128)(2,1)S(1)}, bf16[32,32,512]{2,1,0:T(8,128)(2,1)S(1)}, u32[]{:S(2)}, u32[]{:S(2)}) collective-permute-start(bf16[32,32,512]{2,1,0:T(8,128)(2,1)S(1)} %get-tuple-element.45), channel_id=1, source_target_pairs={{0,2},{2,0},{1,3},{3,1},{4,6},{6,4},{5,7},{7,5},{8,10},{10,8},{9,1... | collective-permute-start | bytes 3145736 | tf_op jit(solution)/shard_map/ppermute | solution.py:464
  17.7 19.0 %copy-start.4 = (bf16[128,256]{1,0:T(8,128)(2,1)S(1)}, bf16[128,256]{1,0:T(8,128)(2,1)}, u32[]{:S(2)}) copy-start(bf16[128,256]{1,0:T(8,128)(2,1)} %constant.27.to_j_ref) | copy-start | bytes 196612
  17.7 19.0 %copy-start.6 = (bf16[32,256]{1,0:T(8,128)(2,1)S(1)}, bf16[32,256]{1,0:T(8,128)(2,1)}, u32[]{:S(2)}) copy-start(bf16[32,256]{1,0:T(8,128)(2,1)} %constant.26.to_i_ref) | copy-start | bytes 49156
  22.5 8.2 %collective-permute-start.2 = (bf16[3,16,16,128]{3,2,1,0:T(8,128)(2,1)S(1)}, bf16[3,16,16,128]{3,2,1,0:T(8,128)(2,1)S(1)}, u32[]{:S(2)}, u32[]{:S(2)}) collective-permute-start(bf16[3,16,16,128]{3,2,1,0:T(8,128)(2,1)S(1)} %get-tuple-element.46), channel_id=1, source_target_pairs={{0,4},{4,0},{8,12},{12,8},{1,5},{5,1},{9,13},{13,9},{2,6},{6,2},{1... | collective-permute-start | bytes 589832 | tf_op jit(solution)/shard_map/ppermute | solution.py:470
  30.7 6.0 %collective-permute-start.3 = (bf16[32,32,512]{2,1,0:T(8,128)(2,1)S(1)}, bf16[32,32,512]{2,1,0:T(8,128)(2,1)S(1)}, u32[]{:S(2)}, u32[]{:S(2)}) collective-permute-start(bf16[32,32,512]{2,1,0:T(8,128)(2,1)S(1)} %collective-permute-done.1.j_ref), channel_id=1, source_target_pairs={{0,1},{1,0},{2,3},{3,2},{4,5},{5,4},{6,7},{7,6},{8,9},{9,8},{10,11... | collective-permute-start | bytes 3145736 | tf_op jit(solution)/shard_map/ppermute | solution.py:467
  30.7 25.6 %collective-permute-start.4 = (bf16[32,32,512]{2,1,0:T(8,128)(2,1)S(1)}, bf16[32,32,512]{2,1,0:T(8,128)(2,1)S(1)}, u32[]{:S(2)}, u32[]{:S(2)}) collective-permute-start(bf16[32,32,512]{2,1,0:T(8,128)(2,1)S(1)} %get-tuple-element.51), channel_id=1, source_target_pairs={{0,2},{2,0},{1,3},{3,1},{4,6},{6,4},{5,7},{7,5},{8,10},{10,8},{9,1... | collective-permute-start | bytes 3145736 | tf_op jit(solution)/shard_map/ppermute | solution.py:464
  32.4 19.3 %collective-permute-start.6 = (bf16[3,16,16,128]{3,2,1,0:T(8,128)(2,1)S(1)}, bf16[3,16,16,128]{3,2,1,0:T(8,128)(2,1)S(1)}, u32[]{:S(2)}, u32[]{:S(2)}) collective-permute-start(bf16[3,16,16,128]{3,2,1,0:T(8,128)(2,1)S(1)} %get-tuple-element.55), channel_id=1, source_target_pairs={{0,4},{4,0},{8,12},{12,8},{1,5},{5,1},{9,13},{13,9},{2,6},{6,2},{1... | collective-permute-start | bytes 589832 | tf_op jit(solution)/shard_map/ppermute | solution.py:470
  34.0 17.7 %collective-permute-start.5 = (bf16[3,16,16,128]{3,2,1,0:T(8,128)(2,1)S(1)}, bf16[3,16,16,128]{3,2,1,0:T(8,128)(2,1)S(1)}, u32[]{:S(2)}, u32[]{:S(2)}) collective-permute-start(bf16[3,16,16,128]{3,2,1,0:T(8,128)(2,1)S(1)} %add_convert_fusion.2), channel_id=1, source_target_pairs={{0,8},{4,12},{8,0},{12,4},{1,9},{5,13},{9,1},{13,5},{2,10},{6,14},... | collective-permute-start | bytes 589832 | tf_op jit(solution)/shard_map/ppermute | solution.py:470
  51.7 9.3 %collective-permute-start.7 = (bf16[5,16,16,128]{3,2,1,0:T(8,128)(2,1)S(1)}, bf16[5,16,16,128]{3,2,1,0:T(8,128)(2,1)S(1)}, u32[]{:S(2)}, u32[]{:S(2)}) collective-permute-start(bf16[5,16,16,128]{3,2,1,0:T(8,128)(2,1)S(1)} %get-tuple-element.56), channel_id=1, source_target_pairs={{0,4},{4,0},{8,12},{12,8},{1,5},{5,1},{9,13},{13,9},{2,6},{6,2},{1... | collective-permute-start | bytes 983048 | tf_op jit(solution)/shard_map/ppermute | solution.py:470
  61.0 2.7 %collective-permute-start.8 = (bf16[32,32,512]{2,1,0:T(8,128)(2,1)S(1)}, bf16[32,32,512]{2,1,0:T(8,128)(2,1)S(1)}, u32[]{:S(2)}, u32[]{:S(2)}) collective-permute-start(bf16[32,32,512]{2,1,0:T(8,128)(2,1)S(1)} %collective-permute-done.4.j_ref), channel_id=1, source_target_pairs={{0,1},{1,0},{2,3},{3,2},{4,5},{5,4},{6,7},{7,6},{8,9},{9,8},{10,11... | collective-permute-start | bytes 3145736 | tf_op jit(solution)/shard_map/ppermute | solution.py:467
  61.1 18.0 %collective-permute-start.9 = (bf16[5,16,16,128]{3,2,1,0:T(8,128)(2,1)S(1)}, bf16[5,16,16,128]{3,2,1,0:T(8,128)(2,1)S(1)}, u32[]{:S(2)}, u32[]{:S(2)}) collective-permute-start(bf16[5,16,16,128]{3,2,1,0:T(8,128)(2,1)S(1)} %add_convert_fusion), channel_id=1, source_target_pairs={{0,8},{4,12},{8,0},{12,4},{1,9},{5,13},{9,1},{13,5},{2,10},{6,14},... | collective-permute-start | bytes 983048 | tf_op jit(solution)/shard_map/ppermute | solution.py:470
  61.5 15.1 %collective-permute-start.10 = (bf16[2,16,16,128]{3,2,1,0:T(8,128)(2,1)S(1)}, bf16[2,16,16,128]{3,2,1,0:T(8,128)(2,1)S(1)}, u32[]{:S(2)}, u32[]{:S(2)}) collective-permute-start(bf16[2,16,16,128]{3,2,1,0:T(8,128)(2,1)S(1)} %get-tuple-element.66), channel_id=1, source_target_pairs={{0,4},{4,0},{8,12},{12,8},{1,5},{5,1},{9,13},{13,9},{2,6},{6,2},{1... | collective-permute-start | bytes 393224 | tf_op jit(solution)/shard_map/ppermute | solution.py:470
  76.1 8.7 %collective-permute-start.11 = (bf16[4,16,16,128]{3,2,1,0:T(8,128)(2,1)S(1)}, bf16[4,16,16,128]{3,2,1,0:T(8,128)(2,1)S(1)}, u32[]{:S(2)}, u32[]{:S(2)}) collective-permute-start(bf16[4,16,16,128]{3,2,1,0:T(8,128)(2,1)S(1)} %get-tuple-element.65), channel_id=1, source_target_pairs={{0,4},{4,0},{8,12},{12,8},{1,5},{5,1},{9,13},{13,9},{2,6},{6,2},{1... | collective-permute-start | bytes 786440 | tf_op jit(solution)/shard_map/ppermute | solution.py:470
  83.2 11.9 %collective-permute-start.12 = (bf16[4,16,16,128]{3,2,1,0:T(8,128)(2,1)S(1)}, bf16[4,16,16,128]{3,2,1,0:T(8,128)(2,1)S(1)}, u32[]{:S(2)}, u32[]{:S(2)}) collective-permute-start(bf16[4,16,16,128]{3,2,1,0:T(8,128)(2,1)S(1)} %pad_maximum_fusion), channel_id=1, source_target_pairs={{0,4},{4,0},{8,12},{12,8},{1,5},{5,1},{9,13},{13,9},{2,6},{6,2},{1... | collective-permute-start | bytes 786440 | tf_op jit(solution)/shard_map/ppermute | solution.py:470
  84.8 16.5 %collective-permute-start.14 = (bf16[4,16,16,128]{3,2,1,0:T(8,128)(2,1)S(1)}, bf16[4,16,16,128]{3,2,1,0:T(8,128)(2,1)S(1)}, u32[]{:S(2)}, u32[]{:S(2)}) collective-permute-start(bf16[4,16,16,128]{3,2,1,0:T(8,128)(2,1)S(1)} %add_convert_fusion.1), channel_id=1, source_target_pairs={{0,8},{4,12},{8,0},{12,4},{1,9},{5,13},{9,1},{13,5},{2,10},{6,14},... | collective-permute-start | bytes 786440 | tf_op jit(solution)/shard_map/ppermute | solution.py:470
  89.4 12.0 %collective-permute-start.13 = (bf16[3,16,16,128]{3,2,1,0:T(8,128)(2,1)S(1)}, bf16[3,16,16,128]{3,2,1,0:T(8,128)(2,1)S(1)}, u32[]{:S(2)}, u32[]{:S(2)}) collective-permute-start(bf16[3,16,16,128]{3,2,1,0:T(8,128)(2,1)S(1)} %get-tuple-element.75), channel_id=1, source_target_pairs={{0,4},{4,0},{8,12},{12,8},{1,5},{5,1},{9,13},{13,9},{2,6},{6,2},{1... | collective-permute-start | bytes 589832 | tf_op jit(solution)/shard_map/ppermute | solution.py:470

commit v3 on v2

--- a/solution.py
+++ b/solution.py
@@ -36,18 +36,23 @@
     return pl.BlockSpec(memory_space=pltpu.VMEM)
 
 
+def bin_order(bins):
+    return np.concatenate([np.arange(0, bins, 2), np.arange(1, bins, 2)])
+
+
 def dft_rows_table(samples):
     bins = samples // 2
-    turns = (np.arange(bins)[:, None] * np.arange(samples)[None, :]) % samples
+    turns = (bin_order(bins)[:, None] * np.arange(samples // 2)[None, :]) % samples
     angles = turns.astype(np.float32) * np.float32(2.0 * math.pi / samples)
-    table = np.concatenate([np.cos(angles), -np.sin(angles)], axis=0)
+    halves = np.split(angles, 2)
+    table = np.concatenate([part for half in halves for part in (np.cos(half), -np.sin(half))], axis=0)
     return jnp.asarray(table.astype(np.float32)).astype(jnp.bfloat16)
 
 
 def lag_rows_table(samples, scale):
     bins = samples // 2
     offsets = np.arange(LAGS) - LAGS // 2
-    turns = (offsets[:, None] * np.arange(bins)[None, :]) % samples
+    turns = (offsets[:, None] * bin_order(bins)[None, :]) % samples
     angles = turns.astype(np.float32) * np.float32(2.0 * math.pi / samples)
     table = np.concatenate([np.cos(angles), -np.sin(angles)], axis=1) * np.float32(scale)
     return jnp.asarray(table.astype(np.float32)).astype(jnp.bfloat16)
@@ -177,6 +182,7 @@
     line = depth // folded
     pitch = line + 1
     per_step = 2 * folded
+    half_bins = bins // 2
     batch = 8
 
     def kernel(j_ref, i_ref, table_ref, to_i_ref, to_j_ref, i_out, j_out, wide):
@@ -188,11 +194,13 @@
                 here = j_ref[win]
                 stacked += [here, jnp.where(same, here, i_ref[win])]
             wave = jnp.concatenate(stacked, axis=0)
+            first, second = wave[:, :bins].astype(jnp.float32), wave[:, bins:].astype(jnp.float32)
+            folds = [(first + second).astype(jnp.bfloat16), (first - second).astype(jnp.bfloat16)]
             return [
                 lax.dot_general(
-                    table_ref[part * bins : (part + 1) * bins], wave, NT, preferred_element_type=jnp.float32
+                    table_ref[odd * bins : (odd + 1) * bins], fold, NT, preferred_element_type=jnp.float32
                 )
-                for part in range(2)
+                for odd, fold in enumerate(folds)
             ]
 
         def keep(group, spectrum):
@@ -204,7 +212,10 @@
                         row = half * wins + part * pairs + group
                     else:
                         row = part * pairs + 2 * group + half
-                    wide[pl.ds(row, bins, stride=pitch), :] = white[part][:, half * LANES : (half + 1) * LANES]
+                    for odd in range(2):
+                        wide[pl.ds(odd * half_bins * pitch + row, half_bins, stride=pitch), :] = white[odd][
+                            part * half_bins : (part + 1) * half_bins, half * LANES : (half + 1) * LANES
+                        ]
 
         groups = wins // per_step
         at_once = 4

time: 103 us -> 102 us (level)
  Pallas kernels: 54.1 us -> 52.4 us
    pallas_call x3, Pallas kernels: 23.7 us -> 22.1 us  [spectra(): kernel_call(kernel, 'spectra', 4 * samples * samples * wins * given, 4 *...]
    ppermute x2, waiting for transfers between devices: 8.33 us -> 9.55 us  [over_sub(): return lax.ppermute(rows, 'sub', [(0, 1), (1, 0)])]
  transfers between devices with their start and end apart: 15 -> 15, of which waited for: 10 -> 10; matrix products, arithmetic and copies ran while one was open for 0% -> 0% of each run, Pallas kernels for 49% -> 48%
where the time goes in v3:
time: 102 us
  Pallas kernels  52.4 us (51%)
  waiting for transfers between devices  31.4 us (31%)
  starting transfers between devices  16.4 us (16%)
    pallas_call x5, Pallas kernels, partial_correlations(): kernel_call(kernel, 'partial_correlations', 4 * total * bins * depth * LA...  26.8 us
    pallas_call x3, Pallas kernels, spectra(): kernel_call(kernel, 'spectra', 4 * samples * samples * wins * given, 4 *...  22.1 us
    ppermute x10, waiting for transfers between devices, with_device(): lax.ppermute(share, 'chan', [(z, z ^ apart) for z in range(chan_count)])  19.7 us
    ppermute x10, starting transfers between devices, with_device(): lax.ppermute(share, 'chan', [(z, z ^ apart) for z in range(chan_count)])  11.6 us
    ppermute x2, waiting for transfers between devices, over_sub(): return lax.ppermute(rows, 'sub', [(0, 1), (1, 0)])  9.55 us
    ppermute x2, starting transfers between devices, over_sub(): return lax.ppermute(rows, 'sub', [(0, 1), (1, 0)])  4.24 us
    pallas_call x1, Pallas kernels, order_rows(): kernel_call(kernel, 'order_rows', 0, 3 * traces.size * 2, vmem_bytes=ORDE...  2.26 us
    ppermute x3, waiting for transfers between devices, over_core(): return lax.ppermute(rows, 'rep', [(0, 1), (1, 0)])  2.21 us
  transfers between devices with their start and end apart: 15, of which 10 were waited for; matrix products, arithmetic and copies ran while one was open for 0% of the time, Pallas kernels for 48%

profile of v3, /device:TPU:0, one launch (start us, length us, event | category | flops | bytes accessed | tf_op | source)
XLA Modules:
  0.0 101.5 jit_solution(16534822127995969859)
XLA Ops:
  0.7 2.3 %order_rows.1 = (bf16[32,64,512]{2,1,0:T(8,128)(2,1)S(1)}, bf16[32,32,512]{2,1,0:T(8,128)(2,1)S(1)}, bf16[32,32,512]{2,1,0:T(8,128)(2,1)S(1)}) custom-call(s32[64]{0:T(128)S(1)} %copy-done.2, bf16[64,32,512]{2,1,0:T(8,128)(2,1)} %traces_ref.1), custom_call_target="tpu_custom_call" | custom-call | bytes 6291456 | tf_op jit(solution)/shard_map/order_rows/pallas_call | solution.py:152
  3.5 2.6 %collective-permute-start.1 = (bf16[32,32,512]{2,1,0:T(8,128)(2,1)S(1)}, bf16[32,32,512]{2,1,0:T(8,128)(2,1)S(1)}, u32[]{:S(2)}, u32[]{:S(2)}) collective-permute-start(bf16[32,32,512]{2,1,0:T(8,128)(2,1)S(1)} %get-tuple-element.45), channel_id=1, source_target_pairs={{0,2},{2,0},{1,3},{3,1},{4,6},{6,4},{5,7},{7,5},{8,10},{10,8},{9,1... | collective-permute-start | bytes 3145736 | tf_op jit(solution)/shard_map/ppermute | solution.py:475
  6.0 1.2 %collective-permute-done.i_ref = bf16[32,64,512]{2,1,0:T(8,128)(2,1)S(1)} collective-permute-done((bf16[32,64,512]{2,1,0:T(8,128)(2,1)S(1)}, bf16[32,64,512]{2,1,0:T(8,128)(2,1)S(1)}, u32[]{:S(2)}, u32[]{:S(2)}) %collective-permute-start) | collective-permute-done | bytes 2097184 | tf_op jit(solution)/shard_map/ppermute | solution.py:478
  7.2 9.6 %spectra.3 = (bf16[256,32,128]{2,1,0:T(8,128)(2,1)S(1)}, bf16[256,64,128]{2,1,0:T(8,128)(2,1)S(1)}) custom-call(bf16[32,64,512]{2,1,0:T(8,128)(2,1)S(1)} %get-tuple-element.41.j_ref, bf16[32,64,512]{2,1,0:T(8,128)(2,1)S(1)} %collective-permute-done.i_ref, bf16[512,256]{1,0:T(8,128)(2,1)S(1)} %copy-done.3, bf16[32,256]{1,0:T(8,128)(2,1)S(1)} %copy-done.7, ...), custom_call_target="tpu_custom_call" | custom-call | flops 2147483648 | bytes 8388608 | tf_op jit(solution)/shard_map/spectra/pallas_call | solution.py:267
  16.9 4.8 %partial_correlations.5 = (bf16[3,16,16,128]{3,2,1,0:T(8,128)(2,1)S(1)}, bf16[3,16,16,128]{3,2,1,0:T(8,128)(2,1)S(1)}, f32[3,16,16,128]{3,2,1,0:T(8,128)S(1)}, bf16[3,16,16,128]{3,2,1,0:T(8,128)(2,1)S(1)}) custom-call(bf16[256,32,128]{2,1,0:T(8,128)(2,1)S(1)} %get-tuple-element.42.refs_0_, bf16[256,64,128]{2,1,0:T(8,128)(2,1)S(1)} %get-tuple-element.43.refs_1_.refs_2_, ...), custom_call_target="tpu_custom_call" | custom-call | flops 805306368 | bytes 6291456 | tf_op jit(solution)/shard_map/partial_correlations/pallas_call | solution.py:408
  21.7 3.0 %collective-permute-start.2 = (bf16[3,16,16,128]{3,2,1,0:T(8,128)(2,1)S(1)}, bf16[3,16,16,128]{3,2,1,0:T(8,128)(2,1)S(1)}, u32[]{:S(2)}, u32[]{:S(2)}) collective-permute-start(bf16[3,16,16,128]{3,2,1,0:T(8,128)(2,1)S(1)} %get-tuple-element.46), channel_id=1, source_target_pairs={{0,4},{4,0},{8,12},{12,8},{1,5},{5,1},{9,13},{13,9},{2,6},{6,2},{1... | collective-permute-start | bytes 589832 | tf_op jit(solution)/shard_map/ppermute | solution.py:481
  24.7 5.0 %collective-permute-done.1.j_ref = bf16[32,32,512]{2,1,0:T(8,128)(2,1)S(1)} collective-permute-done((bf16[32,32,512]{2,1,0:T(8,128)(2,1)S(1)}, bf16[32,32,512]{2,1,0:T(8,128)(2,1)S(1)}, u32[]{:S(2)}, u32[]{:S(2)}) %collective-permute-start.1) | collective-permute-done | bytes 1048608 | tf_op jit(solution)/shard_map/ppermute | solution.py:475
  29.9 1.7 %collective-permute-start.4 = (bf16[32,32,512]{2,1,0:T(8,128)(2,1)S(1)}, bf16[32,32,512]{2,1,0:T(8,128)(2,1)S(1)}, u32[]{:S(2)}, u32[]{:S(2)}) collective-permute-start(bf16[32,32,512]{2,1,0:T(8,128)(2,1)S(1)} %get-tuple-element.51), channel_id=1, source_target_pairs={{0,2},{2,0},{1,3},{3,1},{4,6},{6,4},{5,7},{7,5},{8,10},{10,8},{9,1... | collective-permute-start | bytes 3145736 | tf_op jit(solution)/shard_map/ppermute | solution.py:475
  31.6 1.6 %collective-permute-start.6 = (bf16[3,16,16,128]{3,2,1,0:T(8,128)(2,1)S(1)}, bf16[3,16,16,128]{3,2,1,0:T(8,128)(2,1)S(1)}, u32[]{:S(2)}, u32[]{:S(2)}) collective-permute-start(bf16[3,16,16,128]{3,2,1,0:T(8,128)(2,1)S(1)} %get-tuple-element.55), channel_id=1, source_target_pairs={{0,4},{4,0},{8,12},{12,8},{1,5},{5,1},{9,13},{13,9},{2,6},{6,2},{1... | collective-permute-start | bytes 589832 | tf_op jit(solution)/shard_map/ppermute | solution.py:481
  33.2 2.7 %collective-permute-start.5 = (bf16[3,16,16,128]{3,2,1,0:T(8,128)(2,1)S(1)}, bf16[3,16,16,128]{3,2,1,0:T(8,128)(2,1)S(1)}, u32[]{:S(2)}, u32[]{:S(2)}) collective-permute-start(bf16[3,16,16,128]{3,2,1,0:T(8,128)(2,1)S(1)} %add_convert_fusion.2), channel_id=1, source_target_pairs={{0,8},{4,12},{8,0},{12,4},{1,9},{5,13},{9,1},{13,5},{2,10},{6,14},... | collective-permute-start | bytes 589832 | tf_op jit(solution)/shard_map/ppermute | solution.py:481
  35.9 6.3 %spectra.4 = (bf16[256,16,128]{2,1,0:T(8,128)(2,1)S(1)}, bf16[256,64,128]{2,1,0:T(8,128)(2,1)S(1)}) custom-call(bf16[32,32,512]{2,1,0:T(8,128)(2,1)S(1)} %collective-permute-done.1.j_ref, bf16[32,32,512]{2,1,0:T(8,128)(2,1)S(1)} %collective-permute-done.3.i_ref, bf16[512,256]{1,0:T(8,128)(2,1)S(1)} %copy-done.3, bf16[32,256]{1,0:T(8,128)(2,1)S(1)} %copy-done.6, ...), custom_call_target="tpu_custom_call" | custom-call | flops 1073741824 | bytes 4194304 | tf_op jit(solution)/shard_map/spectra/pallas_call | solution.py:267
  42.1 8.3 %partial_correlations.6 = (bf16[5,16,16,128]{3,2,1,0:T(8,128)(2,1)S(1)}, bf16[5,16,16,128]{3,2,1,0:T(8,128)(2,1)S(1)}, f32[2,16,16,128]{3,2,1,0:T(8,128)S(1)}, bf16[2,16,16,128]{3,2,1,0:T(8,128)(2,1)S(1)}) custom-call(bf16[256,32,128]{2,1,0:T(8,128)(2,1)S(1)} %get-tuple-element.42.refs_0_, bf16[256,16,128]{2,1,0:T(8,128)(2,1)S(1)} %get-tuple-element.48.refs_1_, ...), custom_call_target="tpu_custom_call" | custom-call | flops 1610612736 | bytes 11534336 | tf_op jit(solution)/shard_map/partial_correlations/pallas_call | solution.py:408
  51.0 4.5 %collective-permute-done.4.j_ref = bf16[32,32,512]{2,1,0:T(8,128)(2,1)S(1)} collective-permute-done((bf16[32,32,512]{2,1,0:T(8,128)(2,1)S(1)}, bf16[32,32,512]{2,1,0:T(8,128)(2,1)S(1)}, u32[]{:S(2)}, u32[]{:S(2)}) %collective-permute-start.4) | collective-permute-done | bytes 1048608 | tf_op jit(solution)/shard_map/ppermute | solution.py:475
  55.5 4.3 %collective-permute-done.7 = bf16[5,16,16,128]{3,2,1,0:T(8,128)(2,1)S(1)} collective-permute-done((bf16[5,16,16,128]{3,2,1,0:T(8,128)(2,1)S(1)}, bf16[5,16,16,128]{3,2,1,0:T(8,128)(2,1)S(1)}, u32[]{:S(2)}, u32[]{:S(2)}) %collective-permute-start.7) | collective-permute-done | bytes 327712 | tf_op jit(solution)/shard_map/ppermute | solution.py:481
  62.5 6.3 %spectra.5 = (bf16[256,16,128]{2,1,0:T(8,128)(2,1)S(1)}, bf16[256,64,128]{2,1,0:T(8,128)(2,1)S(1)}) custom-call(bf16[32,32,512]{2,1,0:T(8,128)(2,1)S(1)} %collective-permute-done.4.j_ref, bf16[32,32,512]{2,1,0:T(8,128)(2,1)S(1)} %collective-permute-done.8.i_ref, bf16[512,256]{1,0:T(8,128)(2,1)S(1)} %copy-done.3, bf16[32,256]{1,0:T(8,128)(2,1)S(1)} %copy-done.6, ...), custom_call_target="tpu_custom_call" | custom-call | flops 1073741824 | bytes 4194304 | tf_op jit(solution)/shard_map/spectra/pallas_call | solution.py:267
  68.7 5.7 %partial_correlations.7 = (bf16[4,16,16,128]{3,2,1,0:T(8,128)(2,1)S(1)}, bf16[4,16,16,128]{3,2,1,0:T(8,128)(2,1)S(1)}, f32[1,16,16,128]{3,2,1,0:T(8,128)S(1)}, bf16[1,16,16,128]{3,2,1,0:T(8,128)(2,1)S(1)}) custom-call(bf16[256,32,128]{2,1,0:T(8,128)(2,1)S(1)} %get-tuple-element.42.refs_0_, bf16[256,16,128]{2,1,0:T(8,128)(2,1)S(1)} %get-tuple-element.48.refs_1_, ...), custom_call_target="tpu_custom_call" | custom-call | flops 1207959552 | bytes 7340032 | tf_op jit(solution)/shard_map/partial_correlations/pallas_call | solution.py:408
  75.0 3.0 %collective-permute-done.9.refs_10_ = bf16[5,16,16,128]{3,2,1,0:T(8,128)(2,1)S(1)} collective-permute-done((bf16[5,16,16,128]{3,2,1,0:T(8,128)(2,1)S(1)}, bf16[5,16,16,128]{3,2,1,0:T(8,128)(2,1)S(1)}, u32[]{:S(2)}, u32[]{:S(2)}) %collective-permute-start.9) | collective-permute-done | bytes 327712 | tf_op jit(solution)/shard_map/ppermute | solution.py:481
  78.0 4.0 %partial_correlations.8 = (f32[3,16,16,128]{3,2,1,0:T(8,128)S(1)}, bf16[3,16,16,128]{3,2,1,0:T(8,128)(2,1)S(1)}) custom-call(bf16[256,16,128]{2,1,0:T(8,128)(2,1)S(1)} %get-tuple-element.71.refs_0_, bf16[256,64,128]{2,1,0:T(8,128)(2,1)S(1)} %get-tuple-element.49.refs_3_.refs_1_, bf16[256,64,128]{2,1,0:T(8,128)(2,1)S(1)} %get-tuple-element.67.refs_2_, ...), custom_call_target="tpu_custom_call" | custom-call | flops 402653184 | bytes 9437184 | tf_op jit(solution)/shard_map/partial_correlations/pallas_call | solution.py:408
  82.1 1.4 %collective-permute-done.11 = bf16[4,16,16,128]{3,2,1,0:T(8,128)(2,1)S(1)} collective-permute-done((bf16[4,16,16,128]{3,2,1,0:T(8,128)(2,1)S(1)}, bf16[4,16,16,128]{3,2,1,0:T(8,128)(2,1)S(1)}, u32[]{:S(2)}, u32[]{:S(2)}) %collective-permute-start.11) | collective-permute-done | bytes 262176 | tf_op jit(solution)/shard_map/ppermute | solution.py:481
  83.8 4.0 %partial_correlations.9 = (f32[3,16,16,128]{3,2,1,0:T(8,128)S(1)}, bf16[3,16,16,128]{3,2,1,0:T(8,128)(2,1)S(1)}) custom-call(bf16[256,16,128]{2,1,0:T(8,128)(2,1)S(1)} %get-tuple-element.71.refs_0_, bf16[256,64,128]{2,1,0:T(8,128)(2,1)S(1)} %get-tuple-element.43.refs_1_.refs_2_, bf16[128,512]{1,0:T(8,128)(2,1)S(1)} %copy-done, bf16[256,256]{1,0:T(8,128)(2,1)S(1)} %copy-done.1), custom_call_target="tpu_custom_call" | custom-call | flops 402653184 | bytes 5242880 | tf_op jit(solution)/shard_map/partial_correlations/pallas_call | solution.py:408
  87.8 1.6 %collective-permute-start.13 = (bf16[3,16,16,128]{3,2,1,0:T(8,128)(2,1)S(1)}, bf16[3,16,16,128]{3,2,1,0:T(8,128)(2,1)S(1)}, u32[]{:S(2)}, u32[]{:S(2)}) collective-permute-start(bf16[3,16,16,128]{3,2,1,0:T(8,128)(2,1)S(1)} %get-tuple-element.75), channel_id=1, source_target_pairs={{0,4},{4,0},{8,12},{12,8},{1,5},{5,1},{9,13},{13,9},{2,6},{6,2},{1... | collective-permute-start | bytes 589832 | tf_op jit(solution)/shard_map/ppermute | solution.py:481
  89.4 4.2 %collective-permute-done.12.refs_7_ = bf16[4,16,16,128]{3,2,1,0:T(8,128)(2,1)S(1)} collective-permute-done((bf16[4,16,16,128]{3,2,1,0:T(8,128)(2,1)S(1)}, bf16[4,16,16,128]{3,2,1,0:T(8,128)(2,1)S(1)}, u32[]{:S(2)}, u32[]{:S(2)}) %collective-permute-start.12) | collective-permute-done | bytes 262176 | tf_op jit(solution)/shard_map/ppermute | solution.py:481
  93.6 6.6 %collective-permute-done.13.refs_8_ = bf16[3,16,16,128]{3,2,1,0:T(8,128)(2,1)S(1)} collective-permute-done((bf16[3,16,16,128]{3,2,1,0:T(8,128)(2,1)S(1)}, bf16[3,16,16,128]{3,2,1,0:T(8,128)(2,1)S(1)}, u32[]{:S(2)}, u32[]{:S(2)}) %collective-permute-start.13) | collective-permute-done | bytes 196640 | tf_op jit(solution)/shard_map/ppermute | solution.py:481
  100.1 1.2 %assembled.1 = f32[3,1,32,32,128]{4,3,2,1,0:T(8,128)} custom-call(f32[3,16,16,128]{3,2,1,0:T(8,128)S(1)} %get-tuple-element.44.refs_0_, f32[2,16,16,128]{3,2,1,0:T(8,128)S(1)} %get-tuple-element.50.refs_1_, f32[1,16,16,128]{3,2,1,0:T(8,128)S(1)} %get-tuple-element.62.refs_2_, f32[3,16,16,128]{3,2,1,0:T(8,128)S(1)} %get-tuple-element.68.refs_3_, ...), custom_call_target="tpu_custom_call" | custom-call | bytes 2359296 | tf_op jit(solution)/shard_map/assembled/pallas_call | solution.py:452
  (36 shorter events, 5.4 us)
Async XLA Ops:
  0.0 0.7 copy-start.2
  0.7 6.6 %copy-start.3 = (bf16[512,256]{1,0:T(8,128)(2,1)S(1)}, bf16[512,256]{1,0:T(8,128)(2,1)}, u32[]{:S(2)}) copy-start(bf16[512,256]{1,0:T(8,128)(2,1)} %constant.21.table_ref) | copy-start | bytes 786436
  0.7 6.6 %copy-start.5 = (bf16[128,128]{1,0:T(8,128)(2,1)S(1)}, bf16[128,128]{1,0:T(8,128)(2,1)}, u32[]{:S(2)}) copy-start(bf16[128,128]{1,0:T(8,128)(2,1)} %constant.23.to_j_ref) | copy-start | bytes 98308
  0.7 6.6 %copy-start.7 = (bf16[32,256]{1,0:T(8,128)(2,1)S(1)}, bf16[32,256]{1,0:T(8,128)(2,1)}, u32[]{:S(2)}) copy-start(bf16[32,256]{1,0:T(8,128)(2,1)} %constant.22.to_i_ref) | copy-start | bytes 49156
  2.9 4.3 %collective-permute-start = (bf16[32,64,512]{2,1,0:T(8,128)(2,1)S(1)}, bf16[32,64,512]{2,1,0:T(8,128)(2,1)S(1)}, u32[]{:S(2)}, u32[]{:S(2)}) collective-permute-start(bf16[32,64,512]{2,1,0:T(8,128)(2,1)S(1)} %get-tuple-element.41.j_ref), channel_id=1, source_target_pairs={{0,1},{1,0},{2,3},{3,2},{4,5},{5,4},{6,7},{7,6},{8,9},{9,8},{10,11... | collective-permute-start | bytes 6291464 | tf_op jit(solution)/shard_map/ppermute | solution.py:478
  3.5 13.4 %copy-start = (bf16[128,512]{1,0:T(8,128)(2,1)S(1)}, bf16[128,512]{1,0:T(8,128)(2,1)}, u32[]{:S(2)}) copy-start(bf16[128,512]{1,0:T(8,128)(2,1)} %constant.24.refs_2_.refs_4_.refs_3_) | copy-start | bytes 393220
  3.5 13.4 %copy-start.1 = (bf16[256,256]{1,0:T(8,128)(2,1)S(1)}, bf16[256,256]{1,0:T(8,128)(2,1)}, u32[]{:S(2)}) copy-start(bf16[256,256]{1,0:T(8,128)(2,1)} %constant.25.refs_3_.refs_5_.refs_4_) | copy-start | bytes 393220
  3.5 26.3 %collective-permute-start.1 = (bf16[32,32,512]{2,1,0:T(8,128)(2,1)S(1)}, bf16[32,32,512]{2,1,0:T(8,128)(2,1)S(1)}, u32[]{:S(2)}, u32[]{:S(2)}) collective-permute-start(bf16[32,32,512]{2,1,0:T(8,128)(2,1)S(1)} %get-tuple-element.45), channel_id=1, source_target_pairs={{0,2},{2,0},{1,3},{3,1},{4,6},{6,4},{5,7},{7,5},{8,10},{10,8},{9,1... | collective-permute-start | bytes 3145736 | tf_op jit(solution)/shard_map/ppermute | solution.py:475
  16.9 19.0 %copy-start.4 = (bf16[128,256]{1,0:T(8,128)(2,1)S(1)}, bf16[128,256]{1,0:T(8,128)(2,1)}, u32[]{:S(2)}) copy-start(bf16[128,256]{1,0:T(8,128)(2,1)} %constant.27.to_j_ref) | copy-start | bytes 196612
  16.9 19.0 %copy-start.6 = (bf16[32,256]{1,0:T(8,128)(2,1)S(1)}, bf16[32,256]{1,0:T(8,128)(2,1)}, u32[]{:S(2)}) copy-start(bf16[32,256]{1,0:T(8,128)(2,1)} %constant.26.to_i_ref) | copy-start | bytes 49156
  21.7 8.2 %collective-permute-start.2 = (bf16[3,16,16,128]{3,2,1,0:T(8,128)(2,1)S(1)}, bf16[3,16,16,128]{3,2,1,0:T(8,128)(2,1)S(1)}, u32[]{:S(2)}, u32[]{:S(2)}) collective-permute-start(bf16[3,16,16,128]{3,2,1,0:T(8,128)(2,1)S(1)} %get-tuple-element.46), channel_id=1, source_target_pairs={{0,4},{4,0},{8,12},{12,8},{1,5},{5,1},{9,13},{13,9},{2,6},{6,2},{1... | collective-permute-start | bytes 589832 | tf_op jit(solution)/shard_map/ppermute | solution.py:481
  29.9 6.0 %collective-permute-start.3 = (bf16[32,32,512]{2,1,0:T(8,128)(2,1)S(1)}, bf16[32,32,512]{2,1,0:T(8,128)(2,1)S(1)}, u32[]{:S(2)}, u32[]{:S(2)}) collective-permute-start(bf16[32,32,512]{2,1,0:T(8,128)(2,1)S(1)} %collective-permute-done.1.j_ref), channel_id=1, source_target_pairs={{0,1},{1,0},{2,3},{3,2},{4,5},{5,4},{6,7},{7,6},{8,9},{9,8},{10,11... | collective-permute-start | bytes 3145736 | tf_op jit(solution)/shard_map/ppermute | solution.py:478
  29.9 25.6 %collective-permute-start.4 = (bf16[32,32,512]{2,1,0:T(8,128)(2,1)S(1)}, bf16[32,32,512]{2,1,0:T(8,128)(2,1)S(1)}, u32[]{:S(2)}, u32[]{:S(2)}) collective-permute-start(bf16[32,32,512]{2,1,0:T(8,128)(2,1)S(1)} %get-tuple-element.51), channel_id=1, source_target_pairs={{0,2},{2,0},{1,3},{3,1},{4,6},{6,4},{5,7},{7,5},{8,10},{10,8},{9,1... | collective-permute-start | bytes 3145736 | tf_op jit(solution)/shard_map/ppermute | solution.py:475
  31.6 18.9 %collective-permute-start.6 = (bf16[3,16,16,128]{3,2,1,0:T(8,128)(2,1)S(1)}, bf16[3,16,16,128]{3,2,1,0:T(8,128)(2,1)S(1)}, u32[]{:S(2)}, u32[]{:S(2)}) collective-permute-start(bf16[3,16,16,128]{3,2,1,0:T(8,128)(2,1)S(1)} %get-tuple-element.55), channel_id=1, source_target_pairs={{0,4},{4,0},{8,12},{12,8},{1,5},{5,1},{9,13},{13,9},{2,6},{6,2},{1... | collective-permute-start | bytes 589832 | tf_op jit(solution)/shard_map/ppermute | solution.py:481
  33.2 17.3 %collective-permute-start.5 = (bf16[3,16,16,128]{3,2,1,0:T(8,128)(2,1)S(1)}, bf16[3,16,16,128]{3,2,1,0:T(8,128)(2,1)S(1)}, u32[]{:S(2)}, u32[]{:S(2)}) collective-permute-start(bf16[3,16,16,128]{3,2,1,0:T(8,128)(2,1)S(1)} %add_convert_fusion.2), channel_id=1, source_target_pairs={{0,8},{4,12},{8,0},{12,4},{1,9},{5,13},{9,1},{13,5},{2,10},{6,14},... | collective-permute-start | bytes 589832 | tf_op jit(solution)/shard_map/ppermute | solution.py:481
  50.5 9.3 %collective-permute-start.7 = (bf16[5,16,16,128]{3,2,1,0:T(8,128)(2,1)S(1)}, bf16[5,16,16,128]{3,2,1,0:T(8,128)(2,1)S(1)}, u32[]{:S(2)}, u32[]{:S(2)}) collective-permute-start(bf16[5,16,16,128]{3,2,1,0:T(8,128)(2,1)S(1)} %get-tuple-element.56), channel_id=1, source_target_pairs={{0,4},{4,0},{8,12},{12,8},{1,5},{5,1},{9,13},{13,9},{2,6},{6,2},{1... | collective-permute-start | bytes 983048 | tf_op jit(solution)/shard_map/ppermute | solution.py:481
  59.8 2.7 %collective-permute-start.8 = (bf16[32,32,512]{2,1,0:T(8,128)(2,1)S(1)}, bf16[32,32,512]{2,1,0:T(8,128)(2,1)S(1)}, u32[]{:S(2)}, u32[]{:S(2)}) collective-permute-start(bf16[32,32,512]{2,1,0:T(8,128)(2,1)S(1)} %collective-permute-done.4.j_ref), channel_id=1, source_target_pairs={{0,1},{1,0},{2,3},{3,2},{4,5},{5,4},{6,7},{7,6},{8,9},{9,8},{10,11... | collective-permute-start | bytes 3145736 | tf_op jit(solution)/shard_map/ppermute | solution.py:478
  59.9 18.1 %collective-permute-start.9 = (bf16[5,16,16,128]{3,2,1,0:T(8,128)(2,1)S(1)}, bf16[5,16,16,128]{3,2,1,0:T(8,128)(2,1)S(1)}, u32[]{:S(2)}, u32[]{:S(2)}) collective-permute-start(bf16[5,16,16,128]{3,2,1,0:T(8,128)(2,1)S(1)} %add_convert_fusion), channel_id=1, source_target_pairs={{0,8},{4,12},{8,0},{12,4},{1,9},{5,13},{9,1},{13,5},{2,10},{6,14},... | collective-permute-start | bytes 983048 | tf_op jit(solution)/shard_map/ppermute | solution.py:481
  60.3 14.7 %collective-permute-start.10 = (bf16[2,16,16,128]{3,2,1,0:T(8,128)(2,1)S(1)}, bf16[2,16,16,128]{3,2,1,0:T(8,128)(2,1)S(1)}, u32[]{:S(2)}, u32[]{:S(2)}) collective-permute-start(bf16[2,16,16,128]{3,2,1,0:T(8,128)(2,1)S(1)} %get-tuple-element.66), channel_id=1, source_target_pairs={{0,4},{4,0},{8,12},{12,8},{1,5},{5,1},{9,13},{13,9},{2,6},{6,2},{1... | collective-permute-start | bytes 393224 | tf_op jit(solution)/shard_map/ppermute | solution.py:481
  74.5 9.1 %collective-permute-start.11 = (bf16[4,16,16,128]{3,2,1,0:T(8,128)(2,1)S(1)}, bf16[4,16,16,128]{3,2,1,0:T(8,128)(2,1)S(1)}, u32[]{:S(2)}, u32[]{:S(2)}) collective-permute-start(bf16[4,16,16,128]{3,2,1,0:T(8,128)(2,1)S(1)} %get-tuple-element.65), channel_id=1, source_target_pairs={{0,4},{4,0},{8,12},{12,8},{1,5},{5,1},{9,13},{13,9},{2,6},{6,2},{1... | collective-permute-start | bytes 786440 | tf_op jit(solution)/shard_map/ppermute | solution.py:481
  82.0 11.5 %collective-permute-start.12 = (bf16[4,16,16,128]{3,2,1,0:T(8,128)(2,1)S(1)}, bf16[4,16,16,128]{3,2,1,0:T(8,128)(2,1)S(1)}, u32[]{:S(2)}, u32[]{:S(2)}) collective-permute-start(bf16[4,16,16,128]{3,2,1,0:T(8,128)(2,1)S(1)} %pad_maximum_fusion), channel_id=1, source_target_pairs={{0,4},{4,0},{8,12},{12,8},{1,5},{5,1},{9,13},{13,9},{2,6},{6,2},{1... | collective-permute-start | bytes 786440 | tf_op jit(solution)/shard_map/ppermute | solution.py:481
  83.6 16.5 %collective-permute-start.14 = (bf16[4,16,16,128]{3,2,1,0:T(8,128)(2,1)S(1)}, bf16[4,16,16,128]{3,2,1,0:T(8,128)(2,1)S(1)}, u32[]{:S(2)}, u32[]{:S(2)}) collective-permute-start(bf16[4,16,16,128]{3,2,1,0:T(8,128)(2,1)S(1)} %add_convert_fusion.1), channel_id=1, source_target_pairs={{0,8},{4,12},{8,0},{12,4},{1,9},{5,13},{9,1},{13,5},{2,10},{6,14},... | collective-permute-start | bytes 786440 | tf_op jit(solution)/shard_map/ppermute | solution.py:481
  87.8 12.4 %collective-permute-start.13 = (bf16[3,16,16,128]{3,2,1,0:T(8,128)(2,1)S(1)}, bf16[3,16,16,128]{3,2,1,0:T(8,128)(2,1)S(1)}, u32[]{:S(2)}, u32[]{:S(2)}) collective-permute-start(bf16[3,16,16,128]{3,2,1,0:T(8,128)(2,1)S(1)} %get-tuple-element.75), channel_id=1, source_target_pairs={{0,4},{4,0},{8,12},{12,8},{1,5},{5,1},{9,13},{13,9},{2,6},{6,2},{1... | collective-permute-start | bytes 589832 | tf_op jit(solution)/shard_map/ppermute | solution.py:481

commit v4 on v1

--- a/solution.py
+++ b/solution.py
@@ -177,7 +177,7 @@
     line = depth // folded
     pitch = line + 1
     per_step = 2 * folded
-    batch = 8
+    batch = 16
 
     def kernel(j_ref, i_ref, table_ref, to_i_ref, to_j_ref, i_out, j_out, wide):
         same = lax.axis_index("sub") == lax.axis_index("rep")
@@ -286,7 +286,7 @@
     for kinds in slices.values():
         kinds.sort()
     total = len(groups) * piece
-    batch = 4
+    batch = 8 if len(groups) == 1 else 4
 
     def first_of(at):
         (out,) = [positions for positions in outs if at in positions]

time: 103 us -> 102 us (level)
  Pallas kernels: 54.3 us -> 52 us
  waiting for transfers between devices: 30.5 us -> 31.9 us
    pallas_call x3, Pallas kernels: 23.9 us -> 21.7 us  [spectra(): kernel_call(kernel, 'spectra', 4 * samples * samples * wins * given, 4 *...]
    ppermute x2, waiting for transfers between devices: 8.2 us -> 9.61 us  [over_sub(): return lax.ppermute(rows, 'sub', [(0, 1), (1, 0)])]
  transfers between devices with their start and end apart: 15 -> 15, of which waited for: 10 -> 10; matrix products, arithmetic and copies ran while one was open for 0% -> 0% of each run, Pallas kernels for 49% -> 48%
where the time goes in v4:
time: 102 us; the launch traced here: 101 us
  Pallas kernels  52 us (51%)
  waiting for transfers between devices  31.9 us (31%)
  starting transfers between devices  16.4 us (16%)
    pallas_call x5, Pallas kernels, partial_correlations(): kernel_call(kernel, 'partial_correlations', 4 * total * bins * depth * LA...  26.8 us
    pallas_call x3, Pallas kernels, spectra(): kernel_call(kernel, 'spectra', 4 * samples * samples * wins * given, 4 *...  21.7 us
    ppermute x10, waiting for transfers between devices, with_device(): lax.ppermute(share, 'chan', [(z, z ^ apart) for z in range(chan_count)])  20 us
    ppermute x10, starting transfers between devices, with_device(): lax.ppermute(share, 'chan', [(z, z ^ apart) for z in range(chan_count)])  11.6 us
    ppermute x2, waiting for transfers between devices, over_sub(): return lax.ppermute(rows, 'sub', [(0, 1), (1, 0)])  9.61 us
    ppermute x2, starting transfers between devices, over_sub(): return lax.ppermute(rows, 'sub', [(0, 1), (1, 0)])  4.24 us
    pallas_call x1, Pallas kernels, order_rows(): kernel_call(kernel, 'order_rows', 0, 3 * traces.size * 2, vmem_bytes=ORDE...  2.28 us
    ppermute x3, waiting for transfers between devices, over_core(): return lax.ppermute(rows, 'rep', [(0, 1), (1, 0)])  2.24 us
  transfers between devices with their start and end apart: 15, of which 10 were waited for; matrix products, arithmetic and copies ran while one was open for 0% of the time, Pallas kernels for 48%

profile of v4, /device:TPU:0, one launch (start us, length us, event | category | flops | bytes accessed | tf_op | source)
XLA Modules:
  0.0 101.5 jit_solution(17943815380323643481)
XLA Ops:
  0.7 2.3 %order_rows.1 = (bf16[32,64,512]{2,1,0:T(8,128)(2,1)S(1)}, bf16[32,32,512]{2,1,0:T(8,128)(2,1)S(1)}, bf16[32,32,512]{2,1,0:T(8,128)(2,1)S(1)}) custom-call(s32[64]{0:T(128)S(1)} %copy-done.2, bf16[64,32,512]{2,1,0:T(8,128)(2,1)} %traces_ref.1), custom_call_target="tpu_custom_call" | custom-call | bytes 6291456 | tf_op jit(solution)/shard_map/order_rows/pallas_call | solution.py:147
  3.5 2.6 %collective-permute-start.1 = (bf16[32,32,512]{2,1,0:T(8,128)(2,1)S(1)}, bf16[32,32,512]{2,1,0:T(8,128)(2,1)S(1)}, u32[]{:S(2)}, u32[]{:S(2)}) collective-permute-start(bf16[32,32,512]{2,1,0:T(8,128)(2,1)S(1)} %get-tuple-element.45), channel_id=1, source_target_pairs={{0,2},{2,0},{1,3},{3,1},{4,6},{6,4},{5,7},{7,5},{8,10},{10,8},{9,1... | collective-permute-start | bytes 3145736 | tf_op jit(solution)/shard_map/ppermute | solution.py:461
  6.1 1.2 %collective-permute-done.i_ref = bf16[32,64,512]{2,1,0:T(8,128)(2,1)S(1)} collective-permute-done((bf16[32,64,512]{2,1,0:T(8,128)(2,1)S(1)}, bf16[32,64,512]{2,1,0:T(8,128)(2,1)S(1)}, u32[]{:S(2)}, u32[]{:S(2)}) %collective-permute-start) | collective-permute-done | bytes 2097184 | tf_op jit(solution)/shard_map/ppermute | solution.py:464
  7.3 9.9 %spectra.3 = (bf16[256,32,128]{2,1,0:T(8,128)(2,1)S(1)}, bf16[256,64,128]{2,1,0:T(8,128)(2,1)S(1)}) custom-call(bf16[32,64,512]{2,1,0:T(8,128)(2,1)S(1)} %get-tuple-element.41.j_ref, bf16[32,64,512]{2,1,0:T(8,128)(2,1)S(1)} %collective-permute-done.i_ref, bf16[512,512]{1,0:T(8,128)(2,1)S(1)} %copy-done.3, bf16[32,256]{1,0:T(8,128)(2,1)S(1)} %copy-done.7, ...), custom_call_target="tpu_custom_call" | custom-call | flops 2147483648 | bytes 8388608 | tf_op jit(solution)/shard_map/spectra/pallas_call | solution.py:253
  17.2 4.8 %partial_correlations.5 = (bf16[3,16,16,128]{3,2,1,0:T(8,128)(2,1)S(1)}, bf16[3,16,16,128]{3,2,1,0:T(8,128)(2,1)S(1)}, f32[3,16,16,128]{3,2,1,0:T(8,128)S(1)}, bf16[3,16,16,128]{3,2,1,0:T(8,128)(2,1)S(1)}) custom-call(bf16[256,32,128]{2,1,0:T(8,128)(2,1)S(1)} %get-tuple-element.42.refs_0_, bf16[256,64,128]{2,1,0:T(8,128)(2,1)S(1)} %get-tuple-element.43.refs_1_.refs_2_, ...), custom_call_target="tpu_custom_call" | custom-call | flops 805306368 | bytes 6291456 | tf_op jit(solution)/shard_map/partial_correlations/pallas_call | solution.py:394
  22.1 3.0 %collective-permute-start.2 = (bf16[3,16,16,128]{3,2,1,0:T(8,128)(2,1)S(1)}, bf16[3,16,16,128]{3,2,1,0:T(8,128)(2,1)S(1)}, u32[]{:S(2)}, u32[]{:S(2)}) collective-permute-start(bf16[3,16,16,128]{3,2,1,0:T(8,128)(2,1)S(1)} %get-tuple-element.46), channel_id=1, source_target_pairs={{0,4},{4,0},{8,12},{12,8},{1,5},{5,1},{9,13},{13,9},{2,6},{6,2},{1... | collective-permute-start | bytes 589832 | tf_op jit(solution)/shard_map/ppermute | solution.py:467
  25.1 4.7 %collective-permute-done.1.j_ref = bf16[32,32,512]{2,1,0:T(8,128)(2,1)S(1)} collective-permute-done((bf16[32,32,512]{2,1,0:T(8,128)(2,1)S(1)}, bf16[32,32,512]{2,1,0:T(8,128)(2,1)S(1)}, u32[]{:S(2)}, u32[]{:S(2)}) %collective-permute-start.1) | collective-permute-done | bytes 1048608 | tf_op jit(solution)/shard_map/ppermute | solution.py:461
  30.3 1.7 %collective-permute-start.4 = (bf16[32,32,512]{2,1,0:T(8,128)(2,1)S(1)}, bf16[32,32,512]{2,1,0:T(8,128)(2,1)S(1)}, u32[]{:S(2)}, u32[]{:S(2)}) collective-permute-start(bf16[32,32,512]{2,1,0:T(8,128)(2,1)S(1)} %get-tuple-element.51), channel_id=1, source_target_pairs={{0,2},{2,0},{1,3},{3,1},{4,6},{6,4},{5,7},{7,5},{8,10},{10,8},{9,1... | collective-permute-start | bytes 3145736 | tf_op jit(solution)/shard_map/ppermute | solution.py:461
  31.9 1.6 %collective-permute-start.6 = (bf16[3,16,16,128]{3,2,1,0:T(8,128)(2,1)S(1)}, bf16[3,16,16,128]{3,2,1,0:T(8,128)(2,1)S(1)}, u32[]{:S(2)}, u32[]{:S(2)}) collective-permute-start(bf16[3,16,16,128]{3,2,1,0:T(8,128)(2,1)S(1)} %get-tuple-element.55), channel_id=1, source_target_pairs={{0,4},{4,0},{8,12},{12,8},{1,5},{5,1},{9,13},{13,9},{2,6},{6,2},{1... | collective-permute-start | bytes 589832 | tf_op jit(solution)/shard_map/ppermute | solution.py:467
  33.6 2.7 %collective-permute-start.5 = (bf16[3,16,16,128]{3,2,1,0:T(8,128)(2,1)S(1)}, bf16[3,16,16,128]{3,2,1,0:T(8,128)(2,1)S(1)}, u32[]{:S(2)}, u32[]{:S(2)}) collective-permute-start(bf16[3,16,16,128]{3,2,1,0:T(8,128)(2,1)S(1)} %add_convert_fusion.2), channel_id=1, source_target_pairs={{0,8},{4,12},{8,0},{12,4},{1,9},{5,13},{9,1},{13,5},{2,10},{6,14},... | collective-permute-start | bytes 589832 | tf_op jit(solution)/shard_map/ppermute | solution.py:467
  36.2 5.9 %spectra.4 = (bf16[256,16,128]{2,1,0:T(8,128)(2,1)S(1)}, bf16[256,64,128]{2,1,0:T(8,128)(2,1)S(1)}) custom-call(bf16[32,32,512]{2,1,0:T(8,128)(2,1)S(1)} %collective-permute-done.1.j_ref, bf16[32,32,512]{2,1,0:T(8,128)(2,1)S(1)} %collective-permute-done.3.i_ref, bf16[512,512]{1,0:T(8,128)(2,1)S(1)} %copy-done.3, bf16[32,256]{1,0:T(8,128)(2,1)S(1)} %copy-done.6, ...), custom_call_target="tpu_custom_call" | custom-call | flops 1073741824 | bytes 4194304 | tf_op jit(solution)/shard_map/spectra/pallas_call | solution.py:253
  42.1 8.3 %partial_correlations.6 = (bf16[5,16,16,128]{3,2,1,0:T(8,128)(2,1)S(1)}, bf16[5,16,16,128]{3,2,1,0:T(8,128)(2,1)S(1)}, f32[2,16,16,128]{3,2,1,0:T(8,128)S(1)}, bf16[2,16,16,128]{3,2,1,0:T(8,128)(2,1)S(1)}) custom-call(bf16[256,32,128]{2,1,0:T(8,128)(2,1)S(1)} %get-tuple-element.42.refs_0_, bf16[256,16,128]{2,1,0:T(8,128)(2,1)S(1)} %get-tuple-element.48.refs_1_, ...), custom_call_target="tpu_custom_call" | custom-call | flops 1610612736 | bytes 11534336 | tf_op jit(solution)/shard_map/partial_correlations/pallas_call | solution.py:394
  50.9 4.9 %collective-permute-done.4.j_ref = bf16[32,32,512]{2,1,0:T(8,128)(2,1)S(1)} collective-permute-done((bf16[32,32,512]{2,1,0:T(8,128)(2,1)S(1)}, bf16[32,32,512]{2,1,0:T(8,128)(2,1)S(1)}, u32[]{:S(2)}, u32[]{:S(2)}) %collective-permute-start.4) | collective-permute-done | bytes 1048608 | tf_op jit(solution)/shard_map/ppermute | solution.py:461
  55.8 3.9 %collective-permute-done.7 = bf16[5,16,16,128]{3,2,1,0:T(8,128)(2,1)S(1)} collective-permute-done((bf16[5,16,16,128]{3,2,1,0:T(8,128)(2,1)S(1)}, bf16[5,16,16,128]{3,2,1,0:T(8,128)(2,1)S(1)}, u32[]{:S(2)}, u32[]{:S(2)}) %collective-permute-start.7) | collective-permute-done | bytes 327712 | tf_op jit(solution)/shard_map/ppermute | solution.py:467
  62.4 5.9 %spectra.5 = (bf16[256,16,128]{2,1,0:T(8,128)(2,1)S(1)}, bf16[256,64,128]{2,1,0:T(8,128)(2,1)S(1)}) custom-call(bf16[32,32,512]{2,1,0:T(8,128)(2,1)S(1)} %collective-permute-done.4.j_ref, bf16[32,32,512]{2,1,0:T(8,128)(2,1)S(1)} %collective-permute-done.8.i_ref, bf16[512,512]{1,0:T(8,128)(2,1)S(1)} %copy-done.3, bf16[32,256]{1,0:T(8,128)(2,1)S(1)} %copy-done.6, ...), custom_call_target="tpu_custom_call" | custom-call | flops 1073741824 | bytes 4194304 | tf_op jit(solution)/shard_map/spectra/pallas_call | solution.py:253
  68.3 5.7 %partial_correlations.7 = (bf16[4,16,16,128]{3,2,1,0:T(8,128)(2,1)S(1)}, bf16[4,16,16,128]{3,2,1,0:T(8,128)(2,1)S(1)}, f32[1,16,16,128]{3,2,1,0:T(8,128)S(1)}, bf16[1,16,16,128]{3,2,1,0:T(8,128)(2,1)S(1)}) custom-call(bf16[256,32,128]{2,1,0:T(8,128)(2,1)S(1)} %get-tuple-element.42.refs_0_, bf16[256,16,128]{2,1,0:T(8,128)(2,1)S(1)} %get-tuple-element.48.refs_1_, ...), custom_call_target="tpu_custom_call" | custom-call | flops 1207959552 | bytes 7340032 | tf_op jit(solution)/shard_map/partial_correlations/pallas_call | solution.py:394
  74.6 3.4 %collective-permute-done.9.refs_10_ = bf16[5,16,16,128]{3,2,1,0:T(8,128)(2,1)S(1)} collective-permute-done((bf16[5,16,16,128]{3,2,1,0:T(8,128)(2,1)S(1)}, bf16[5,16,16,128]{3,2,1,0:T(8,128)(2,1)S(1)}, u32[]{:S(2)}, u32[]{:S(2)}) %collective-permute-start.9) | collective-permute-done | bytes 327712 | tf_op jit(solution)/shard_map/ppermute | solution.py:467
  78.0 4.0 %partial_correlations.8 = (f32[3,16,16,128]{3,2,1,0:T(8,128)S(1)}, bf16[3,16,16,128]{3,2,1,0:T(8,128)(2,1)S(1)}) custom-call(bf16[256,16,128]{2,1,0:T(8,128)(2,1)S(1)} %get-tuple-element.71.refs_0_, bf16[256,64,128]{2,1,0:T(8,128)(2,1)S(1)} %get-tuple-element.49.refs_3_.refs_1_, bf16[256,64,128]{2,1,0:T(8,128)(2,1)S(1)} %get-tuple-element.67.refs_2_, ...), custom_call_target="tpu_custom_call" | custom-call | flops 402653184 | bytes 9437184 | tf_op jit(solution)/shard_map/partial_correlations/pallas_call | solution.py:394
  82.1 1.4 %collective-permute-done.11 = bf16[4,16,16,128]{3,2,1,0:T(8,128)(2,1)S(1)} collective-permute-done((bf16[4,16,16,128]{3,2,1,0:T(8,128)(2,1)S(1)}, bf16[4,16,16,128]{3,2,1,0:T(8,128)(2,1)S(1)}, u32[]{:S(2)}, u32[]{:S(2)}) %collective-permute-start.11) | collective-permute-done | bytes 262176 | tf_op jit(solution)/shard_map/ppermute | solution.py:467
  83.7 4.0 %partial_correlations.9 = (f32[3,16,16,128]{3,2,1,0:T(8,128)S(1)}, bf16[3,16,16,128]{3,2,1,0:T(8,128)(2,1)S(1)}) custom-call(bf16[256,16,128]{2,1,0:T(8,128)(2,1)S(1)} %get-tuple-element.71.refs_0_, bf16[256,64,128]{2,1,0:T(8,128)(2,1)S(1)} %get-tuple-element.43.refs_1_.refs_2_, bf16[128,512]{1,0:T(8,128)(2,1)S(1)} %copy-done, bf16[256,256]{1,0:T(8,128)(2,1)S(1)} %copy-done.1), custom_call_target="tpu_custom_call" | custom-call | flops 402653184 | bytes 5242880 | tf_op jit(solution)/shard_map/partial_correlations/pallas_call | solution.py:394
  87.7 1.6 %collective-permute-start.13 = (bf16[3,16,16,128]{3,2,1,0:T(8,128)(2,1)S(1)}, bf16[3,16,16,128]{3,2,1,0:T(8,128)(2,1)S(1)}, u32[]{:S(2)}, u32[]{:S(2)}) collective-permute-start(bf16[3,16,16,128]{3,2,1,0:T(8,128)(2,1)S(1)} %get-tuple-element.75), channel_id=1, source_target_pairs={{0,4},{4,0},{8,12},{12,8},{1,5},{5,1},{9,13},{13,9},{2,6},{6,2},{1... | collective-permute-start | bytes 589832 | tf_op jit(solution)/shard_map/ppermute | solution.py:467
  89.3 4.2 %collective-permute-done.12.refs_7_ = bf16[4,16,16,128]{3,2,1,0:T(8,128)(2,1)S(1)} collective-permute-done((bf16[4,16,16,128]{3,2,1,0:T(8,128)(2,1)S(1)}, bf16[4,16,16,128]{3,2,1,0:T(8,128)(2,1)S(1)}, u32[]{:S(2)}, u32[]{:S(2)}) %collective-permute-start.12) | collective-permute-done | bytes 262176 | tf_op jit(solution)/shard_map/ppermute | solution.py:467
  93.4 6.7 %collective-permute-done.13.refs_8_ = bf16[3,16,16,128]{3,2,1,0:T(8,128)(2,1)S(1)} collective-permute-done((bf16[3,16,16,128]{3,2,1,0:T(8,128)(2,1)S(1)}, bf16[3,16,16,128]{3,2,1,0:T(8,128)(2,1)S(1)}, u32[]{:S(2)}, u32[]{:S(2)}) %collective-permute-start.13) | collective-permute-done | bytes 196640 | tf_op jit(solution)/shard_map/ppermute | solution.py:467
  100.1 1.2 %assembled.1 = f32[3,1,32,32,128]{4,3,2,1,0:T(8,128)} custom-call(f32[3,16,16,128]{3,2,1,0:T(8,128)S(1)} %get-tuple-element.44.refs_0_, f32[2,16,16,128]{3,2,1,0:T(8,128)S(1)} %get-tuple-element.50.refs_1_, f32[1,16,16,128]{3,2,1,0:T(8,128)S(1)} %get-tuple-element.62.refs_2_, f32[3,16,16,128]{3,2,1,0:T(8,128)S(1)} %get-tuple-element.68.refs_3_, ...), custom_call_target="tpu_custom_call" | custom-call | bytes 2359296 | tf_op jit(solution)/shard_map/assembled/pallas_call | solution.py:438
  (36 shorter events, 5.8 us)
Async XLA Ops:
  0.0 0.7 copy-start.2
  0.7 6.6 %copy-start.3 = (bf16[512,512]{1,0:T(8,128)(2,1)S(1)}, bf16[512,512]{1,0:T(8,128)(2,1)}, u32[]{:S(2)}) copy-start(bf16[512,512]{1,0:T(8,128)(2,1)} %constant.21.table_ref) | copy-start | bytes 1572868
  0.7 6.6 %copy-start.5 = (bf16[128,128]{1,0:T(8,128)(2,1)S(1)}, bf16[128,128]{1,0:T(8,128)(2,1)}, u32[]{:S(2)}) copy-start(bf16[128,128]{1,0:T(8,128)(2,1)} %constant.23.to_j_ref) | copy-start | bytes 98308
  0.7 6.6 %copy-start.7 = (bf16[32,256]{1,0:T(8,128)(2,1)S(1)}, bf16[32,256]{1,0:T(8,128)(2,1)}, u32[]{:S(2)}) copy-start(bf16[32,256]{1,0:T(8,128)(2,1)} %constant.22.to_i_ref) | copy-start | bytes 49156
  2.9 4.3 %collective-permute-start = (bf16[32,64,512]{2,1,0:T(8,128)(2,1)S(1)}, bf16[32,64,512]{2,1,0:T(8,128)(2,1)S(1)}, u32[]{:S(2)}, u32[]{:S(2)}) collective-permute-start(bf16[32,64,512]{2,1,0:T(8,128)(2,1)S(1)} %get-tuple-element.41.j_ref), channel_id=1, source_target_pairs={{0,1},{1,0},{2,3},{3,2},{4,5},{5,4},{6,7},{7,6},{8,9},{9,8},{10,11... | collective-permute-start | bytes 6291464 | tf_op jit(solution)/shard_map/ppermute | solution.py:464
  3.5 13.7 %copy-start = (bf16[128,512]{1,0:T(8,128)(2,1)S(1)}, bf16[128,512]{1,0:T(8,128)(2,1)}, u32[]{:S(2)}) copy-start(bf16[128,512]{1,0:T(8,128)(2,1)} %constant.24.refs_2_.refs_4_.refs_3_) | copy-start | bytes 393220
  3.5 13.7 %copy-start.1 = (bf16[256,256]{1,0:T(8,128)(2,1)S(1)}, bf16[256,256]{1,0:T(8,128)(2,1)}, u32[]{:S(2)}) copy-start(bf16[256,256]{1,0:T(8,128)(2,1)} %constant.25.refs_3_.refs_5_.refs_4_) | copy-start | bytes 393220
  3.5 26.3 %collective-permute-start.1 = (bf16[32,32,512]{2,1,0:T(8,128)(2,1)S(1)}, bf16[32,32,512]{2,1,0:T(8,128)(2,1)S(1)}, u32[]{:S(2)}, u32[]{:S(2)}) collective-permute-start(bf16[32,32,512]{2,1,0:T(8,128)(2,1)S(1)} %get-tuple-element.45), channel_id=1, source_target_pairs={{0,2},{2,0},{1,3},{3,1},{4,6},{6,4},{5,7},{7,5},{8,10},{10,8},{9,1... | collective-permute-start | bytes 3145736 | tf_op jit(solution)/shard_map/ppermute | solution.py:461
  17.2 19.0 %copy-start.4 = (bf16[128,256]{1,0:T(8,128)(2,1)S(1)}, bf16[128,256]{1,0:T(8,128)(2,1)}, u32[]{:S(2)}) copy-start(bf16[128,256]{1,0:T(8,128)(2,1)} %constant.27.to_j_ref) | copy-start | bytes 196612
  17.2 19.0 %copy-start.6 = (bf16[32,256]{1,0:T(8,128)(2,1)S(1)}, bf16[32,256]{1,0:T(8,128)(2,1)}, u32[]{:S(2)}) copy-start(bf16[32,256]{1,0:T(8,128)(2,1)} %constant.26.to_i_ref) | copy-start | bytes 49156
  22.1 8.2 %collective-permute-start.2 = (bf16[3,16,16,128]{3,2,1,0:T(8,128)(2,1)S(1)}, bf16[3,16,16,128]{3,2,1,0:T(8,128)(2,1)S(1)}, u32[]{:S(2)}, u32[]{:S(2)}) collective-permute-start(bf16[3,16,16,128]{3,2,1,0:T(8,128)(2,1)S(1)} %get-tuple-element.46), channel_id=1, source_target_pairs={{0,4},{4,0},{8,12},{12,8},{1,5},{5,1},{9,13},{13,9},{2,6},{6,2},{1... | collective-permute-start | bytes 589832 | tf_op jit(solution)/shard_map/ppermute | solution.py:467
  30.3 6.0 %collective-permute-start.3 = (bf16[32,32,512]{2,1,0:T(8,128)(2,1)S(1)}, bf16[32,32,512]{2,1,0:T(8,128)(2,1)S(1)}, u32[]{:S(2)}, u32[]{:S(2)}) collective-permute-start(bf16[32,32,512]{2,1,0:T(8,128)(2,1)S(1)} %collective-permute-done.1.j_ref), channel_id=1, source_target_pairs={{0,1},{1,0},{2,3},{3,2},{4,5},{5,4},{6,7},{7,6},{8,9},{9,8},{10,11... | collective-permute-start | bytes 3145736 | tf_op jit(solution)/shard_map/ppermute | solution.py:464
  30.3 25.6 %collective-permute-start.4 = (bf16[32,32,512]{2,1,0:T(8,128)(2,1)S(1)}, bf16[32,32,512]{2,1,0:T(8,128)(2,1)S(1)}, u32[]{:S(2)}, u32[]{:S(2)}) collective-permute-start(bf16[32,32,512]{2,1,0:T(8,128)(2,1)S(1)} %get-tuple-element.51), channel_id=1, source_target_pairs={{0,2},{2,0},{1,3},{3,1},{4,6},{6,4},{5,7},{7,5},{8,10},{10,8},{9,1... | collective-permute-start | bytes 3145736 | tf_op jit(solution)/shard_map/ppermute | solution.py:461
  31.9 18.5 %collective-permute-start.6 = (bf16[3,16,16,128]{3,2,1,0:T(8,128)(2,1)S(1)}, bf16[3,16,16,128]{3,2,1,0:T(8,128)(2,1)S(1)}, u32[]{:S(2)}, u32[]{:S(2)}) collective-permute-start(bf16[3,16,16,128]{3,2,1,0:T(8,128)(2,1)S(1)} %get-tuple-element.55), channel_id=1, source_target_pairs={{0,4},{4,0},{8,12},{12,8},{1,5},{5,1},{9,13},{13,9},{2,6},{6,2},{1... | collective-permute-start | bytes 589832 | tf_op jit(solution)/shard_map/ppermute | solution.py:467
  33.6 16.9 %collective-permute-start.5 = (bf16[3,16,16,128]{3,2,1,0:T(8,128)(2,1)S(1)}, bf16[3,16,16,128]{3,2,1,0:T(8,128)(2,1)S(1)}, u32[]{:S(2)}, u32[]{:S(2)}) collective-permute-start(bf16[3,16,16,128]{3,2,1,0:T(8,128)(2,1)S(1)} %add_convert_fusion.2), channel_id=1, source_target_pairs={{0,8},{4,12},{8,0},{12,4},{1,9},{5,13},{9,1},{13,5},{2,10},{6,14},... | collective-permute-start | bytes 589832 | tf_op jit(solution)/shard_map/ppermute | solution.py:467
  50.4 9.3 %collective-permute-start.7 = (bf16[5,16,16,128]{3,2,1,0:T(8,128)(2,1)S(1)}, bf16[5,16,16,128]{3,2,1,0:T(8,128)(2,1)S(1)}, u32[]{:S(2)}, u32[]{:S(2)}) collective-permute-start(bf16[5,16,16,128]{3,2,1,0:T(8,128)(2,1)S(1)} %get-tuple-element.56), channel_id=1, source_target_pairs={{0,4},{4,0},{8,12},{12,8},{1,5},{5,1},{9,13},{13,9},{2,6},{6,2},{1... | collective-permute-start | bytes 983048 | tf_op jit(solution)/shard_map/ppermute | solution.py:467
  59.8 2.7 %collective-permute-start.8 = (bf16[32,32,512]{2,1,0:T(8,128)(2,1)S(1)}, bf16[32,32,512]{2,1,0:T(8,128)(2,1)S(1)}, u32[]{:S(2)}, u32[]{:S(2)}) collective-permute-start(bf16[32,32,512]{2,1,0:T(8,128)(2,1)S(1)} %collective-permute-done.4.j_ref), channel_id=1, source_target_pairs={{0,1},{1,0},{2,3},{3,2},{4,5},{5,4},{6,7},{7,6},{8,9},{9,8},{10,11... | collective-permute-start | bytes 3145736 | tf_op jit(solution)/shard_map/ppermute | solution.py:464
  59.9 18.1 %collective-permute-start.9 = (bf16[5,16,16,128]{3,2,1,0:T(8,128)(2,1)S(1)}, bf16[5,16,16,128]{3,2,1,0:T(8,128)(2,1)S(1)}, u32[]{:S(2)}, u32[]{:S(2)}) collective-permute-start(bf16[5,16,16,128]{3,2,1,0:T(8,128)(2,1)S(1)} %add_convert_fusion), channel_id=1, source_target_pairs={{0,8},{4,12},{8,0},{12,4},{1,9},{5,13},{9,1},{13,5},{2,10},{6,14},... | collective-permute-start | bytes 983048 | tf_op jit(solution)/shard_map/ppermute | solution.py:467
  60.3 14.3 %collective-permute-start.10 = (bf16[2,16,16,128]{3,2,1,0:T(8,128)(2,1)S(1)}, bf16[2,16,16,128]{3,2,1,0:T(8,128)(2,1)S(1)}, u32[]{:S(2)}, u32[]{:S(2)}) collective-permute-start(bf16[2,16,16,128]{3,2,1,0:T(8,128)(2,1)S(1)} %get-tuple-element.66), channel_id=1, source_target_pairs={{0,4},{4,0},{8,12},{12,8},{1,5},{5,1},{9,13},{13,9},{2,6},{6,2},{1... | collective-permute-start | bytes 393224 | tf_op jit(solution)/shard_map/ppermute | solution.py:467
  74.0 9.4 %collective-permute-start.11 = (bf16[4,16,16,128]{3,2,1,0:T(8,128)(2,1)S(1)}, bf16[4,16,16,128]{3,2,1,0:T(8,128)(2,1)S(1)}, u32[]{:S(2)}, u32[]{:S(2)}) collective-permute-start(bf16[4,16,16,128]{3,2,1,0:T(8,128)(2,1)S(1)} %get-tuple-element.65), channel_id=1, source_target_pairs={{0,4},{4,0},{8,12},{12,8},{1,5},{5,1},{9,13},{13,9},{2,6},{6,2},{1... | collective-permute-start | bytes 786440 | tf_op jit(solution)/shard_map/ppermute | solution.py:467
  82.0 11.4 %collective-permute-start.12 = (bf16[4,16,16,128]{3,2,1,0:T(8,128)(2,1)S(1)}, bf16[4,16,16,128]{3,2,1,0:T(8,128)(2,1)S(1)}, u32[]{:S(2)}, u32[]{:S(2)}) collective-permute-start(bf16[4,16,16,128]{3,2,1,0:T(8,128)(2,1)S(1)} %pad_maximum_fusion), channel_id=1, source_target_pairs={{0,4},{4,0},{8,12},{12,8},{1,5},{5,1},{9,13},{13,9},{2,6},{6,2},{1... | collective-permute-start | bytes 786440 | tf_op jit(solution)/shard_map/ppermute | solution.py:467
  83.6 16.5 %collective-permute-start.14 = (bf16[4,16,16,128]{3,2,1,0:T(8,128)(2,1)S(1)}, bf16[4,16,16,128]{3,2,1,0:T(8,128)(2,1)S(1)}, u32[]{:S(2)}, u32[]{:S(2)}) collective-permute-start(bf16[4,16,16,128]{3,2,1,0:T(8,128)(2,1)S(1)} %add_convert_fusion.1), channel_id=1, source_target_pairs={{0,8},{4,12},{8,0},{12,4},{1,9},{5,13},{9,1},{13,5},{2,10},{6,14},... | collective-permute-start | bytes 786440 | tf_op jit(solution)/shard_map/ppermute | solution.py:467
  87.7 12.4 %collective-permute-start.13 = (bf16[3,16,16,128]{3,2,1,0:T(8,128)(2,1)S(1)}, bf16[3,16,16,128]{3,2,1,0:T(8,128)(2,1)S(1)}, u32[]{:S(2)}, u32[]{:S(2)}) collective-permute-start(bf16[3,16,16,128]{3,2,1,0:T(8,128)(2,1)S(1)} %get-tuple-element.75), channel_id=1, source_target_pairs={{0,4},{4,0},{8,12},{12,8},{1,5},{5,1},{9,13},{13,9},{2,6},{6,2},{1... | collective-permute-start | bytes 589832 | tf_op jit(solution)/shard_map/ppermute | solution.py:467

commit v5 on v4

--- a/solution.py
+++ b/solution.py
@@ -177,7 +177,7 @@
     line = depth // folded
     pitch = line + 1
     per_step = 2 * folded
-    batch = 16
+    batch = 32
 
     def kernel(j_ref, i_ref, table_ref, to_i_ref, to_j_ref, i_out, j_out, wide):
         same = lax.axis_index("sub") == lax.axis_index("rep")
@@ -204,7 +204,7 @@
                     ]
 
         groups = wins // per_step
-        at_once = 4
+        at_once = 8
 
         def some_windows(step, carry):
             first = step * at_once
@@ -268,7 +268,7 @@
     bins, depth, _ = right_arrays[0].shape
     piece = HALF // BLOCKS
     pitch = bins + 1
-    step_bins = 32
+    step_bins = 128
     groups = []
     slices = {}
     for used, groups_here in jobs:

time: 102 us -> 99.3 us (0.974)
  Pallas kernels: 52 us -> 46 us
  waiting for transfers between devices: 31.9 us -> 34.9 us
    pallas_call x5, Pallas kernels: 26.8 us -> 22.8 us  [partial_correlations(): kernel_call(kernel, 'partial_correlations', 4 * total * bins * depth * LA...]
    ppermute x2, waiting for transfers between devices: 9.61 us -> 12.4 us  [over_sub(): return lax.ppermute(rows, 'sub', [(0, 1), (1, 0)])]
    pallas_call x3, Pallas kernels: 21.7 us -> 19.7 us  [spectra(): kernel_call(kernel, 'spectra', 4 * samples * samples * wins * given, 4 *...]
  transfers between devices with their start and end apart: 15 -> 15, of which waited for: 10 -> 9; matrix products, arithmetic and copies ran while one was open for 0% -> 0% of each run, Pallas kernels for 48% -> 43%
where the time goes in v5:
time: 99.3 us; the launch traced here: 99.1 us
  Pallas kernels  46 us (46%)
  waiting for transfers between devices  34.9 us (35%)
  starting transfers between devices  17 us (17%)
    pallas_call x5, Pallas kernels, partial_correlations(): kernel_call(kernel, 'partial_correlations', 4 * total * bins * depth * LA...  22.8 us
    ppermute x10, waiting for transfers between devices, with_device(): lax.ppermute(share, 'chan', [(z, z ^ apart) for z in range(chan_count)])  20.5 us
    pallas_call x3, Pallas kernels, spectra(): kernel_call(kernel, 'spectra', 4 * samples * samples * wins * given, 4 *...  19.7 us
    ppermute x2, waiting for transfers between devices, over_sub(): return lax.ppermute(rows, 'sub', [(0, 1), (1, 0)])  12.4 us
    ppermute x10, starting transfers between devices, with_device(): lax.ppermute(share, 'chan', [(z, z ^ apart) for z in range(chan_count)])  12.1 us
    ppermute x2, starting transfers between devices, over_sub(): return lax.ppermute(rows, 'sub', [(0, 1), (1, 0)])  4.35 us
    pallas_call x1, Pallas kernels, order_rows(): kernel_call(kernel, 'order_rows', 0, 3 * traces.size * 2, vmem_bytes=ORDE...  2.28 us
  transfers between devices with their start and end apart: 15, of which 9 were waited for; matrix products, arithmetic and copies ran while one was open for 0% of the time, Pallas kernels for 43%

profile of v5, /device:TPU:0, one launch (start us, length us, event | category | flops | bytes accessed | tf_op | source)
XLA Modules:
  0.0 99.1 jit_solution(9951136233118309189)
XLA Ops:
  0.7 2.3 %order_rows.1 = (bf16[32,64,512]{2,1,0:T(8,128)(2,1)S(1)}, bf16[32,32,512]{2,1,0:T(8,128)(2,1)S(1)}, bf16[32,32,512]{2,1,0:T(8,128)(2,1)S(1)}) custom-call(s32[64]{0:T(128)S(1)} %copy-done.2, bf16[64,32,512]{2,1,0:T(8,128)(2,1)} %traces_ref.1), custom_call_target="tpu_custom_call" | custom-call | bytes 6291456 | tf_op jit(solution)/shard_map/order_rows/pallas_call | solution.py:147
  3.5 2.6 %collective-permute-start.1 = (bf16[32,32,512]{2,1,0:T(8,128)(2,1)S(1)}, bf16[32,32,512]{2,1,0:T(8,128)(2,1)S(1)}, u32[]{:S(2)}, u32[]{:S(2)}) collective-permute-start(bf16[32,32,512]{2,1,0:T(8,128)(2,1)S(1)} %get-tuple-element.45), channel_id=1, source_target_pairs={{0,2},{2,0},{1,3},{3,1},{4,6},{6,4},{5,7},{7,5},{8,10},{10,8},{9,1... | collective-permute-start | bytes 3145736 | tf_op jit(solution)/shard_map/ppermute | solution.py:461
  7.3 9.3 %spectra.3 = (bf16[256,32,128]{2,1,0:T(8,128)(2,1)S(1)}, bf16[256,64,128]{2,1,0:T(8,128)(2,1)S(1)}) custom-call(bf16[32,64,512]{2,1,0:T(8,128)(2,1)S(1)} %get-tuple-element.41.j_ref, bf16[32,64,512]{2,1,0:T(8,128)(2,1)S(1)} %collective-permute-done.i_ref, bf16[512,512]{1,0:T(8,128)(2,1)S(1)} %copy-done.3, bf16[32,256]{1,0:T(8,128)(2,1)S(1)} %copy-done.7, ...), custom_call_target="tpu_custom_call" | custom-call | flops 2147483648 | bytes 8388608 | tf_op jit(solution)/shard_map/spectra/pallas_call | solution.py:253
  16.6 4.0 %partial_correlations.5 = (bf16[3,16,16,128]{3,2,1,0:T(8,128)(2,1)S(1)}, bf16[3,16,16,128]{3,2,1,0:T(8,128)(2,1)S(1)}, f32[3,16,16,128]{3,2,1,0:T(8,128)S(1)}, bf16[3,16,16,128]{3,2,1,0:T(8,128)(2,1)S(1)}) custom-call(bf16[256,32,128]{2,1,0:T(8,128)(2,1)S(1)} %get-tuple-element.42.refs_0_, bf16[256,64,128]{2,1,0:T(8,128)(2,1)S(1)} %get-tuple-element.43.refs_1_.refs_2_, ...), custom_call_target="tpu_custom_call" | custom-call | flops 805306368 | bytes 6291456 | tf_op jit(solution)/shard_map/partial_correlations/pallas_call | solution.py:394
  20.5 3.0 %collective-permute-start.2 = (bf16[3,16,16,128]{3,2,1,0:T(8,128)(2,1)S(1)}, bf16[3,16,16,128]{3,2,1,0:T(8,128)(2,1)S(1)}, u32[]{:S(2)}, u32[]{:S(2)}) collective-permute-start(bf16[3,16,16,128]{3,2,1,0:T(8,128)(2,1)S(1)} %get-tuple-element.46), channel_id=1, source_target_pairs={{0,4},{4,0},{8,12},{12,8},{1,5},{5,1},{9,13},{13,9},{2,6},{6,2},{1... | collective-permute-start | bytes 589832 | tf_op jit(solution)/shard_map/ppermute | solution.py:467
  23.6 6.2 %collective-permute-done.1.j_ref = bf16[32,32,512]{2,1,0:T(8,128)(2,1)S(1)} collective-permute-done((bf16[32,32,512]{2,1,0:T(8,128)(2,1)S(1)}, bf16[32,32,512]{2,1,0:T(8,128)(2,1)S(1)}, u32[]{:S(2)}, u32[]{:S(2)}) %collective-permute-start.1) | collective-permute-done | bytes 1048608 | tf_op jit(solution)/shard_map/ppermute | solution.py:461
  29.8 1.8 %collective-permute-start.4 = (bf16[32,32,512]{2,1,0:T(8,128)(2,1)S(1)}, bf16[32,32,512]{2,1,0:T(8,128)(2,1)S(1)}, u32[]{:S(2)}, u32[]{:S(2)}) collective-permute-start(bf16[32,32,512]{2,1,0:T(8,128)(2,1)S(1)} %get-tuple-element.51), channel_id=1, source_target_pairs={{0,2},{2,0},{1,3},{3,1},{4,6},{6,4},{5,7},{7,5},{8,10},{10,8},{9,1... | collective-permute-start | bytes 3145736 | tf_op jit(solution)/shard_map/ppermute | solution.py:461
  31.6 1.6 %collective-permute-start.6 = (bf16[3,16,16,128]{3,2,1,0:T(8,128)(2,1)S(1)}, bf16[3,16,16,128]{3,2,1,0:T(8,128)(2,1)S(1)}, u32[]{:S(2)}, u32[]{:S(2)}) collective-permute-start(bf16[3,16,16,128]{3,2,1,0:T(8,128)(2,1)S(1)} %get-tuple-element.55), channel_id=1, source_target_pairs={{0,4},{4,0},{8,12},{12,8},{1,5},{5,1},{9,13},{13,9},{2,6},{6,2},{1... | collective-permute-start | bytes 589832 | tf_op jit(solution)/shard_map/ppermute | solution.py:467
  33.2 2.7 %collective-permute-start.5 = (bf16[3,16,16,128]{3,2,1,0:T(8,128)(2,1)S(1)}, bf16[3,16,16,128]{3,2,1,0:T(8,128)(2,1)S(1)}, u32[]{:S(2)}, u32[]{:S(2)}) collective-permute-start(bf16[3,16,16,128]{3,2,1,0:T(8,128)(2,1)S(1)} %add_convert_fusion.2), channel_id=1, source_target_pairs={{0,8},{4,12},{8,0},{12,4},{1,9},{5,13},{9,1},{13,5},{2,10},{6,14},... | collective-permute-start | bytes 589832 | tf_op jit(solution)/shard_map/ppermute | solution.py:467
  35.9 5.2 %spectra.4 = (bf16[256,16,128]{2,1,0:T(8,128)(2,1)S(1)}, bf16[256,64,128]{2,1,0:T(8,128)(2,1)S(1)}) custom-call(bf16[32,32,512]{2,1,0:T(8,128)(2,1)S(1)} %collective-permute-done.1.j_ref, bf16[32,32,512]{2,1,0:T(8,128)(2,1)S(1)} %collective-permute-done.3.i_ref, bf16[512,512]{1,0:T(8,128)(2,1)S(1)} %copy-done.3, bf16[32,256]{1,0:T(8,128)(2,1)S(1)} %copy-done.6, ...), custom_call_target="tpu_custom_call" | custom-call | flops 1073741824 | bytes 4194304 | tf_op jit(solution)/shard_map/spectra/pallas_call | solution.py:253
  41.1 7.6 %partial_correlations.6 = (bf16[5,16,16,128]{3,2,1,0:T(8,128)(2,1)S(1)}, bf16[5,16,16,128]{3,2,1,0:T(8,128)(2,1)S(1)}, f32[2,16,16,128]{3,2,1,0:T(8,128)S(1)}, bf16[2,16,16,128]{3,2,1,0:T(8,128)(2,1)S(1)}) custom-call(bf16[256,32,128]{2,1,0:T(8,128)(2,1)S(1)} %get-tuple-element.42.refs_0_, bf16[256,16,128]{2,1,0:T(8,128)(2,1)S(1)} %get-tuple-element.48.refs_1_, ...), custom_call_target="tpu_custom_call" | custom-call | flops 1610612736 | bytes 11534336 | tf_op jit(solution)/shard_map/partial_correlations/pallas_call | solution.py:394
  49.2 6.1 %collective-permute-done.4.j_ref = bf16[32,32,512]{2,1,0:T(8,128)(2,1)S(1)} collective-permute-done((bf16[32,32,512]{2,1,0:T(8,128)(2,1)S(1)}, bf16[32,32,512]{2,1,0:T(8,128)(2,1)S(1)}, u32[]{:S(2)}, u32[]{:S(2)}) %collective-permute-start.4) | collective-permute-done | bytes 1048608 | tf_op jit(solution)/shard_map/ppermute | solution.py:461
  55.4 2.7 %collective-permute-done.7 = bf16[5,16,16,128]{3,2,1,0:T(8,128)(2,1)S(1)} collective-permute-done((bf16[5,16,16,128]{3,2,1,0:T(8,128)(2,1)S(1)}, bf16[5,16,16,128]{3,2,1,0:T(8,128)(2,1)S(1)}, u32[]{:S(2)}, u32[]{:S(2)}) %collective-permute-start.7) | collective-permute-done | bytes 327712 | tf_op jit(solution)/shard_map/ppermute | solution.py:467
  58.6 1.4 %collective-permute-start.10 = (bf16[2,16,16,128]{3,2,1,0:T(8,128)(2,1)S(1)}, bf16[2,16,16,128]{3,2,1,0:T(8,128)(2,1)S(1)}, u32[]{:S(2)}, u32[]{:S(2)}) collective-permute-start(bf16[2,16,16,128]{3,2,1,0:T(8,128)(2,1)S(1)} %get-tuple-element.66), channel_id=1, source_target_pairs={{0,4},{4,0},{8,12},{12,8},{1,5},{5,1},{9,13},{13,9},{2,6},{6,2},{1... | collective-permute-start | bytes 393224 | tf_op jit(solution)/shard_map/ppermute | solution.py:467
  60.7 5.2 %spectra.5 = (bf16[256,16,128]{2,1,0:T(8,128)(2,1)S(1)}, bf16[256,64,128]{2,1,0:T(8,128)(2,1)S(1)}) custom-call(bf16[32,32,512]{2,1,0:T(8,128)(2,1)S(1)} %collective-permute-done.4.j_ref, bf16[32,32,512]{2,1,0:T(8,128)(2,1)S(1)} %collective-permute-done.8.i_ref, bf16[512,512]{1,0:T(8,128)(2,1)S(1)} %copy-done.3, bf16[32,256]{1,0:T(8,128)(2,1)S(1)} %copy-done.6, ...), custom_call_target="tpu_custom_call" | custom-call | flops 1073741824 | bytes 4194304 | tf_op jit(solution)/shard_map/spectra/pallas_call | solution.py:253
  65.9 4.7 %partial_correlations.7 = (bf16[4,16,16,128]{3,2,1,0:T(8,128)(2,1)S(1)}, bf16[4,16,16,128]{3,2,1,0:T(8,128)(2,1)S(1)}, f32[1,16,16,128]{3,2,1,0:T(8,128)S(1)}, bf16[1,16,16,128]{3,2,1,0:T(8,128)(2,1)S(1)}) custom-call(bf16[256,32,128]{2,1,0:T(8,128)(2,1)S(1)} %get-tuple-element.42.refs_0_, bf16[256,16,128]{2,1,0:T(8,128)(2,1)S(1)} %get-tuple-element.48.refs_1_, ...), custom_call_target="tpu_custom_call" | custom-call | flops 1207959552 | bytes 7340032 | tf_op jit(solution)/shard_map/partial_correlations/pallas_call | solution.py:394
  71.2 5.1 %collective-permute-done.9.refs_10_ = bf16[5,16,16,128]{3,2,1,0:T(8,128)(2,1)S(1)} collective-permute-done((bf16[5,16,16,128]{3,2,1,0:T(8,128)(2,1)S(1)}, bf16[5,16,16,128]{3,2,1,0:T(8,128)(2,1)S(1)}, u32[]{:S(2)}, u32[]{:S(2)}) %collective-permute-start.9) | collective-permute-done | bytes 327712 | tf_op jit(solution)/shard_map/ppermute | solution.py:467
  76.3 3.3 %partial_correlations.8 = (f32[3,16,16,128]{3,2,1,0:T(8,128)S(1)}, bf16[3,16,16,128]{3,2,1,0:T(8,128)(2,1)S(1)}) custom-call(bf16[256,16,128]{2,1,0:T(8,128)(2,1)S(1)} %get-tuple-element.71.refs_0_, bf16[256,64,128]{2,1,0:T(8,128)(2,1)S(1)} %get-tuple-element.49.refs_3_.refs_1_, bf16[256,64,128]{2,1,0:T(8,128)(2,1)S(1)} %get-tuple-element.67.refs_2_, ...), custom_call_target="tpu_custom_call" | custom-call | flops 402653184 | bytes 9437184 | tf_op jit(solution)/shard_map/partial_correlations/pallas_call | solution.py:394
  79.7 2.1 %collective-permute-done.11 = bf16[4,16,16,128]{3,2,1,0:T(8,128)(2,1)S(1)} collective-permute-done((bf16[4,16,16,128]{3,2,1,0:T(8,128)(2,1)S(1)}, bf16[4,16,16,128]{3,2,1,0:T(8,128)(2,1)S(1)}, u32[]{:S(2)}, u32[]{:S(2)}) %collective-permute-start.11) | collective-permute-done | bytes 262176 | tf_op jit(solution)/shard_map/ppermute | solution.py:467
  81.9 3.3 %partial_correlations.9 = (f32[3,16,16,128]{3,2,1,0:T(8,128)S(1)}, bf16[3,16,16,128]{3,2,1,0:T(8,128)(2,1)S(1)}) custom-call(bf16[256,16,128]{2,1,0:T(8,128)(2,1)S(1)} %get-tuple-element.71.refs_0_, bf16[256,64,128]{2,1,0:T(8,128)(2,1)S(1)} %get-tuple-element.43.refs_1_.refs_2_, bf16[128,512]{1,0:T(8,128)(2,1)S(1)} %copy-done, bf16[256,256]{1,0:T(8,128)(2,1)S(1)} %copy-done.1), custom_call_target="tpu_custom_call" | custom-call | flops 402653184 | bytes 5242880 | tf_op jit(solution)/shard_map/partial_correlations/pallas_call | solution.py:394
  85.2 1.9 %collective-permute-start.13 = (bf16[3,16,16,128]{3,2,1,0:T(8,128)(2,1)S(1)}, bf16[3,16,16,128]{3,2,1,0:T(8,128)(2,1)S(1)}, u32[]{:S(2)}, u32[]{:S(2)}) collective-permute-start(bf16[3,16,16,128]{3,2,1,0:T(8,128)(2,1)S(1)} %get-tuple-element.75), channel_id=1, source_target_pairs={{0,4},{4,0},{8,12},{12,8},{1,5},{5,1},{9,13},{13,9},{2,6},{6,2},{1... | collective-permute-start | bytes 589832 | tf_op jit(solution)/shard_map/ppermute | solution.py:467
  87.1 3.6 %collective-permute-done.12.refs_7_ = bf16[4,16,16,128]{3,2,1,0:T(8,128)(2,1)S(1)} collective-permute-done((bf16[4,16,16,128]{3,2,1,0:T(8,128)(2,1)S(1)}, bf16[4,16,16,128]{3,2,1,0:T(8,128)(2,1)S(1)}, u32[]{:S(2)}, u32[]{:S(2)}) %collective-permute-start.12) | collective-permute-done | bytes 262176 | tf_op jit(solution)/shard_map/ppermute | solution.py:467
  90.7 7.0 %collective-permute-done.13.refs_8_ = bf16[3,16,16,128]{3,2,1,0:T(8,128)(2,1)S(1)} collective-permute-done((bf16[3,16,16,128]{3,2,1,0:T(8,128)(2,1)S(1)}, bf16[3,16,16,128]{3,2,1,0:T(8,128)(2,1)S(1)}, u32[]{:S(2)}, u32[]{:S(2)}) %collective-permute-start.13) | collective-permute-done | bytes 196640 | tf_op jit(solution)/shard_map/ppermute | solution.py:467
  97.7 1.2 %assembled.1 = f32[3,1,32,32,128]{4,3,2,1,0:T(8,128)} custom-call(f32[3,16,16,128]{3,2,1,0:T(8,128)S(1)} %get-tuple-element.44.refs_0_, f32[2,16,16,128]{3,2,1,0:T(8,128)S(1)} %get-tuple-element.50.refs_1_, f32[1,16,16,128]{3,2,1,0:T(8,128)S(1)} %get-tuple-element.62.refs_2_, f32[3,16,16,128]{3,2,1,0:T(8,128)S(1)} %get-tuple-element.68.refs_3_, ...), custom_call_target="tpu_custom_call" | custom-call | bytes 2359296 | tf_op jit(solution)/shard_map/assembled/pallas_call | solution.py:438
  (36 shorter events, 5.0 us)
Async XLA Ops:
  0.0 0.7 copy-start.2
  0.7 6.6 %copy-start.3 = (bf16[512,512]{1,0:T(8,128)(2,1)S(1)}, bf16[512,512]{1,0:T(8,128)(2,1)}, u32[]{:S(2)}) copy-start(bf16[512,512]{1,0:T(8,128)(2,1)} %constant.21.table_ref) | copy-start | bytes 1572868
  0.7 6.6 %copy-start.5 = (bf16[128,128]{1,0:T(8,128)(2,1)S(1)}, bf16[128,128]{1,0:T(8,128)(2,1)}, u32[]{:S(2)}) copy-start(bf16[128,128]{1,0:T(8,128)(2,1)} %constant.23.to_j_ref) | copy-start | bytes 98308
  0.7 6.6 %copy-start.7 = (bf16[32,256]{1,0:T(8,128)(2,1)S(1)}, bf16[32,256]{1,0:T(8,128)(2,1)}, u32[]{:S(2)}) copy-start(bf16[32,256]{1,0:T(8,128)(2,1)} %constant.22.to_i_ref) | copy-start | bytes 49156
  2.9 4.3 %collective-permute-start = (bf16[32,64,512]{2,1,0:T(8,128)(2,1)S(1)}, bf16[32,64,512]{2,1,0:T(8,128)(2,1)S(1)}, u32[]{:S(2)}, u32[]{:S(2)}) collective-permute-start(bf16[32,64,512]{2,1,0:T(8,128)(2,1)S(1)} %get-tuple-element.41.j_ref), channel_id=1, source_target_pairs={{0,1},{1,0},{2,3},{3,2},{4,5},{5,4},{6,7},{7,6},{8,9},{9,8},{10,11... | collective-permute-start | bytes 6291464 | tf_op jit(solution)/shard_map/ppermute | solution.py:464
  3.5 13.1 %copy-start = (bf16[128,512]{1,0:T(8,128)(2,1)S(1)}, bf16[128,512]{1,0:T(8,128)(2,1)}, u32[]{:S(2)}) copy-start(bf16[128,512]{1,0:T(8,128)(2,1)} %constant.24.refs_2_.refs_4_.refs_3_) | copy-start | bytes 393220
  3.5 13.1 %copy-start.1 = (bf16[256,256]{1,0:T(8,128)(2,1)S(1)}, bf16[256,256]{1,0:T(8,128)(2,1)}, u32[]{:S(2)}) copy-start(bf16[256,256]{1,0:T(8,128)(2,1)} %constant.25.refs_3_.refs_5_.refs_4_) | copy-start | bytes 393220
  3.5 26.3 %collective-permute-start.1 = (bf16[32,32,512]{2,1,0:T(8,128)(2,1)S(1)}, bf16[32,32,512]{2,1,0:T(8,128)(2,1)S(1)}, u32[]{:S(2)}, u32[]{:S(2)}) collective-permute-start(bf16[32,32,512]{2,1,0:T(8,128)(2,1)S(1)} %get-tuple-element.45), channel_id=1, source_target_pairs={{0,2},{2,0},{1,3},{3,1},{4,6},{6,4},{5,7},{7,5},{8,10},{10,8},{9,1... | collective-permute-start | bytes 3145736 | tf_op jit(solution)/shard_map/ppermute | solution.py:461
  16.5 19.3 %copy-start.4 = (bf16[128,256]{1,0:T(8,128)(2,1)S(1)}, bf16[128,256]{1,0:T(8,128)(2,1)}, u32[]{:S(2)}) copy-start(bf16[128,256]{1,0:T(8,128)(2,1)} %constant.27.to_j_ref) | copy-start | bytes 196612
  16.6 19.3 %copy-start.6 = (bf16[32,256]{1,0:T(8,128)(2,1)S(1)}, bf16[32,256]{1,0:T(8,128)(2,1)}, u32[]{:S(2)}) copy-start(bf16[32,256]{1,0:T(8,128)(2,1)} %constant.26.to_i_ref) | copy-start | bytes 49156
  20.5 9.2 %collective-permute-start.2 = (bf16[3,16,16,128]{3,2,1,0:T(8,128)(2,1)S(1)}, bf16[3,16,16,128]{3,2,1,0:T(8,128)(2,1)S(1)}, u32[]{:S(2)}, u32[]{:S(2)}) collective-permute-start(bf16[3,16,16,128]{3,2,1,0:T(8,128)(2,1)S(1)} %get-tuple-element.46), channel_id=1, source_target_pairs={{0,4},{4,0},{8,12},{12,8},{1,5},{5,1},{9,13},{13,9},{2,6},{6,2},{1... | collective-permute-start | bytes 589832 | tf_op jit(solution)/shard_map/ppermute | solution.py:467
  29.8 6.1 %collective-permute-start.3 = (bf16[32,32,512]{2,1,0:T(8,128)(2,1)S(1)}, bf16[32,32,512]{2,1,0:T(8,128)(2,1)S(1)}, u32[]{:S(2)}, u32[]{:S(2)}) collective-permute-start(bf16[32,32,512]{2,1,0:T(8,128)(2,1)S(1)} %collective-permute-done.1.j_ref), channel_id=1, source_target_pairs={{0,1},{1,0},{2,3},{3,2},{4,5},{5,4},{6,7},{7,6},{8,9},{9,8},{10,11... | collective-permute-start | bytes 3145736 | tf_op jit(solution)/shard_map/ppermute | solution.py:464
  29.8 25.6 %collective-permute-start.4 = (bf16[32,32,512]{2,1,0:T(8,128)(2,1)S(1)}, bf16[32,32,512]{2,1,0:T(8,128)(2,1)S(1)}, u32[]{:S(2)}, u32[]{:S(2)}) collective-permute-start(bf16[32,32,512]{2,1,0:T(8,128)(2,1)S(1)} %get-tuple-element.51), channel_id=1, source_target_pairs={{0,2},{2,0},{1,3},{3,1},{4,6},{6,4},{5,7},{7,5},{8,10},{10,8},{9,1... | collective-permute-start | bytes 3145736 | tf_op jit(solution)/shard_map/ppermute | solution.py:461
  31.6 17.2 %collective-permute-start.6 = (bf16[3,16,16,128]{3,2,1,0:T(8,128)(2,1)S(1)}, bf16[3,16,16,128]{3,2,1,0:T(8,128)(2,1)S(1)}, u32[]{:S(2)}, u32[]{:S(2)}) collective-permute-start(bf16[3,16,16,128]{3,2,1,0:T(8,128)(2,1)S(1)} %get-tuple-element.55), channel_id=1, source_target_pairs={{0,4},{4,0},{8,12},{12,8},{1,5},{5,1},{9,13},{13,9},{2,6},{6,2},{1... | collective-permute-start | bytes 589832 | tf_op jit(solution)/shard_map/ppermute | solution.py:467
  33.2 15.5 %collective-permute-start.5 = (bf16[3,16,16,128]{3,2,1,0:T(8,128)(2,1)S(1)}, bf16[3,16,16,128]{3,2,1,0:T(8,128)(2,1)S(1)}, u32[]{:S(2)}, u32[]{:S(2)}) collective-permute-start(bf16[3,16,16,128]{3,2,1,0:T(8,128)(2,1)S(1)} %add_convert_fusion.2), channel_id=1, source_target_pairs={{0,8},{4,12},{8,0},{12,4},{1,9},{5,13},{9,1},{13,5},{2,10},{6,14},... | collective-permute-start | bytes 589832 | tf_op jit(solution)/shard_map/ppermute | solution.py:467
  48.7 9.3 %collective-permute-start.7 = (bf16[5,16,16,128]{3,2,1,0:T(8,128)(2,1)S(1)}, bf16[5,16,16,128]{3,2,1,0:T(8,128)(2,1)S(1)}, u32[]{:S(2)}, u32[]{:S(2)}) collective-permute-start(bf16[5,16,16,128]{3,2,1,0:T(8,128)(2,1)S(1)} %get-tuple-element.56), channel_id=1, source_target_pairs={{0,4},{4,0},{8,12},{12,8},{1,5},{5,1},{9,13},{13,9},{2,6},{6,2},{1... | collective-permute-start | bytes 983048 | tf_op jit(solution)/shard_map/ppermute | solution.py:467
  58.1 2.7 %collective-permute-start.8 = (bf16[32,32,512]{2,1,0:T(8,128)(2,1)S(1)}, bf16[32,32,512]{2,1,0:T(8,128)(2,1)S(1)}, u32[]{:S(2)}, u32[]{:S(2)}) collective-permute-start(bf16[32,32,512]{2,1,0:T(8,128)(2,1)S(1)} %collective-permute-done.4.j_ref), channel_id=1, source_target_pairs={{0,1},{1,0},{2,3},{3,2},{4,5},{5,4},{6,7},{7,6},{8,9},{9,8},{10,11... | collective-permute-start | bytes 3145736 | tf_op jit(solution)/shard_map/ppermute | solution.py:464
  58.2 18.1 %collective-permute-start.9 = (bf16[5,16,16,128]{3,2,1,0:T(8,128)(2,1)S(1)}, bf16[5,16,16,128]{3,2,1,0:T(8,128)(2,1)S(1)}, u32[]{:S(2)}, u32[]{:S(2)}) collective-permute-start(bf16[5,16,16,128]{3,2,1,0:T(8,128)(2,1)S(1)} %add_convert_fusion), channel_id=1, source_target_pairs={{0,8},{4,12},{8,0},{12,4},{1,9},{5,13},{9,1},{13,5},{2,10},{6,14},... | collective-permute-start | bytes 983048 | tf_op jit(solution)/shard_map/ppermute | solution.py:467
  58.6 12.6 %collective-permute-start.10 = (bf16[2,16,16,128]{3,2,1,0:T(8,128)(2,1)S(1)}, bf16[2,16,16,128]{3,2,1,0:T(8,128)(2,1)S(1)}, u32[]{:S(2)}, u32[]{:S(2)}) collective-permute-start(bf16[2,16,16,128]{3,2,1,0:T(8,128)(2,1)S(1)} %get-tuple-element.66), channel_id=1, source_target_pairs={{0,4},{4,0},{8,12},{12,8},{1,5},{5,1},{9,13},{13,9},{2,6},{6,2},{1... | collective-permute-start | bytes 393224 | tf_op jit(solution)/shard_map/ppermute | solution.py:467
  70.6 11.2 %collective-permute-start.11 = (bf16[4,16,16,128]{3,2,1,0:T(8,128)(2,1)S(1)}, bf16[4,16,16,128]{3,2,1,0:T(8,128)(2,1)S(1)}, u32[]{:S(2)}, u32[]{:S(2)}) collective-permute-start(bf16[4,16,16,128]{3,2,1,0:T(8,128)(2,1)S(1)} %get-tuple-element.65), channel_id=1, source_target_pairs={{0,4},{4,0},{8,12},{12,8},{1,5},{5,1},{9,13},{13,9},{2,6},{6,2},{1... | collective-permute-start | bytes 786440 | tf_op jit(solution)/shard_map/ppermute | solution.py:467
  79.6 11.1 %collective-permute-start.12 = (bf16[4,16,16,128]{3,2,1,0:T(8,128)(2,1)S(1)}, bf16[4,16,16,128]{3,2,1,0:T(8,128)(2,1)S(1)}, u32[]{:S(2)}, u32[]{:S(2)}) collective-permute-start(bf16[4,16,16,128]{3,2,1,0:T(8,128)(2,1)S(1)} %pad_maximum_fusion), channel_id=1, source_target_pairs={{0,4},{4,0},{8,12},{12,8},{1,5},{5,1},{9,13},{13,9},{2,6},{6,2},{1... | collective-permute-start | bytes 786440 | tf_op jit(solution)/shard_map/ppermute | solution.py:467
  81.9 15.8 %collective-permute-start.14 = (bf16[4,16,16,128]{3,2,1,0:T(8,128)(2,1)S(1)}, bf16[4,16,16,128]{3,2,1,0:T(8,128)(2,1)S(1)}, u32[]{:S(2)}, u32[]{:S(2)}) collective-permute-start(bf16[4,16,16,128]{3,2,1,0:T(8,128)(2,1)S(1)} %add_convert_fusion.1), channel_id=1, source_target_pairs={{0,8},{4,12},{8,0},{12,4},{1,9},{5,13},{9,1},{13,5},{2,10},{6,14},... | collective-permute-start | bytes 786440 | tf_op jit(solution)/shard_map/ppermute | solution.py:467
  85.2 12.5 %collective-permute-start.13 = (bf16[3,16,16,128]{3,2,1,0:T(8,128)(2,1)S(1)}, bf16[3,16,16,128]{3,2,1,0:T(8,128)(2,1)S(1)}, u32[]{:S(2)}, u32[]{:S(2)}) collective-permute-start(bf16[3,16,16,128]{3,2,1,0:T(8,128)(2,1)S(1)} %get-tuple-element.75), channel_id=1, source_target_pairs={{0,4},{4,0},{8,12},{12,8},{1,5},{5,1},{9,13},{13,9},{2,6},{6,2},{1... | collective-permute-start | bytes 589832 | tf_op jit(solution)/shard_map/ppermute | solution.py:467

commit v6 on v5

--- a/solution.py
+++ b/solution.py
@@ -86,7 +86,7 @@
     piece = rows // BLOCKS
     step_wins = 16
     steps = wins // step_wins
-    batch = 4
+    batch = 8
     used = max(kinds, key=len)
     pitch = len(used) * piece + 1
 
@@ -138,7 +138,7 @@
                         ]
                 return carry
 
-            lax.fori_loop(0, step_wins, pack, 0, unroll=2)
+            lax.fori_loop(0, step_wins, pack, 0, unroll=4)
 
         for step in range(steps):
             copies[step].wait()
@@ -268,7 +268,7 @@
     bins, depth, _ = right_arrays[0].shape
     piece = HALF // BLOCKS
     pitch = bins + 1
-    step_bins = 128
+    step_bins = 256
     groups = []
     slices = {}
     for used, groups_here in jobs:

time: 99.3 us -> 98.8 us (level)
    pallas_call x5, Pallas kernels: 22.8 us -> 21.8 us  [partial_correlations(): kernel_call(kernel, 'partial_correlations', 4 * total * bins * depth * LA...]
  transfers between devices with their start and end apart: 15 -> 15, of which waited for: 9 -> 9; matrix products, arithmetic and copies ran while one was open for 0% -> 0% of each run, Pallas kernels for 43% -> 42%
where the time goes in v6:
time: 98.8 us; the launch traced here: 98.6 us
  Pallas kernels  45.2 us (46%)
  waiting for transfers between devices  34.9 us (35%)
  starting transfers between devices  17.2 us (17%)
    pallas_call x5, Pallas kernels, partial_correlations(): kernel_call(kernel, 'partial_correlations', 4 * total * bins * depth * LA...  21.8 us
    ppermute x10, waiting for transfers between devices, with_device(): lax.ppermute(share, 'chan', [(z, z ^ apart) for z in range(chan_count)])  20.5 us
    pallas_call x3, Pallas kernels, spectra(): kernel_call(kernel, 'spectra', 4 * samples * samples * wins * given, 4 *...  20 us
    ppermute x2, waiting for transfers between devices, over_sub(): return lax.ppermute(rows, 'sub', [(0, 1), (1, 0)])  12.7 us
    ppermute x10, starting transfers between devices, with_device(): lax.ppermute(share, 'chan', [(z, z ^ apart) for z in range(chan_count)])  12.4 us
    ppermute x2, starting transfers between devices, over_sub(): return lax.ppermute(rows, 'sub', [(0, 1), (1, 0)])  4.35 us
    pallas_call x1, Pallas kernels, order_rows(): kernel_call(kernel, 'order_rows', 0, 3 * traces.size * 2, vmem_bytes=ORDE...  2.12 us
  transfers between devices with their start and end apart: 15, of which 9 were waited for; matrix products, arithmetic and copies ran while one was open for 0% of the time, Pallas kernels for 42%

profile of v6, /device:TPU:0, one launch (start us, length us, event | category | flops | bytes accessed | tf_op | source)
XLA Modules:
  0.0 98.6 jit_solution(14946492053921212032)
XLA Ops:
  0.7 2.1 %order_rows.1 = (bf16[32,64,512]{2,1,0:T(8,128)(2,1)S(1)}, bf16[32,32,512]{2,1,0:T(8,128)(2,1)S(1)}, bf16[32,32,512]{2,1,0:T(8,128)(2,1)S(1)}) custom-call(s32[64]{0:T(128)S(1)} %copy-done.2, bf16[64,32,512]{2,1,0:T(8,128)(2,1)} %traces_ref.1), custom_call_target="tpu_custom_call" | custom-call | bytes 6291456 | tf_op jit(solution)/shard_map/order_rows/pallas_call | solution.py:147
  3.3 2.6 %collective-permute-start.1 = (bf16[32,32,512]{2,1,0:T(8,128)(2,1)S(1)}, bf16[32,32,512]{2,1,0:T(8,128)(2,1)S(1)}, u32[]{:S(2)}, u32[]{:S(2)}) collective-permute-start(bf16[32,32,512]{2,1,0:T(8,128)(2,1)S(1)} %get-tuple-element.45), channel_id=1, source_target_pairs={{0,2},{2,0},{1,3},{3,1},{4,6},{6,4},{5,7},{7,5},{8,10},{10,8},{9,1... | collective-permute-start | bytes 3145736 | tf_op jit(solution)/shard_map/ppermute | solution.py:461
  7.1 9.3 %spectra.3 = (bf16[256,32,128]{2,1,0:T(8,128)(2,1)S(1)}, bf16[256,64,128]{2,1,0:T(8,128)(2,1)S(1)}) custom-call(bf16[32,64,512]{2,1,0:T(8,128)(2,1)S(1)} %get-tuple-element.41.j_ref, bf16[32,64,512]{2,1,0:T(8,128)(2,1)S(1)} %collective-permute-done.i_ref, bf16[512,512]{1,0:T(8,128)(2,1)S(1)} %copy-done.3, bf16[32,256]{1,0:T(8,128)(2,1)S(1)} %copy-done.7, ...), custom_call_target="tpu_custom_call" | custom-call | flops 2147483648 | bytes 8388608 | tf_op jit(solution)/shard_map/spectra/pallas_call | solution.py:253
  16.4 3.8 %partial_correlations.5 = (bf16[3,16,16,128]{3,2,1,0:T(8,128)(2,1)S(1)}, bf16[3,16,16,128]{3,2,1,0:T(8,128)(2,1)S(1)}, f32[3,16,16,128]{3,2,1,0:T(8,128)S(1)}, bf16[3,16,16,128]{3,2,1,0:T(8,128)(2,1)S(1)}) custom-call(bf16[256,32,128]{2,1,0:T(8,128)(2,1)S(1)} %get-tuple-element.42.refs_0_, bf16[256,64,128]{2,1,0:T(8,128)(2,1)S(1)} %get-tuple-element.43.refs_1_.refs_2_, ...), custom_call_target="tpu_custom_call" | custom-call | flops 805306368 | bytes 6291456 | tf_op jit(solution)/shard_map/partial_correlations/pallas_call | solution.py:394
  20.2 3.0 %collective-permute-start.2 = (bf16[3,16,16,128]{3,2,1,0:T(8,128)(2,1)S(1)}, bf16[3,16,16,128]{3,2,1,0:T(8,128)(2,1)S(1)}, u32[]{:S(2)}, u32[]{:S(2)}) collective-permute-start(bf16[3,16,16,128]{3,2,1,0:T(8,128)(2,1)S(1)} %get-tuple-element.46), channel_id=1, source_target_pairs={{0,4},{4,0},{8,12},{12,8},{1,5},{5,1},{9,13},{13,9},{2,6},{6,2},{1... | collective-permute-start | bytes 589832 | tf_op jit(solution)/shard_map/ppermute | solution.py:467
  23.3 6.4 %collective-permute-done.1.j_ref = bf16[32,32,512]{2,1,0:T(8,128)(2,1)S(1)} collective-permute-done((bf16[32,32,512]{2,1,0:T(8,128)(2,1)S(1)}, bf16[32,32,512]{2,1,0:T(8,128)(2,1)S(1)}, u32[]{:S(2)}, u32[]{:S(2)}) %collective-permute-start.1) | collective-permute-done | bytes 1048608 | tf_op jit(solution)/shard_map/ppermute | solution.py:461
  29.6 1.8 %collective-permute-start.4 = (bf16[32,32,512]{2,1,0:T(8,128)(2,1)S(1)}, bf16[32,32,512]{2,1,0:T(8,128)(2,1)S(1)}, u32[]{:S(2)}, u32[]{:S(2)}) collective-permute-start(bf16[32,32,512]{2,1,0:T(8,128)(2,1)S(1)} %get-tuple-element.51), channel_id=1, source_target_pairs={{0,2},{2,0},{1,3},{3,1},{4,6},{6,4},{5,7},{7,5},{8,10},{10,8},{9,1... | collective-permute-start | bytes 3145736 | tf_op jit(solution)/shard_map/ppermute | solution.py:461
  31.4 1.6 %collective-permute-start.6 = (bf16[3,16,16,128]{3,2,1,0:T(8,128)(2,1)S(1)}, bf16[3,16,16,128]{3,2,1,0:T(8,128)(2,1)S(1)}, u32[]{:S(2)}, u32[]{:S(2)}) collective-permute-start(bf16[3,16,16,128]{3,2,1,0:T(8,128)(2,1)S(1)} %get-tuple-element.55), channel_id=1, source_target_pairs={{0,4},{4,0},{8,12},{12,8},{1,5},{5,1},{9,13},{13,9},{2,6},{6,2},{1... | collective-permute-start | bytes 589832 | tf_op jit(solution)/shard_map/ppermute | solution.py:467
  33.0 2.7 %collective-permute-start.5 = (bf16[3,16,16,128]{3,2,1,0:T(8,128)(2,1)S(1)}, bf16[3,16,16,128]{3,2,1,0:T(8,128)(2,1)S(1)}, u32[]{:S(2)}, u32[]{:S(2)}) collective-permute-start(bf16[3,16,16,128]{3,2,1,0:T(8,128)(2,1)S(1)} %add_convert_fusion.2), channel_id=1, source_target_pairs={{0,8},{4,12},{8,0},{12,4},{1,9},{5,13},{9,1},{13,5},{2,10},{6,14},... | collective-permute-start | bytes 589832 | tf_op jit(solution)/shard_map/ppermute | solution.py:467
  35.7 5.3 %spectra.4 = (bf16[256,16,128]{2,1,0:T(8,128)(2,1)S(1)}, bf16[256,64,128]{2,1,0:T(8,128)(2,1)S(1)}) custom-call(bf16[32,32,512]{2,1,0:T(8,128)(2,1)S(1)} %collective-permute-done.1.j_ref, bf16[32,32,512]{2,1,0:T(8,128)(2,1)S(1)} %collective-permute-done.3.i_ref, bf16[512,512]{1,0:T(8,128)(2,1)S(1)} %copy-done.3, bf16[32,256]{1,0:T(8,128)(2,1)S(1)} %copy-done.6, ...), custom_call_target="tpu_custom_call" | custom-call | flops 1073741824 | bytes 4194304 | tf_op jit(solution)/shard_map/spectra/pallas_call | solution.py:253
  41.1 7.3 %partial_correlations.6 = (bf16[5,16,16,128]{3,2,1,0:T(8,128)(2,1)S(1)}, bf16[5,16,16,128]{3,2,1,0:T(8,128)(2,1)S(1)}, f32[2,16,16,128]{3,2,1,0:T(8,128)S(1)}, bf16[2,16,16,128]{3,2,1,0:T(8,128)(2,1)S(1)}) custom-call(bf16[256,32,128]{2,1,0:T(8,128)(2,1)S(1)} %get-tuple-element.42.refs_0_, bf16[256,16,128]{2,1,0:T(8,128)(2,1)S(1)} %get-tuple-element.48.refs_1_, ...), custom_call_target="tpu_custom_call" | custom-call | flops 1610612736 | bytes 11534336 | tf_op jit(solution)/shard_map/partial_correlations/pallas_call | solution.py:394
  48.9 6.3 %collective-permute-done.4.j_ref = bf16[32,32,512]{2,1,0:T(8,128)(2,1)S(1)} collective-permute-done((bf16[32,32,512]{2,1,0:T(8,128)(2,1)S(1)}, bf16[32,32,512]{2,1,0:T(8,128)(2,1)S(1)}, u32[]{:S(2)}, u32[]{:S(2)}) %collective-permute-start.4) | collective-permute-done | bytes 1048608 | tf_op jit(solution)/shard_map/ppermute | solution.py:461
  55.2 2.5 %collective-permute-done.7 = bf16[5,16,16,128]{3,2,1,0:T(8,128)(2,1)S(1)} collective-permute-done((bf16[5,16,16,128]{3,2,1,0:T(8,128)(2,1)S(1)}, bf16[5,16,16,128]{3,2,1,0:T(8,128)(2,1)S(1)}, u32[]{:S(2)}, u32[]{:S(2)}) %collective-permute-start.7) | collective-permute-done | bytes 327712 | tf_op jit(solution)/shard_map/ppermute | solution.py:467
  58.2 1.6 %collective-permute-start.10 = (bf16[2,16,16,128]{3,2,1,0:T(8,128)(2,1)S(1)}, bf16[2,16,16,128]{3,2,1,0:T(8,128)(2,1)S(1)}, u32[]{:S(2)}, u32[]{:S(2)}) collective-permute-start(bf16[2,16,16,128]{3,2,1,0:T(8,128)(2,1)S(1)} %get-tuple-element.66), channel_id=1, source_target_pairs={{0,4},{4,0},{8,12},{12,8},{1,5},{5,1},{9,13},{13,9},{2,6},{6,2},{1... | collective-permute-start | bytes 393224 | tf_op jit(solution)/shard_map/ppermute | solution.py:467
  60.4 5.4 %spectra.5 = (bf16[256,16,128]{2,1,0:T(8,128)(2,1)S(1)}, bf16[256,64,128]{2,1,0:T(8,128)(2,1)S(1)}) custom-call(bf16[32,32,512]{2,1,0:T(8,128)(2,1)S(1)} %collective-permute-done.4.j_ref, bf16[32,32,512]{2,1,0:T(8,128)(2,1)S(1)} %collective-permute-done.8.i_ref, bf16[512,512]{1,0:T(8,128)(2,1)S(1)} %copy-done.3, bf16[32,256]{1,0:T(8,128)(2,1)S(1)} %copy-done.6, ...), custom_call_target="tpu_custom_call" | custom-call | flops 1073741824 | bytes 4194304 | tf_op jit(solution)/shard_map/spectra/pallas_call | solution.py:253
  65.8 4.5 %partial_correlations.7 = (bf16[4,16,16,128]{3,2,1,0:T(8,128)(2,1)S(1)}, bf16[4,16,16,128]{3,2,1,0:T(8,128)(2,1)S(1)}, f32[1,16,16,128]{3,2,1,0:T(8,128)S(1)}, bf16[1,16,16,128]{3,2,1,0:T(8,128)(2,1)S(1)}) custom-call(bf16[256,32,128]{2,1,0:T(8,128)(2,1)S(1)} %get-tuple-element.42.refs_0_, bf16[256,16,128]{2,1,0:T(8,128)(2,1)S(1)} %get-tuple-element.48.refs_1_, ...), custom_call_target="tpu_custom_call" | custom-call | flops 1207959552 | bytes 7340032 | tf_op jit(solution)/shard_map/partial_correlations/pallas_call | solution.py:394
  70.8 5.1 %collective-permute-done.9.refs_10_ = bf16[5,16,16,128]{3,2,1,0:T(8,128)(2,1)S(1)} collective-permute-done((bf16[5,16,16,128]{3,2,1,0:T(8,128)(2,1)S(1)}, bf16[5,16,16,128]{3,2,1,0:T(8,128)(2,1)S(1)}, u32[]{:S(2)}, u32[]{:S(2)}) %collective-permute-start.9) | collective-permute-done | bytes 327712 | tf_op jit(solution)/shard_map/ppermute | solution.py:467
  75.9 3.1 %partial_correlations.8 = (f32[3,16,16,128]{3,2,1,0:T(8,128)S(1)}, bf16[3,16,16,128]{3,2,1,0:T(8,128)(2,1)S(1)}) custom-call(bf16[256,16,128]{2,1,0:T(8,128)(2,1)S(1)} %get-tuple-element.71.refs_0_, bf16[256,64,128]{2,1,0:T(8,128)(2,1)S(1)} %get-tuple-element.49.refs_3_.refs_1_, bf16[256,64,128]{2,1,0:T(8,128)(2,1)S(1)} %get-tuple-element.67.refs_2_, ...), custom_call_target="tpu_custom_call" | custom-call | flops 402653184 | bytes 9437184 | tf_op jit(solution)/shard_map/partial_correlations/pallas_call | solution.py:394
  79.2 2.3 %collective-permute-done.11 = bf16[4,16,16,128]{3,2,1,0:T(8,128)(2,1)S(1)} collective-permute-done((bf16[4,16,16,128]{3,2,1,0:T(8,128)(2,1)S(1)}, bf16[4,16,16,128]{3,2,1,0:T(8,128)(2,1)S(1)}, u32[]{:S(2)}, u32[]{:S(2)}) %collective-permute-start.11) | collective-permute-done | bytes 262176 | tf_op jit(solution)/shard_map/ppermute | solution.py:467
  81.6 3.1 %partial_correlations.9 = (f32[3,16,16,128]{3,2,1,0:T(8,128)S(1)}, bf16[3,16,16,128]{3,2,1,0:T(8,128)(2,1)S(1)}) custom-call(bf16[256,16,128]{2,1,0:T(8,128)(2,1)S(1)} %get-tuple-element.71.refs_0_, bf16[256,64,128]{2,1,0:T(8,128)(2,1)S(1)} %get-tuple-element.43.refs_1_.refs_2_, bf16[128,512]{1,0:T(8,128)(2,1)S(1)} %copy-done, bf16[256,256]{1,0:T(8,128)(2,1)S(1)} %copy-done.1), custom_call_target="tpu_custom_call" | custom-call | flops 402653184 | bytes 5242880 | tf_op jit(solution)/shard_map/partial_correlations/pallas_call | solution.py:394
  84.7 2.0 %collective-permute-start.13 = (bf16[3,16,16,128]{3,2,1,0:T(8,128)(2,1)S(1)}, bf16[3,16,16,128]{3,2,1,0:T(8,128)(2,1)S(1)}, u32[]{:S(2)}, u32[]{:S(2)}) collective-permute-start(bf16[3,16,16,128]{3,2,1,0:T(8,128)(2,1)S(1)} %get-tuple-element.75), channel_id=1, source_target_pairs={{0,4},{4,0},{8,12},{12,8},{1,5},{5,1},{9,13},{13,9},{2,6},{6,2},{1... | collective-permute-start | bytes 589832 | tf_op jit(solution)/shard_map/ppermute | solution.py:467
  86.7 3.6 %collective-permute-done.12.refs_7_ = bf16[4,16,16,128]{3,2,1,0:T(8,128)(2,1)S(1)} collective-permute-done((bf16[4,16,16,128]{3,2,1,0:T(8,128)(2,1)S(1)}, bf16[4,16,16,128]{3,2,1,0:T(8,128)(2,1)S(1)}, u32[]{:S(2)}, u32[]{:S(2)}) %collective-permute-start.12) | collective-permute-done | bytes 262176 | tf_op jit(solution)/shard_map/ppermute | solution.py:467
  90.3 6.9 %collective-permute-done.13.refs_8_ = bf16[3,16,16,128]{3,2,1,0:T(8,128)(2,1)S(1)} collective-permute-done((bf16[3,16,16,128]{3,2,1,0:T(8,128)(2,1)S(1)}, bf16[3,16,16,128]{3,2,1,0:T(8,128)(2,1)S(1)}, u32[]{:S(2)}, u32[]{:S(2)}) %collective-permute-start.13) | collective-permute-done | bytes 196640 | tf_op jit(solution)/shard_map/ppermute | solution.py:467
  97.2 1.2 %assembled.1 = f32[3,1,32,32,128]{4,3,2,1,0:T(8,128)} custom-call(f32[3,16,16,128]{3,2,1,0:T(8,128)S(1)} %get-tuple-element.44.refs_0_, f32[2,16,16,128]{3,2,1,0:T(8,128)S(1)} %get-tuple-element.50.refs_1_, f32[1,16,16,128]{3,2,1,0:T(8,128)S(1)} %get-tuple-element.62.refs_2_, f32[3,16,16,128]{3,2,1,0:T(8,128)S(1)} %get-tuple-element.68.refs_3_, ...), custom_call_target="tpu_custom_call" | custom-call | bytes 2359296 | tf_op jit(solution)/shard_map/assembled/pallas_call | solution.py:438
  (36 shorter events, 4.8 us)
Async XLA Ops:
  0.0 0.7 copy-start.2
  0.7 6.4 %copy-start.3 = (bf16[512,512]{1,0:T(8,128)(2,1)S(1)}, bf16[512,512]{1,0:T(8,128)(2,1)}, u32[]{:S(2)}) copy-start(bf16[512,512]{1,0:T(8,128)(2,1)} %constant.21.table_ref) | copy-start | bytes 1572868
  0.7 6.4 %copy-start.5 = (bf16[128,128]{1,0:T(8,128)(2,1)S(1)}, bf16[128,128]{1,0:T(8,128)(2,1)}, u32[]{:S(2)}) copy-start(bf16[128,128]{1,0:T(8,128)(2,1)} %constant.23.to_j_ref) | copy-start | bytes 98308
  0.7 6.4 %copy-start.7 = (bf16[32,256]{1,0:T(8,128)(2,1)S(1)}, bf16[32,256]{1,0:T(8,128)(2,1)}, u32[]{:S(2)}) copy-start(bf16[32,256]{1,0:T(8,128)(2,1)} %constant.22.to_i_ref) | copy-start | bytes 49156
  2.8 4.3 %collective-permute-start = (bf16[32,64,512]{2,1,0:T(8,128)(2,1)S(1)}, bf16[32,64,512]{2,1,0:T(8,128)(2,1)S(1)}, u32[]{:S(2)}, u32[]{:S(2)}) collective-permute-start(bf16[32,64,512]{2,1,0:T(8,128)(2,1)S(1)} %get-tuple-element.41.j_ref), channel_id=1, source_target_pairs={{0,1},{1,0},{2,3},{3,2},{4,5},{5,4},{6,7},{7,6},{8,9},{9,8},{10,11... | collective-permute-start | bytes 6291464 | tf_op jit(solution)/shard_map/ppermute | solution.py:464
  3.3 13.1 %copy-start = (bf16[128,512]{1,0:T(8,128)(2,1)S(1)}, bf16[128,512]{1,0:T(8,128)(2,1)}, u32[]{:S(2)}) copy-start(bf16[128,512]{1,0:T(8,128)(2,1)} %constant.24.refs_2_.refs_4_.refs_3_) | copy-start | bytes 393220
  3.3 13.1 %copy-start.1 = (bf16[256,256]{1,0:T(8,128)(2,1)S(1)}, bf16[256,256]{1,0:T(8,128)(2,1)}, u32[]{:S(2)}) copy-start(bf16[256,256]{1,0:T(8,128)(2,1)} %constant.25.refs_3_.refs_5_.refs_4_) | copy-start | bytes 393220
  3.3 26.3 %collective-permute-start.1 = (bf16[32,32,512]{2,1,0:T(8,128)(2,1)S(1)}, bf16[32,32,512]{2,1,0:T(8,128)(2,1)S(1)}, u32[]{:S(2)}, u32[]{:S(2)}) collective-permute-start(bf16[32,32,512]{2,1,0:T(8,128)(2,1)S(1)} %get-tuple-element.45), channel_id=1, source_target_pairs={{0,2},{2,0},{1,3},{3,1},{4,6},{6,4},{5,7},{7,5},{8,10},{10,8},{9,1... | collective-permute-start | bytes 3145736 | tf_op jit(solution)/shard_map/ppermute | solution.py:461
  16.4 19.3 %copy-start.4 = (bf16[128,256]{1,0:T(8,128)(2,1)S(1)}, bf16[128,256]{1,0:T(8,128)(2,1)}, u32[]{:S(2)}) copy-start(bf16[128,256]{1,0:T(8,128)(2,1)} %constant.27.to_j_ref) | copy-start | bytes 196612
  16.4 19.3 %copy-start.6 = (bf16[32,256]{1,0:T(8,128)(2,1)S(1)}, bf16[32,256]{1,0:T(8,128)(2,1)}, u32[]{:S(2)}) copy-start(bf16[32,256]{1,0:T(8,128)(2,1)} %constant.26.to_i_ref) | copy-start | bytes 49156
  20.2 9.4 %collective-permute-start.2 = (bf16[3,16,16,128]{3,2,1,0:T(8,128)(2,1)S(1)}, bf16[3,16,16,128]{3,2,1,0:T(8,128)(2,1)S(1)}, u32[]{:S(2)}, u32[]{:S(2)}) collective-permute-start(bf16[3,16,16,128]{3,2,1,0:T(8,128)(2,1)S(1)} %get-tuple-element.46), channel_id=1, source_target_pairs={{0,4},{4,0},{8,12},{12,8},{1,5},{5,1},{9,13},{13,9},{2,6},{6,2},{1... | collective-permute-start | bytes 589832 | tf_op jit(solution)/shard_map/ppermute | solution.py:467
  29.6 6.1 %collective-permute-start.3 = (bf16[32,32,512]{2,1,0:T(8,128)(2,1)S(1)}, bf16[32,32,512]{2,1,0:T(8,128)(2,1)S(1)}, u32[]{:S(2)}, u32[]{:S(2)}) collective-permute-start(bf16[32,32,512]{2,1,0:T(8,128)(2,1)S(1)} %collective-permute-done.1.j_ref), channel_id=1, source_target_pairs={{0,1},{1,0},{2,3},{3,2},{4,5},{5,4},{6,7},{7,6},{8,9},{9,8},{10,11... | collective-permute-start | bytes 3145736 | tf_op jit(solution)/shard_map/ppermute | solution.py:464
  29.6 25.6 %collective-permute-start.4 = (bf16[32,32,512]{2,1,0:T(8,128)(2,1)S(1)}, bf16[32,32,512]{2,1,0:T(8,128)(2,1)S(1)}, u32[]{:S(2)}, u32[]{:S(2)}) collective-permute-start(bf16[32,32,512]{2,1,0:T(8,128)(2,1)S(1)} %get-tuple-element.51), channel_id=1, source_target_pairs={{0,2},{2,0},{1,3},{3,1},{4,6},{6,4},{5,7},{7,5},{8,10},{10,8},{9,1... | collective-permute-start | bytes 3145736 | tf_op jit(solution)/shard_map/ppermute | solution.py:461
  31.4 17.0 %collective-permute-start.6 = (bf16[3,16,16,128]{3,2,1,0:T(8,128)(2,1)S(1)}, bf16[3,16,16,128]{3,2,1,0:T(8,128)(2,1)S(1)}, u32[]{:S(2)}, u32[]{:S(2)}) collective-permute-start(bf16[3,16,16,128]{3,2,1,0:T(8,128)(2,1)S(1)} %get-tuple-element.55), channel_id=1, source_target_pairs={{0,4},{4,0},{8,12},{12,8},{1,5},{5,1},{9,13},{13,9},{2,6},{6,2},{1... | collective-permute-start | bytes 589832 | tf_op jit(solution)/shard_map/ppermute | solution.py:467
  33.0 15.4 %collective-permute-start.5 = (bf16[3,16,16,128]{3,2,1,0:T(8,128)(2,1)S(1)}, bf16[3,16,16,128]{3,2,1,0:T(8,128)(2,1)S(1)}, u32[]{:S(2)}, u32[]{:S(2)}) collective-permute-start(bf16[3,16,16,128]{3,2,1,0:T(8,128)(2,1)S(1)} %add_convert_fusion.2), channel_id=1, source_target_pairs={{0,8},{4,12},{8,0},{12,4},{1,9},{5,13},{9,1},{13,5},{2,10},{6,14},... | collective-permute-start | bytes 589832 | tf_op jit(solution)/shard_map/ppermute | solution.py:467
  48.4 9.4 %collective-permute-start.7 = (bf16[5,16,16,128]{3,2,1,0:T(8,128)(2,1)S(1)}, bf16[5,16,16,128]{3,2,1,0:T(8,128)(2,1)S(1)}, u32[]{:S(2)}, u32[]{:S(2)}) collective-permute-start(bf16[5,16,16,128]{3,2,1,0:T(8,128)(2,1)S(1)} %get-tuple-element.56), channel_id=1, source_target_pairs={{0,4},{4,0},{8,12},{12,8},{1,5},{5,1},{9,13},{13,9},{2,6},{6,2},{1... | collective-permute-start | bytes 983048 | tf_op jit(solution)/shard_map/ppermute | solution.py:467
  57.8 2.7 %collective-permute-start.8 = (bf16[32,32,512]{2,1,0:T(8,128)(2,1)S(1)}, bf16[32,32,512]{2,1,0:T(8,128)(2,1)S(1)}, u32[]{:S(2)}, u32[]{:S(2)}) collective-permute-start(bf16[32,32,512]{2,1,0:T(8,128)(2,1)S(1)} %collective-permute-done.4.j_ref), channel_id=1, source_target_pairs={{0,1},{1,0},{2,3},{3,2},{4,5},{5,4},{6,7},{7,6},{8,9},{9,8},{10,11... | collective-permute-start | bytes 3145736 | tf_op jit(solution)/shard_map/ppermute | solution.py:464
  57.9 18.1 %collective-permute-start.9 = (bf16[5,16,16,128]{3,2,1,0:T(8,128)(2,1)S(1)}, bf16[5,16,16,128]{3,2,1,0:T(8,128)(2,1)S(1)}, u32[]{:S(2)}, u32[]{:S(2)}) collective-permute-start(bf16[5,16,16,128]{3,2,1,0:T(8,128)(2,1)S(1)} %add_convert_fusion), channel_id=1, source_target_pairs={{0,8},{4,12},{8,0},{12,4},{1,9},{5,13},{9,1},{13,5},{2,10},{6,14},... | collective-permute-start | bytes 983048 | tf_op jit(solution)/shard_map/ppermute | solution.py:467
  58.2 12.6 %collective-permute-start.10 = (bf16[2,16,16,128]{3,2,1,0:T(8,128)(2,1)S(1)}, bf16[2,16,16,128]{3,2,1,0:T(8,128)(2,1)S(1)}, u32[]{:S(2)}, u32[]{:S(2)}) collective-permute-start(bf16[2,16,16,128]{3,2,1,0:T(8,128)(2,1)S(1)} %get-tuple-element.66), channel_id=1, source_target_pairs={{0,4},{4,0},{8,12},{12,8},{1,5},{5,1},{9,13},{13,9},{2,6},{6,2},{1... | collective-permute-start | bytes 393224 | tf_op jit(solution)/shard_map/ppermute | solution.py:467
  70.3 11.2 %collective-permute-start.11 = (bf16[4,16,16,128]{3,2,1,0:T(8,128)(2,1)S(1)}, bf16[4,16,16,128]{3,2,1,0:T(8,128)(2,1)S(1)}, u32[]{:S(2)}, u32[]{:S(2)}) collective-permute-start(bf16[4,16,16,128]{3,2,1,0:T(8,128)(2,1)S(1)} %get-tuple-element.65), channel_id=1, source_target_pairs={{0,4},{4,0},{8,12},{12,8},{1,5},{5,1},{9,13},{13,9},{2,6},{6,2},{1... | collective-permute-start | bytes 786440 | tf_op jit(solution)/shard_map/ppermute | solution.py:467
  79.1 11.2 %collective-permute-start.12 = (bf16[4,16,16,128]{3,2,1,0:T(8,128)(2,1)S(1)}, bf16[4,16,16,128]{3,2,1,0:T(8,128)(2,1)S(1)}, u32[]{:S(2)}, u32[]{:S(2)}) collective-permute-start(bf16[4,16,16,128]{3,2,1,0:T(8,128)(2,1)S(1)} %pad_maximum_fusion), channel_id=1, source_target_pairs={{0,4},{4,0},{8,12},{12,8},{1,5},{5,1},{9,13},{13,9},{2,6},{6,2},{1... | collective-permute-start | bytes 786440 | tf_op jit(solution)/shard_map/ppermute | solution.py:467
  81.5 15.7 %collective-permute-start.14 = (bf16[4,16,16,128]{3,2,1,0:T(8,128)(2,1)S(1)}, bf16[4,16,16,128]{3,2,1,0:T(8,128)(2,1)S(1)}, u32[]{:S(2)}, u32[]{:S(2)}) collective-permute-start(bf16[4,16,16,128]{3,2,1,0:T(8,128)(2,1)S(1)} %add_convert_fusion.1), channel_id=1, source_target_pairs={{0,8},{4,12},{8,0},{12,4},{1,9},{5,13},{9,1},{13,5},{2,10},{6,14},... | collective-permute-start | bytes 786440 | tf_op jit(solution)/shard_map/ppermute | solution.py:467
  84.7 12.5 %collective-permute-start.13 = (bf16[3,16,16,128]{3,2,1,0:T(8,128)(2,1)S(1)}, bf16[3,16,16,128]{3,2,1,0:T(8,128)(2,1)S(1)}, u32[]{:S(2)}, u32[]{:S(2)}) collective-permute-start(bf16[3,16,16,128]{3,2,1,0:T(8,128)(2,1)S(1)} %get-tuple-element.75), channel_id=1, source_target_pairs={{0,4},{4,0},{8,12},{12,8},{1,5},{5,1},{9,13},{13,9},{2,6},{6,2},{1... | collective-permute-start | bytes 589832 | tf_op jit(solution)/shard_map/ppermute | solution.py:467
